TPU v7x, 128 devices: a whole 4x4x4 slice. The times are simulated.
128 devices in a mesh: row: 16 (over x, z_hi, core), col: 8 (over y, z_lo).
Axes of the slice: x: 4, y: 4, z: 4 (z_hi: 2, z_lo: 2; z = z_hi * 2 + z_lo), core: 2. Of those that a mesh axis runs over, the one named last changes fastest.
Arguments:
- context: bfloat16 [4096, 16384], P('row', 'col'), may hold values from -6 to 6
- out_weight: bfloat16 [16384, 16384], P('col', 'row'), may hold values from -0.046875 to 0.046875
- residual: bfloat16 [4096, 16384], P('col', 'row')
- norm_gain: float32 [16384], P('row'), may hold values from 0.25 to 1.75
- span_lengths: int32 [8, 384], P('col'), may hold values from 1 to 4, 512 in all within a row
- projector: bfloat16 [16384, 2048], P('row'), may hold values from -0.046875 to 0.046875
- student: bfloat16 [8, 384, 2048], P('col'), may hold values from -6 to 6
Outputs:
- projected: bfloat16 [8, 384, 2048], P('col', 'row')
- gradient: float32 [16384, 2048], P('row', 'col')
Inputs may be any that keep to these rules, and one draw needn't show every extreme that they name: Each row of span_lengths sums to 512, and every row has an entry equal to 4.
All inputs are finite; a program needn't handle non-finite values.
Results may differ from a plain program's by a relative error of at most 0.0052.
Values may be sent and summed in bfloat16 or wider, within the bound.
No kernel may reach another device: no remote copies, remote signals or barrier semaphores. Data moves between devices by JAX's collectives and lax.ppermute only.
A program may use at most 128 MiB of HBM per device.

v0:
```python
import math

import jax
import jax.numpy as jnp
from jax import lax
from jax.sharding import PartitionSpec as P


def body(context, out_weight, residual, norm_gain, span_lengths, projector, student):
    gathered = lax.all_gather(context, "row", axis=0, tiled=True)
    token_rows = residual.shape[0]
    attended = lax.psum_scatter(
        jnp.dot(gathered, out_weight, preferred_element_type=jnp.float32),
        "col",
        scatter_dimension=0,
        tiled=True,
    )
    stream = residual.astype(jnp.float32) + attended
    squares = lax.psum(jnp.sum(stream * stream, axis=1), "row")
    model_width = norm_gain.shape[0] * lax.axis_size("row")
    inverse_rms = lax.rsqrt(squares / model_width + 1e-05)
    hidden = (stream * inverse_rms[:, None] * norm_gain[None, :]).astype(jnp.bfloat16)
    span_sizes = span_lengths[0]
    span_ends = jnp.cumsum(span_sizes)
    span_starts = span_ends - span_sizes
    positions = jnp.arange(token_rows, dtype=jnp.int32)
    member = (positions[None, :] >= span_starts[:, None]) & (
        positions[None, :] < span_ends[:, None]
    )
    onehot = member.astype(jnp.bfloat16)
    summed = jnp.dot(onehot, hidden, preferred_element_type=jnp.float32)
    pooled = (summed / span_sizes.astype(jnp.float32)[:, None]).astype(jnp.bfloat16)
    student_rows = student[0]
    student_count = student_rows.shape[0]
    loss_factor = 1.0 / math.sqrt(lax.axis_size("col") * student_count)
    block_rows = student_count // lax.axis_size("row")
    block_first = lax.axis_index("row") * block_rows
    full_proj = lax.psum(jnp.dot(pooled, projector, preferred_element_type=jnp.float32), "row")
    mismatch = (full_proj - student_rows.astype(jnp.float32)).astype(jnp.bfloat16)
    outer_sum = lax.dot_general(
        pooled, mismatch, (((0,), (0,)), ((), ())), preferred_element_type=jnp.float32
    )
    out_block = lax.dynamic_slice_in_dim(full_proj, block_first, block_rows, 0)
    gradient = lax.psum_scatter(outer_sum * loss_factor, "col", scatter_dimension=1, tiled=True)
    return (out_block.astype(jnp.bfloat16)[None], gradient)


def solution(mesh):
    placed = (
        P("row", "col"),
        P("col", "row"),
        P("col", "row"),
        P("row"),
        P("col", None),
        P("row", None),
        P("col", None, None),
    )
    return jax.shard_map(
        body,
        mesh=mesh,
        in_specs=placed,
        out_specs=(P("col", "row", None), P("row", "col")),
        check_vma=False,
    )
```

profile of v0, /device:TPU:1, one launch (start us, length us, event | category | flops | bytes accessed | tf_op | source)
XLA Modules:
  0.0 846.1 jit_solution(13650265144109991876)
XLA Ops:
  7.2 0.0 all-gather.2.cloned.1.call-start
  7.2 0.7 all-gather.2.cloned.1.call-update
  7.9 0.0 reduce-scatter.3.cloned.1.call-start
  7.9 116.4 %all-gather.2.cloned.1.call-done = bf16[4096,2048]{1,0:T(8,128)(2,1)} async-done(((bf16[256,2048]{1,0:T(8,128)(2,1)}), bf16[4096,2048]{1,0:T(8,128)(2,1)}) %all-gather.2.cloned.1.call-update) | async-done | bytes 16777232 | tf_op jit(solution)/shard_map/all_gather | solution.py:10
  124.3 23.4 %fusion.11 = f32[4096,1024]{1,0:T(8,128)} fusion(bf16[4096,2048]{1,0:T(8,128)(2,1)} %all-gather.2.cloned.1.call-done, bf16[2048,1024]{1,0:T(8,128)(2,1)} %param.8), kind=kOutput, calls=%fused_computation.21 | convolution fusion | flops 17179869184 | bytes 37748736 | tf_op jit(solution)/shard_map/dot_general | solution.py:13
  147.7 0.0 reduce-scatter.3.cloned.1.call-update
  147.8 0.0 all-reduce.2.cloned.1.call-start
  147.8 0.6 copy-done.5
  148.4 0.3 reduce-window.9
  148.7 0.1 slice.7
  148.9 0.1 slice_reduce_fusion
  149.0 0.1 fusion.10
  149.1 322.6 %reduce-scatter.3.cloned.1.call-done = f32[512,1024]{1,0:T(8,128)} async-done(((f32[4096,1024]{1,0:T(8,128)}), f32[512,1024]{1,0:T(8,128)}) %reduce-scatter.3.cloned.1.call-update) | async-done | bytes 2097168 | tf_op jit(solution)/shard_map/reduce_scatter | solution.py:12
  471.6 2.1 multiply_reduce_fusion
  473.7 33.1 %psum.14 = f32[512]{0:T(512)S(1)} all-reduce(f32[512]{0:T(512)S(1)} %multiply_reduce_fusion), channel_id=1, replica_groups=mesh['row'=16,'col'=8] {'row'}, use_global_device_ids=true, to_apply=%region_4.5 | all-reduce | flops 512 | bytes 4096 | tf_op jit(solution)/shard_map/psum | solution.py:19
  506.9 0.9 divide_convert_fusion
  507.9 0.9 copy-done.3
  508.7 0.6 copy-done.6
  509.4 3.5 fusion.12
  512.8 0.0 reduce-scatter.5.cloned.1.call-start
  512.9 148.5 %all-reduce.2.cloned.1.call-done = f32[384,2048]{1,0:T(8,128)} async-done(((f32[384,2048]{1,0:T(8,128)}), f32[384,2048]{1,0:T(8,128)}) %all-reduce.2.cloned.1.call-update) | async-done | bytes 3145744 | tf_op jit(solution)/shard_map/psum | solution.py:38
  661.4 7.5 convolution_multiply_fusion
  668.9 1.6 fusion.9
  670.5 169.1 %reduce-scatter.5.cloned.1.call-done = f32[1024,256]{1,0:T(8,128)} async-done(((f32[1024,2048]{1,0:T(8,128)}), f32[1024,256]{1,0:T(8,128)}) %reduce-scatter.5.cloned.1.call-update) | async-done | bytes 1048592 | tf_op jit(solution)/shard_map/reduce_scatter | solution.py:44
  (18 shorter events, 0.1 us)
Async XLA Ops:
  7.2 117.2 %all-gather.2.cloned.1.call-start = ((), (), s32[]{:S(2)}) async-start(), calls=%async_computation.2 | async-start | bytes 17825792 | tf_op jit(solution)/shard_map/all_gather | solution.py:10
  7.9 463.7 %reduce-scatter.3.cloned.1.call-start = ((), (), s32[]{:S(2)}) async-start(), calls=%async_computation.3 | async-start | bytes 18874368 | tf_op jit(solution)/shard_map/reduce_scatter | solution.py:12
  147.7 0.7 copy-start.5
  147.7 323.9 %copy-start.2 = (bf16[512,1024]{1,0:T(8,128)(2,1)S(1)}, bf16[512,1024]{1,0:T(8,128)(2,1)}, u32[]{:S(2)}) copy-start(bf16[512,1024]{1,0:T(8,128)(2,1)} %param.9) | copy-start | bytes 3145732
  147.8 359.1 %copy-start.7 = (f32[1024]{0:T(1024)S(1)}, f32[1024]{0:T(1024)}, u32[]{:S(2)}) copy-start(f32[1024]{0:T(1024)} %param.10) | copy-start | bytes 12292
  147.8 513.6 %all-reduce.2.cloned.1.call-start = ((), (), s32[]{:S(2)}) async-start(), calls=%async_computation.4 | async-start | bytes 6291456 | tf_op jit(solution)/shard_map/psum | solution.py:38
  471.6 35.2 %copy-start = (f32[512,1024]{1,0:T(8,128)S(1)}, f32[512,1024]{1,0:T(8,128)}, u32[]{:S(2)}) copy-start(f32[512,1024]{1,0:T(8,128)} %reduce-scatter.3.cloned.1.call-done) | copy-start | bytes 6291460
  506.9 2.5 copy-start.6
  507.8 0.9 copy-start.3
  512.8 148.5 %copy-start.1 = (bf16[1,384,2048]{2,1,0:T(8,128)(2,1)S(1)}, bf16[1,384,2048]{2,1,0:T(8,128)(2,1)}, u32[]{:S(2)}) copy-start(bf16[1,384,2048]{2,1,0:T(8,128)(2,1)} %param.13) | copy-start | bytes 4718596
  512.8 148.5 %copy-start.4 = (bf16[384,1024]{1,0:T(8,128)(2,1)S(1)}, bf16[384,1024]{1,0:T(8,128)(2,1)}, u32[]{:S(2)}) copy-start(bf16[384,1024]{1,0:T(8,128)(2,1)} %copy-done.3) | copy-start | bytes 2359300
  512.8 326.7 %reduce-scatter.5.cloned.1.call-start = ((), (), s32[]{:S(2)}) async-start(), calls=%async_computation.5 | async-start | bytes 9437184 | tf_op jit(solution)/shard_map/reduce_scatter | solution.py:44
Sparse Core Ops, SparseCore 0:
  10.4 113.8 all-gather.1
  147.9 323.7 reduce-scatter.2
  513.0 148.3 all-reduce.1
  669.0 170.5 reduce-scatter.4
where the time goes:
time: 846 us
  waiting for transfers between devices  757 us (89%)
  matrix products  35.3 us (4%)
  blocking collectives  33.1 us (4%)
  between operations  13.8 us (2%)
    reduce_scatter x1, waiting for transfers between devices, body(): lax.psum_scatter(jnp.dot(gathered, out_weight, preferred_element_type=jnp...  323 us
    reduce_scatter x1, waiting for transfers between devices, body(): lax.psum_scatter(outer_sum * loss_factor, 'col', scatter_dimension=1, til...  169 us
    psum x1, waiting for transfers between devices, body(): lax.psum(jnp.dot(pooled, projector, preferred_element_type=jnp.float32),...  148 us
    all_gather x1, waiting for transfers between devices, body(): gathered = lax.all_gather(context, 'row', axis=0, tiled=True)  116 us
    psum x1, blocking collectives, body(): squares = lax.psum(jnp.sum(stream * stream, axis=1), 'row')  33.1 us
    dot_general x1, matrix products, body(): jnp.dot(gathered, out_weight, preferred_element_type=jnp.float32)  23.4 us
  transfers between devices with their start and end apart: 4, of which 4 were waited for; matrix products, arithmetic and copies ran while one was open for 0% of the time, Pallas kernels for 0%

commit v1 on v0

v1 whole, which is shorter than its diff:
```python
import math

import jax
import jax.numpy as jnp
from jax import lax
from jax.sharding import PartitionSpec as P

F32 = jnp.float32
BF16 = jnp.bfloat16
RUNS = (64, 64)


def body(context, out_weight, residual, norm_gain, span_lengths, projector, student):
    rows, cols = lax.axis_size("row"), lax.axis_size("col")
    xs, ys = rows // 4, cols // 2
    row, col = lax.axis_index("row"), lax.axis_index("col")
    x, zh, core = row // 4, (row // 2) % 2, row % 2
    y, zl = col // 2, col % 2

    near, following = 1 + 2 * core, 3 - 2 * core
    masks = (0, near, following, 2)

    def mask(r, second):
        return 1 if (r % 2 == 0) != second else 3

    def by_row(move):
        return [(r, move(r)) for r in range(rows)]

    def by_both(move):
        return [(r * cols + c, r * cols + move(r, c)) for r in range(rows) for c in range(cols)]

    x_near = by_row(lambda r: (r // 4 ^ mask(r, False)) * 4 + r % 4)
    x_next = by_row(lambda r: (r // 4 ^ mask(r, True)) * 4 + r % 4)
    y_near = by_both(lambda r, c: (c // 2 ^ mask(r, False)) * 2 + c % 2)
    y_next = by_both(lambda r, c: (c // 2 ^ mask(r, True)) * 2 + c % 2)
    z_far, twin = by_row(lambda r: r ^ 2), by_row(lambda r: r ^ 1)
    y_far = [(c, c ^ 4) for c in range(cols)]
    z_near = [(c, c ^ 1) for c in range(cols)]

    def over_row(value, pairs):
        return lax.ppermute(value, "row", pairs)

    def over_col(value, pairs):
        return lax.ppermute(value, "col", pairs)

    def over_both(value, pairs):
        return lax.ppermute(value, ("row", "col"), pairs)

    def tie(*values):
        return lax.optimization_barrier(values)

    def middle_exchanged(value, axis):
        return jnp.take(value, jnp.array([0, 2, 1, 3]), axis=axis)

    def place_of(distance):
        return jnp.where(distance == 0, 0, jnp.where(distance == 2, 3, jnp.where(distance == near, 1, 2)))

    shard, depth = context.shape
    width = out_weight.shape[1]
    head = shard - sum(RUNS)
    weight_twin = over_row(out_weight, twin)
    first, later = context[:head], context[head:]
    paired = over_row(first, x_near)
    first_far = over_row(first, z_far)
    later_far = over_row(later, z_far)
    paired, weight_twin = tie(paired, weight_twin)
    weight = jnp.concatenate([out_weight, weight_twin], axis=1)

    def later_unit(j):
        span = slice(sum(RUNS[:j]), sum(RUNS[: j + 1]))
        return jnp.concatenate([later[span], later_far[span]])

    def toward(terms, distance):
        place = place_of(jnp.bitwise_xor(jnp.bitwise_xor(y, distance), x))
        return lax.dynamic_index_in_dim(terms, place, 0, keepdims=False)

    def second_of(terms, arrived):
        kept = [
            toward(terms, k).astype(F32) + arrived[i].astype(F32) for i, k in enumerate((0, near))
        ]
        return kept[0], over_both(kept[1].astype(BF16), y_near)

    units, unit, coming = 2 + len(RUNS), first, first_far
    halves, firsts, seconds, all_terms = ([None] * units for _ in range(4))
    for j in range(units):
        if j >= 2:
            paired, all_terms[j - 2] = tie(paired, all_terms[j - 2])
        lane = jnp.concatenate([unit, paired])
        others = over_row(lane, x_next)
        if j == 0:
            others, later_far = tie(others, later_far)
        if j + 1 < units:
            coming, lane = tie(coming, lane)
            coming_paired = over_row(coming, x_near)
        tokens = jnp.concatenate([lane, others])
        terms = jnp.dot(tokens, weight, preferred_element_type=F32).astype(BF16)
        if 1 <= j < units - 1:
            terms, firsts[j - 1] = tie(terms, firsts[j - 1])
        if 2 <= j < units - 1:
            terms, seconds[j - 2] = tie(terms, seconds[j - 2])
        all_terms[j] = terms.reshape(xs, -1, 2 * width)
        firsts[j] = over_both(
            jnp.stack([toward(all_terms[j], following), toward(all_terms[j], 2)]), y_next
        )
        if j >= 1:
            halves[j - 1], seconds[j - 1] = second_of(all_terms[j - 1], firsts[j - 1])
        if j + 1 < units:
            unit, paired = coming, coming_paired
        if j + 2 < units:
            coming = later_unit(j)
    halves[-1], seconds[-1] = second_of(all_terms[-1], firsts[-1])
    sums = [half + second.astype(F32) for half, second in zip(halves, seconds)]

    same = zl == zh
    attended = []
    pairs = [(sums[0], sums[1])] + [(value[:run], value[run:]) for value, run in zip(sums[2:], RUNS)]
    for own, other in pairs:
        held, away = jnp.where(same, own, other), jnp.where(same, other, own)
        attended.append(held + over_col(away.astype(BF16), z_near).astype(F32))
    held = jnp.concatenate([value[:, :width] for value in attended])
    swapped = jnp.concatenate([over_row(value[:, width:], twin) for value in attended])
    attended = jnp.where(core == 0, jnp.concatenate([held, swapped]), jnp.concatenate([swapped, held]))
    stream = attended + residual.astype(F32)

    squares = jnp.sum(stream * stream, axis=1)
    for pairs in (twin, x_near, x_next, z_far):
        squares = squares + over_row(squares, pairs)
    inverse_rms = lax.rsqrt(squares / (width * rows) + 1e-05)
    hidden = (stream * inverse_rms[:, None] * norm_gain[None, :]).astype(BF16)

    span_sizes = span_lengths[0]
    span_ends = jnp.cumsum(span_sizes)
    count = span_sizes.shape[0]
    block = count // rows
    spans = jnp.stack([span_ends - span_sizes, span_ends, span_sizes]).reshape(3, xs, 2, 2, block)
    spans = jnp.where(core == 0, spans, spans[:, :, :, ::-1])
    spans = jnp.where(zh == 0, spans, spans[:, :, ::-1])
    spans = [lax.dynamic_slice_in_dim(spans, jnp.bitwise_xor(x, k), 1, 1) for k in masks]
    starts, ends, sizes = jnp.concatenate(spans, axis=1).reshape(3, count)
    positions = jnp.arange(stream.shape[0], dtype=jnp.int32)
    member = (positions[None, :] >= starts[:, None]) & (positions[None, :] < ends[:, None])
    summed = jnp.dot(member.astype(BF16), hidden, preferred_element_type=F32)
    pooled = (summed / sizes.astype(F32)[:, None]).astype(BF16)
    pooled_near = over_both(pooled, y_near)

    features = projector.shape[1]
    proj = jnp.dot(pooled, projector, preferred_element_type=F32).reshape(xs, 2, 2, block, features)
    proj = proj[:, :, 0] + over_row(middle_exchanged(proj[:, :, 1].astype(BF16), 0), twin).astype(F32)
    arrived = over_row(proj[2:].astype(BF16), x_next)
    proj = proj[:2] + arrived.astype(F32)
    arrived, pooled_near = tie(over_row(proj[1].astype(BF16), x_near), pooled_near)
    pooled_lane = jnp.concatenate([pooled, pooled_near])
    pooled_rest = over_both(pooled_lane, y_next)
    proj = proj[0] + arrived.astype(F32)
    full_proj = proj + over_row(proj[::-1].astype(BF16), z_far).astype(F32)
    places = [x * 4 + jnp.bitwise_xor(zh, kz) * 2 + core for kz in range(2)]
    student_rows = [lax.dynamic_slice_in_dim(student[0], place * block, block, 0) for place in places]
    mismatch = (full_proj - jnp.stack(student_rows).astype(F32)).astype(BF16)

    by_owner = mismatch.reshape(2 * block, ys, 2, features // cols)
    by_owner = jnp.where(zl == 0, by_owner, by_owner[:, :, ::-1]).reshape(2 * block, ys, features // ys)

    def quarter(distance):
        return lax.dynamic_index_in_dim(by_owner, jnp.bitwise_xor(y, distance), 1, keepdims=False)

    part = [
        quarter(0),
        over_both(quarter(near), y_near),
        over_both(quarter(following), y_next),
        over_col(quarter(2), y_far),
    ]
    part = jnp.stack(part)[None]
    part = jnp.concatenate([part, over_row(part, x_near)])
    others, pooled_rest = tie(over_row(part, x_next), pooled_rest)
    part = jnp.concatenate([part, others])
    twin_part = middle_exchanged(middle_exchanged(over_row(part, twin), 0), 1)
    part = jnp.stack([part, twin_part]).reshape(2, xs, ys, 2, block, features // ys)
    part = part.transpose(2, 1, 3, 0, 4, 5).reshape(ys * count, features // ys)
    all_pooled = jnp.concatenate([pooled_lane, pooled_rest])
    loss_factor = 1.0 / math.sqrt(cols * count)

    def outer(columns):
        product = lax.dot_general(
            all_pooled, columns, (((0,), (0,)), ((), ())), preferred_element_type=F32
        )
        return product * loss_factor

    own = features // cols
    theirs = over_col(outer(part[:, own:]).astype(BF16), z_near)
    ours, theirs = tie(outer(part[:, :own]), theirs)
    gradient = ours + theirs.astype(F32)
    return (full_proj[0].astype(BF16)[None], gradient)


def solution(mesh):
    placed = (
        P("row", "col"),
        P("col", "row"),
        P("col", "row"),
        P("row"),
        P("col", None),
        P("row", None),
        P("col", None, None),
    )
    return jax.shard_map(
        body,
        mesh=mesh,
        in_specs=placed,
        out_specs=(P("col", "row", None), P("row", "col")),
        check_vma=False,
    )
```

time: 846 us -> 255 us (0.30)
  waiting for transfers between devices: 757 us -> 121 us
  starting transfers between devices: 0.16 us -> 60 us
  blocking collectives: 33.1 us -> 0 us
  other arithmetic: 2.54 us -> 21 us
  local copies, waits for them, and re-layouts: 3.9 us -> 21.2 us
  between operations: 13.8 us -> 1.85 us
    reduce_scatter x2 -> x0, waiting for transfers between devices: 492 us -> none  [the longest x1 323 us: body(): lax.psum_scatter(jnp.dot(gathered, out_weight, preferred_element_type=jnp...]
    psum x1 -> x0, waiting for transfers between devices: 148 us -> none  [body(): lax.psum(jnp.dot(pooled, projector, preferred_element_type=jnp.float32),...]
    ppermute x0 -> x42, waiting for transfers between devices: none -> 121 us  [the longest x25 59 us: over_row(): return lax.ppermute(value, 'row', pairs)]
    all_gather x1 -> x0, waiting for transfers between devices: 116 us -> none  [body(): gathered = lax.all_gather(context, 'row', axis=0, tiled=True)]
    ppermute x0 -> x42, starting transfers between devices: none -> 60 us  [the longest x25 37.3 us: over_row(): return lax.ppermute(value, 'row', pairs)]
    psum x1 -> x0, blocking collectives: 33.1 us -> none  [body(): squares = lax.psum(jnp.sum(stream * stream, axis=1), 'row')]
    dot_general x4 -> x8, matrix products: 35.3 us -> 28.4 us  [the longest x4 19 us: body(): terms = jnp.dot(tokens, weight, preferred_element_type=F32).astype(BF16)]
  transfers between devices with their start and end apart: 4 -> 42, of which waited for: 4 -> 28; matrix products, arithmetic and copies ran while one was open for 0% -> 20% of each run, Pallas kernels for 0% -> 0%
where the time goes in v1:
time: 255 us; the launch traced here: 254 us
  waiting for transfers between devices  121 us (47%)
  starting transfers between devices  60 us (24%)
  matrix products  28.4 us (11%)
  local copies, waits for them, and re-layouts  21.2 us (8%)
  other arithmetic  21 us (8%)
    ppermute x25, waiting for transfers between devices, over_row(): return lax.ppermute(value, 'row', pairs)  59 us
    ppermute x25, starting transfers between devices, over_row(): return lax.ppermute(value, 'row', pairs)  37.3 us
    ppermute x12, waiting for transfers between devices, over_both(): return lax.ppermute(value, ('row', 'col'), pairs)  31.4 us
    ppermute x5, waiting for transfers between devices, over_col(): return lax.ppermute(value, 'col', pairs)  31 us
    dot_general x4, matrix products, body(): terms = jnp.dot(tokens, weight, preferred_element_type=F32).astype(BF16)  19 us
    ppermute x12, starting transfers between devices, over_both(): return lax.ppermute(value, ('row', 'col'), pairs)  13.5 us
    ppermute x5, starting transfers between devices, over_col(): return lax.ppermute(value, 'col', pairs)  9.17 us
    unnamed x90, local copies, waits for them, and re-layouts  8.7 us
  transfers between devices with their start and end apart: 42, of which 28 were waited for; matrix products, arithmetic and copies ran while one was open for 20% of the time, Pallas kernels for 0%

profile of v1, /device:TPU:1, one launch (start us, length us, event | category | flops | bytes accessed | tf_op | source)
XLA Modules:
  0.0 253.9 jit_solution(3247039547860007207)
XLA Ops:
  6.1 3.6 %collective-permute-start = (bf16[128,2048]{1,0:T(8,128)(2,1)S(1)}, bf16[128,2048]{1,0:T(8,128)(2,1)S(1)}, u32[]{:S(2)}, u32[]{:S(2)}) collective-permute-start(bf16[128,2048]{1,0:T(8,128)(2,1)S(1)} %get-tuple-element.67), channel_id=1, source_target_pairs={{0,16},{8,24},{16,0},{24,8},{32,48},{40,56},{48,32},{56,40},{64,80... | collective-permute-start | bytes 1572872 | tf_op jit(solution)/shard_map/ppermute | solution.py:41
  17.1 5.0 %collective-permute-done = bf16[128,2048]{1,0:T(8,128)(2,1)S(1)} collective-permute-done((bf16[128,2048]{1,0:T(8,128)(2,1)S(1)}, bf16[128,2048]{1,0:T(8,128)(2,1)S(1)}, u32[]{:S(2)}, u32[]{:S(2)}) %collective-permute-start) | collective-permute-done | bytes 524320 | tf_op jit(solution)/shard_map/ppermute | solution.py:41
  24.8 10.2 %collective-permute-done.5 = bf16[128,2048]{1,0:T(8,128)(2,1)S(1)} collective-permute-done((bf16[128,2048]{1,0:T(8,128)(2,1)S(1)}, bf16[128,2048]{1,0:T(8,128)(2,1)S(1)}, u32[]{:S(2)}, u32[]{:S(2)}) %collective-permute-start.5) | collective-permute-done | bytes 524320 | tf_op jit(solution)/shard_map/ppermute | solution.py:41
  37.7 4.7 %convolution_convert_fusion.3 = bf16[512,2048]{1,0:T(8,128)(2,1)S(1)} fusion(bf16[2048,2048]{1,0:T(8,128)(2,1)S(1)} %constant_dynamic-update-slice_fusion.3, bf16[256,2048]{1,0:T(8,128)(2,1)S(1)} %collective-permute-done.3, bf16[256,2048]{1,0:T(8,128)(2,1)S(1)} %pad_maximum_fusion.4), kind=kOutput, calls=%fused_computation.7 | convolution fusion | flops 4300210176 | bytes 12582912 | tf_op jit(solution)/shard_map/dot_general | solution.py:96
  44.0 6.4 %collective-permute-done.8 = bf16[128,2048]{1,0:T(8,128)(2,1)S(1)} collective-permute-done((bf16[128,2048]{1,0:T(8,128)(2,1)S(1)}, bf16[128,2048]{1,0:T(8,128)(2,1)S(1)}, u32[]{:S(2)}, u32[]{:S(2)}) %collective-permute-start.8) | collective-permute-done | bytes 524320 | tf_op jit(solution)/shard_map/ppermute | solution.py:41
  54.6 4.7 %convolution_convert_fusion.2 = bf16[512,2048]{1,0:T(8,128)(2,1)S(1)} fusion(bf16[2048,2048]{1,0:T(8,128)(2,1)S(1)} %constant_dynamic-update-slice_fusion.3, bf16[256,2048]{1,0:T(8,128)(2,1)S(1)} %collective-permute-done.6, bf16[256,2048]{1,0:T(8,128)(2,1)S(1)} %constant_dynamic-update-slice_fusion.5), kind=kOutput, calls=%fused_computation.6 | convolution fusion | flops 4300210176 | bytes 12582912 | tf_op jit(solution)/shard_map/dot_general | solution.py:96
  66.4 5.1 %collective-permute-done.9 = bf16[256,2048]{1,0:T(8,128)(2,1)S(1)} collective-permute-done((bf16[256,2048]{1,0:T(8,128)(2,1)S(1)}, bf16[256,2048]{1,0:T(8,128)(2,1)S(1)}, u32[]{:S(2)}, u32[]{:S(2)}) %collective-permute-start.9) | collective-permute-done | bytes 1048608 | tf_op jit(solution)/shard_map/ppermute | solution.py:41
  71.5 4.7 %convolution_convert_fusion.1 = bf16[512,2048]{1,0:T(8,128)(2,1)S(1)} fusion(bf16[2048,2048]{1,0:T(8,128)(2,1)S(1)} %constant_dynamic-update-slice_fusion.3, bf16[256,2048]{1,0:T(8,128)(2,1)S(1)} %collective-permute-done.9, bf16[256,2048]{1,0:T(8,128)(2,1)S(1)} %get-tuple-element.86), kind=kOutput, calls=%fused_computation.5 | convolution fusion | flops 4300210176 | bytes 12582912 | tf_op jit(solution)/shard_map/dot_general | solution.py:96
  76.2 3.0 %collective-permute-done.10 = bf16[2,128,2048]{2,1,0:T(8,128)(2,1)S(1)} collective-permute-done((bf16[2,128,2048]{2,1,0:T(8,128)(2,1)S(1)}, bf16[2,128,2048]{2,1,0:T(8,128)(2,1)S(1)}, u32[]{:S(2)}, u32[]{:S(2)}) %collective-permute-start.10) | collective-permute-done | bytes 1048608 | tf_op jit(solution)/shard_map/ppermute | solution.py:47
  84.6 4.8 %convolution_convert_fusion = bf16[512,2048]{1,0:T(8,128)(2,1)S(1)} fusion(bf16[2048,2048]{1,0:T(8,128)(2,1)S(1)} %constant_dynamic-update-slice_fusion.3, bf16[256,2048]{1,0:T(8,128)(2,1)S(1)} %collective-permute-done.18, bf16[128,2048]{1,0:T(8,128)(2,1)S(1)} %collective-permute-done.17, bf16[128,2048]{1,0:T(8,128)(2,1)S(1)} %get-tuple-element.42), kind=kOutput, calls=%fused_computation.4 | convolution fusion | flops 4302307328 | bytes 12582912 | tf_op jit(solution)/shard_map/dot_general | solution.py:96
  96.5 7.5 %collective-permute-done.14 = bf16[2,128,2048]{2,1,0:T(8,128)(2,1)} collective-permute-done((bf16[2,128,2048]{2,1,0:T(8,128)(2,1)}, bf16[2,128,2048]{2,1,0:T(8,128)(2,1)}, u32[]{:S(2)}, u32[]{:S(2)}) %collective-permute-start.14) | collective-permute-done | bytes 1048608 | tf_op jit(solution)/shard_map/ppermute | solution.py:47
  105.7 14.9 %collective-permute-done.19 = bf16[2,128,2048]{2,1,0:T(8,128)(2,1)} collective-permute-done((bf16[2,128,2048]{2,1,0:T(8,128)(2,1)}, bf16[2,128,2048]{2,1,0:T(8,128)(2,1)}, u32[]{:S(2)}, u32[]{:S(2)}) %collective-permute-start.19) | collective-permute-done | bytes 1048608 | tf_op jit(solution)/shard_map/ppermute | solution.py:47
  128.1 2.9 %collective-permute-done.20 = bf16[128,2048]{1,0:T(8,128)(2,1)S(1)} collective-permute-done((bf16[128,2048]{1,0:T(8,128)(2,1)S(1)}, bf16[128,2048]{1,0:T(8,128)(2,1)S(1)}, u32[]{:S(2)}, u32[]{:S(2)}) %collective-permute-start.20) | collective-permute-done | bytes 524320 | tf_op jit(solution)/shard_map/ppermute | solution.py:47
  135.6 4.7 %collective-permute-done.21 = bf16[64,2048]{1,0:T(8,128)(2,1)S(1)} collective-permute-done((bf16[64,2048]{1,0:T(8,128)(2,1)S(1)}, bf16[64,2048]{1,0:T(8,128)(2,1)S(1)}, u32[]{:S(2)}, u32[]{:S(2)}) %collective-permute-start.21) | collective-permute-done | bytes 262176 | tf_op jit(solution)/shard_map/ppermute | solution.py:44
  153.4 3.4 %collective-permute-start.28 = (f32[512]{0:T(512)S(1)}, f32[512]{0:T(512)S(1)}, u32[]{:S(2)}, u32[]{:S(2)}) collective-permute-start(f32[512]{0:T(512)S(1)} %add.215), channel_id=1, source_target_pairs={{0,16},{8,24},{16,0},{24,8},{32,48},{40,56},{48,32},{56,40},{64,80... | collective-permute-start | bytes 6152 | tf_op jit(solution)/shard_map/ppermute | solution.py:41
  174.0 4.4 %collective-permute-done.30 = bf16[2,2,24,2048]{3,2,1,0:T(8,128)(2,1)S(1)} collective-permute-done((bf16[2,2,24,2048]{3,2,1,0:T(8,128)(2,1)S(1)}, bf16[2,2,24,2048]{3,2,1,0:T(8,128)(2,1)S(1)}, u32[]{:S(2)}, u32[]{:S(2)}) %collective-permute-start.30) | collective-permute-done | bytes 393248 | tf_op jit(solution)/shard_map/ppermute | solution.py:41
  180.5 3.1 %collective-permute-done.32 = bf16[384,1024]{1,0:T(8,128)(2,1)S(1)} collective-permute-done((bf16[384,1024]{1,0:T(8,128)(2,1)S(1)}, bf16[384,1024]{1,0:T(8,128)(2,1)S(1)}, u32[]{:S(2)}, u32[]{:S(2)}) %collective-permute-start.32) | collective-permute-done | bytes 786464 | tf_op jit(solution)/shard_map/ppermute | solution.py:47
  184.4 3.3 %collective-permute-start.33 = (bf16[2,24,2048]{2,1,0:T(8,128)(2,1)S(1)}, bf16[2,24,2048]{2,1,0:T(8,128)(2,1)S(1)}, u32[]{:S(2)}, u32[]{:S(2)}) collective-permute-start(bf16[2,24,2048]{2,1,0:T(8,128)(2,1)S(1)} %rev.18), channel_id=1, source_target_pairs={{0,16},{8,24},{16,0},{24,8},{32,48},{40,56},{48,32},{56,40},{64,80... | collective-permute-start | bytes 589832 | tf_op jit(solution)/shard_map/ppermute | solution.py:41
  193.0 3.2 %collective-permute-start.36 = (bf16[48,512]{1,0:T(8,128)(2,1)S(1)}, bf16[48,512]{1,0:T(8,128)(2,1)S(1)}, u32[]{:S(2)}, u32[]{:S(2)}) collective-permute-start(bf16[48,512]{1,0:T(8,128)(2,1)S(1)} %get-tuple-element.75), channel_id=1, source_target_pairs={{0,4},{1,5},{2,6},{3,7},{4,0},{5,1},{6,2},{7,3},{8,12},{9,13},{10,... | collective-permute-start | bytes 147464 | tf_op jit(solution)/shard_map/ppermute | solution.py:44
  196.5 16.8 %collective-permute-done.36 = bf16[48,512]{1,0:T(8,128)(2,1)S(1)} collective-permute-done((bf16[48,512]{1,0:T(8,128)(2,1)S(1)}, bf16[48,512]{1,0:T(8,128)(2,1)S(1)}, u32[]{:S(2)}, u32[]{:S(2)}) %collective-permute-start.36) | collective-permute-done | bytes 49184 | tf_op jit(solution)/shard_map/ppermute | solution.py:44
  215.1 4.1 %collective-permute-done.37 = bf16[1,4,48,512]{3,2,1,0:T(8,128)(2,1)S(1)} collective-permute-done((bf16[1,4,48,512]{3,2,1,0:T(8,128)(2,1)S(1)}, bf16[1,4,48,512]{3,2,1,0:T(8,128)(2,1)S(1)}, u32[]{:S(2)}, u32[]{:S(2)}) %collective-permute-start.37) | collective-permute-done | bytes 196640 | tf_op jit(solution)/shard_map/ppermute | solution.py:41
  219.4 6.6 %collective-permute-done.38 = bf16[2,4,48,512]{3,2,1,0:T(8,128)(2,1)S(1)} collective-permute-done((bf16[2,4,48,512]{3,2,1,0:T(8,128)(2,1)S(1)}, bf16[2,4,48,512]{3,2,1,0:T(8,128)(2,1)S(1)}, u32[]{:S(2)}, u32[]{:S(2)}) %collective-permute-start.38) | collective-permute-done | bytes 393248 | tf_op jit(solution)/shard_map/ppermute | solution.py:41
  226.1 5.7 %collective-permute-start.40 = (bf16[4,4,48,512]{3,2,1,0:T(8,128)(2,1)S(1)}, bf16[4,4,48,512]{3,2,1,0:T(8,128)(2,1)S(1)}, u32[]{:S(2)}, u32[]{:S(2)}) collective-permute-start(bf16[4,4,48,512]{3,2,1,0:T(8,128)(2,1)S(1)} %pad_maximum_fusion.10), channel_id=1, source_target_pairs={{0,8},{8,0},{16,24},{24,16},{32,40},{40,32},{48,56},{56,48},{64,72... | collective-permute-start | bytes 2359304 | tf_op jit(solution)/shard_map/ppermute | solution.py:41
  243.6 9.3 %collective-permute-done.41 = bf16[1024,256]{1,0:T(8,128)(2,1)S(1)} collective-permute-done((bf16[1024,256]{1,0:T(8,128)(2,1)S(1)}, bf16[1024,256]{1,0:T(8,128)(2,1)S(1)}, u32[]{:S(2)}, u32[]{:S(2)}) %collective-permute-start.41) | collective-permute-done | bytes 524320 | tf_op jit(solution)/shard_map/ppermute | solution.py:44
  (245 shorter events, 109.9 us)
Async XLA Ops:
  0.6 12.4 %collective-permute-start.2 = (bf16[2048,1024]{1,0:T(8,128)(2,1)}, bf16[2048,1024]{1,0:T(8,128)(2,1)}, u32[]{:S(2)}, u32[]{:S(2)}) collective-permute-start(bf16[2048,1024]{1,0:T(8,128)(2,1)} %param.11), channel_id=1, source_target_pairs={{0,8},{8,0},{16,24},{24,16},{32,40},{40,32},{48,56},{56,48},{64,72... | collective-permute-start | bytes 12582920 | tf_op jit(solution)/shard_map/ppermute | solution.py:41
  6.1 16.0 %collective-permute-start = (bf16[128,2048]{1,0:T(8,128)(2,1)S(1)}, bf16[128,2048]{1,0:T(8,128)(2,1)S(1)}, u32[]{:S(2)}, u32[]{:S(2)}) collective-permute-start(bf16[128,2048]{1,0:T(8,128)(2,1)S(1)} %get-tuple-element.67), channel_id=1, source_target_pairs={{0,16},{8,24},{16,0},{24,8},{32,48},{40,56},{48,32},{56,40},{64,80... | collective-permute-start | bytes 1572872 | tf_op jit(solution)/shard_map/ppermute | solution.py:41
  9.7 25.5 %collective-permute-start.4 = (bf16[128,2048]{1,0:T(8,128)(2,1)S(1)}, bf16[128,2048]{1,0:T(8,128)(2,1)S(1)}, u32[]{:S(2)}, u32[]{:S(2)}) collective-permute-start(bf16[128,2048]{1,0:T(8,128)(2,1)S(1)} %get-tuple-element.66), channel_id=1, source_target_pairs={{0,16},{8,24},{16,0},{24,8},{32,48},{40,56},{48,32},{56,40},{64,80... | collective-permute-start | bytes 1572872 | tf_op jit(solution)/shard_map/ppermute | solution.py:41
  14.2 21.0 %collective-permute-start.3 = (bf16[256,2048]{1,0:T(8,128)(2,1)S(1)}, bf16[256,2048]{1,0:T(8,128)(2,1)S(1)}, u32[]{:S(2)}, u32[]{:S(2)}) collective-permute-start(bf16[256,2048]{1,0:T(8,128)(2,1)S(1)} %pad_maximum_fusion.4), channel_id=1, source_target_pairs={{0,96},{8,40},{16,112},{24,56},{32,64},{40,8},{48,80},{56,24},{64,... | collective-permute-start | bytes 3145736 | tf_op jit(solution)/shard_map/ppermute | solution.py:41
  22.1 12.8 %collective-permute-start.5 = (bf16[128,2048]{1,0:T(8,128)(2,1)S(1)}, bf16[128,2048]{1,0:T(8,128)(2,1)S(1)}, u32[]{:S(2)}, u32[]{:S(2)}) collective-permute-start(bf16[128,2048]{1,0:T(8,128)(2,1)S(1)} %collective-permute-done), channel_id=1, source_target_pairs={{0,32},{8,104},{16,48},{24,120},{32,0},{40,72},{48,16},{56,88},{64... | collective-permute-start | bytes 1572872 | tf_op jit(solution)/shard_map/ppermute | solution.py:41
  35.0 19.6 %collective-permute-start.6 = (bf16[256,2048]{1,0:T(8,128)(2,1)S(1)}, bf16[256,2048]{1,0:T(8,128)(2,1)S(1)}, u32[]{:S(2)}, u32[]{:S(2)}) collective-permute-start(bf16[256,2048]{1,0:T(8,128)(2,1)S(1)} %constant_dynamic-update-slice_fusion.5), channel_id=1, source_target_pairs={{0,96},{8,40},{16,112},{24,56},{32,64},{40,8},{48,80},{56,24},{64,... | collective-permute-start | bytes 3145736 | tf_op jit(solution)/shard_map/ppermute | solution.py:41
  35.3 15.2 %collective-permute-start.8 = (bf16[128,2048]{1,0:T(8,128)(2,1)S(1)}, bf16[128,2048]{1,0:T(8,128)(2,1)S(1)}, u32[]{:S(2)}, u32[]{:S(2)}) collective-permute-start(bf16[128,2048]{1,0:T(8,128)(2,1)S(1)} %pad_maximum_fusion.11), channel_id=1, source_target_pairs={{0,32},{8,104},{16,48},{24,120},{32,0},{40,72},{48,16},{56,88},{64... | collective-permute-start | bytes 1572872 | tf_op jit(solution)/shard_map/ppermute | solution.py:41
  42.6 16.8 %collective-permute-start.7 = (bf16[2,128,2048]{2,1,0:T(8,128)(2,1)S(1)}, bf16[2,128,2048]{2,1,0:T(8,128)(2,1)S(1)}, u32[]{:S(2)}, u32[]{:S(2)}) collective-permute-start(bf16[2,128,2048]{2,1,0:T(8,128)(2,1)S(1)} %pad_maximum_fusion.5), channel_id=1, source_target_pairs={{0,6},{1,7},{2,4},{3,5},{4,2},{5,3},{6,0},{7,1},{8,10},{9,11},{10,... | collective-permute-start | bytes 3145736 | tf_op jit(solution)/shard_map/ppermute | solution.py:47
  50.5 21.0 %collective-permute-start.9 = (bf16[256,2048]{1,0:T(8,128)(2,1)S(1)}, bf16[256,2048]{1,0:T(8,128)(2,1)S(1)}, u32[]{:S(2)}, u32[]{:S(2)}) collective-permute-start(bf16[256,2048]{1,0:T(8,128)(2,1)S(1)} %get-tuple-element.86), channel_id=1, source_target_pairs={{0,96},{8,40},{16,112},{24,56},{32,64},{40,8},{48,80},{56,24},{64,... | collective-permute-start | bytes 3145736 | tf_op jit(solution)/shard_map/ppermute | solution.py:41
  51.2 14.3 %collective-permute-start.17 = (bf16[128,2048]{1,0:T(8,128)(2,1)S(1)}, bf16[128,2048]{1,0:T(8,128)(2,1)S(1)}, u32[]{:S(2)}, u32[]{:S(2)}) collective-permute-start(bf16[128,2048]{1,0:T(8,128)(2,1)S(1)} %get-tuple-element.42), channel_id=1, source_target_pairs={{0,32},{8,104},{16,48},{24,120},{32,0},{40,72},{48,16},{56,88},{64... | collective-permute-start | bytes 1572872 | tf_op jit(solution)/shard_map/ppermute | solution.py:41
  59.6 19.6 %collective-permute-start.10 = (bf16[2,128,2048]{2,1,0:T(8,128)(2,1)S(1)}, bf16[2,128,2048]{2,1,0:T(8,128)(2,1)S(1)}, u32[]{:S(2)}, u32[]{:S(2)}) collective-permute-start(bf16[2,128,2048]{2,1,0:T(8,128)(2,1)S(1)} %pad_maximum_fusion.6), channel_id=1, source_target_pairs={{0,6},{1,7},{2,4},{3,5},{4,2},{5,3},{6,0},{7,1},{8,10},{9,11},{10,... | collective-permute-start | bytes 3145736 | tf_op jit(solution)/shard_map/ppermute | solution.py:47
  61.2 18.1 %collective-permute-start.11 = (bf16[128,2048]{1,0:T(8,128)(2,1)S(1)}, bf16[128,2048]{1,0:T(8,128)(2,1)S(1)}, u32[]{:S(2)}, u32[]{:S(2)}) collective-permute-start(bf16[128,2048]{1,0:T(8,128)(2,1)S(1)} %fusion.23), channel_id=1, source_target_pairs={{0,2},{1,3},{2,0},{3,1},{4,6},{5,7},{6,4},{7,5},{8,14},{9,15},{10,... | collective-permute-start | bytes 1572872 | tf_op jit(solution)/shard_map/ppermute | solution.py:47
  65.6 18.9 %collective-permute-start.18 = (bf16[256,2048]{1,0:T(8,128)(2,1)S(1)}, bf16[256,2048]{1,0:T(8,128)(2,1)S(1)}, u32[]{:S(2)}, u32[]{:S(2)}) collective-permute-start(bf16[256,2048]{1,0:T(8,128)(2,1)S(1)} %pad_maximum_fusion.8), channel_id=1, source_target_pairs={{0,96},{8,40},{16,112},{24,56},{32,64},{40,8},{48,80},{56,24},{64,... | collective-permute-start | bytes 3145736 | tf_op jit(solution)/shard_map/ppermute | solution.py:41
  84.5 19.5 %collective-permute-start.14 = (bf16[2,128,2048]{2,1,0:T(8,128)(2,1)}, bf16[2,128,2048]{2,1,0:T(8,128)(2,1)}, u32[]{:S(2)}, u32[]{:S(2)}) collective-permute-start(bf16[2,128,2048]{2,1,0:T(8,128)(2,1)} %pad_maximum_fusion.7), channel_id=1, source_target_pairs={{0,6},{1,7},{2,4},{3,5},{4,2},{5,3},{6,0},{7,1},{8,10},{9,11},{10,... | collective-permute-start | bytes 3145736 | tf_op jit(solution)/shard_map/ppermute | solution.py:47
  91.0 29.5 %collective-permute-start.19 = (bf16[2,128,2048]{2,1,0:T(8,128)(2,1)}, bf16[2,128,2048]{2,1,0:T(8,128)(2,1)}, u32[]{:S(2)}, u32[]{:S(2)}) collective-permute-start(bf16[2,128,2048]{2,1,0:T(8,128)(2,1)} %pad_maximum_fusion.9), channel_id=1, source_target_pairs={{0,6},{1,7},{2,4},{3,5},{4,2},{5,3},{6,0},{7,1},{8,10},{9,11},{10,... | collective-permute-start | bytes 3145736 | tf_op jit(solution)/shard_map/ppermute | solution.py:47
  94.8 27.7 %collective-permute-start.13 = (bf16[128,2048]{1,0:T(8,128)(2,1)S(1)}, bf16[128,2048]{1,0:T(8,128)(2,1)S(1)}, u32[]{:S(2)}, u32[]{:S(2)}) collective-permute-start(bf16[128,2048]{1,0:T(8,128)(2,1)S(1)} %select_convert_fusion), channel_id=1, source_target_pairs={{0,1},{1,0},{2,3},{3,2},{4,5},{5,4},{6,7},{7,6},{8,9},{9,8},{10,11... | collective-permute-start | bytes 1572872 | tf_op jit(solution)/shard_map/ppermute | solution.py:44
  105.2 19.9 %collective-permute-start.15 = (bf16[128,2048]{1,0:T(8,128)(2,1)S(1)}, bf16[128,2048]{1,0:T(8,128)(2,1)S(1)}, u32[]{:S(2)}, u32[]{:S(2)}) collective-permute-start(bf16[128,2048]{1,0:T(8,128)(2,1)S(1)} %fusion.25), channel_id=1, source_target_pairs={{0,2},{1,3},{2,0},{3,1},{4,6},{5,7},{6,4},{7,5},{8,14},{9,15},{10,... | collective-permute-start | bytes 1572872 | tf_op jit(solution)/shard_map/ppermute | solution.py:47
  125.1 16.4 %collective-permute-start.22 = (f32[128,1024]{1,0:T(8,128)}, f32[128,1024]{1,0:T(8,128)S(1)}, u32[]{:S(2)}, u32[]{:S(2)}) collective-permute-start(f32[128,1024]{1,0:T(8,128)} %slice.167), channel_id=1, source_target_pairs={{0,8},{8,0},{16,24},{24,16},{32,40},{40,32},{48,56},{56,48},{64,72... | collective-permute-start | bytes 1572872 | tf_op jit(solution)/shard_map/ppermute | solution.py:41
  171.5 12.1 %collective-permute-start.32 = (bf16[384,1024]{1,0:T(8,128)(2,1)S(1)}, bf16[384,1024]{1,0:T(8,128)(2,1)S(1)}, u32[]{:S(2)}, u32[]{:S(2)}) collective-permute-start(bf16[384,1024]{1,0:T(8,128)(2,1)S(1)} %copy-done.26), channel_id=1, source_target_pairs={{0,2},{1,3},{2,0},{3,1},{4,6},{5,7},{6,4},{7,5},{8,14},{9,15},{10,... | collective-permute-start | bytes 2359304 | tf_op jit(solution)/shard_map/ppermute | solution.py:47
  190.2 35.8 %collective-permute-start.39 = (bf16[768,1024]{1,0:T(8,128)(2,1)S(1)}, bf16[768,1024]{1,0:T(8,128)(2,1)}, u32[]{:S(2)}, u32[]{:S(2)}) collective-permute-start(bf16[768,1024]{1,0:T(8,128)(2,1)S(1)} %pad_maximum_fusion.1), channel_id=1, source_target_pairs={{0,6},{1,7},{2,4},{3,5},{4,2},{5,3},{6,0},{7,1},{8,10},{9,11},{10,... | collective-permute-start | bytes 4718600 | tf_op jit(solution)/shard_map/ppermute | solution.py:47
  193.0 20.4 %collective-permute-start.36 = (bf16[48,512]{1,0:T(8,128)(2,1)S(1)}, bf16[48,512]{1,0:T(8,128)(2,1)S(1)}, u32[]{:S(2)}, u32[]{:S(2)}) collective-permute-start(bf16[48,512]{1,0:T(8,128)(2,1)S(1)} %get-tuple-element.75), channel_id=1, source_target_pairs={{0,4},{1,5},{2,6},{3,7},{4,0},{5,1},{6,2},{7,3},{8,12},{9,13},{10,... | collective-permute-start | bytes 147464 | tf_op jit(solution)/shard_map/ppermute | solution.py:44
  196.2 17.2 %collective-permute-start.35 = (bf16[48,512]{1,0:T(8,128)(2,1)S(1)}, bf16[48,512]{1,0:T(8,128)(2,1)S(1)}, u32[]{:S(2)}, u32[]{:S(2)}) collective-permute-start(bf16[48,512]{1,0:T(8,128)(2,1)S(1)} %get-tuple-element.76), channel_id=1, source_target_pairs={{0,6},{1,7},{2,4},{3,5},{4,2},{5,3},{6,0},{7,1},{8,10},{9,11},{10,... | collective-permute-start | bytes 147464 | tf_op jit(solution)/shard_map/ppermute | solution.py:47
  196.2 17.2 %collective-permute-start.34 = (bf16[48,512]{1,0:T(8,128)(2,1)S(1)}, bf16[48,512]{1,0:T(8,128)(2,1)S(1)}, u32[]{:S(2)}, u32[]{:S(2)}) collective-permute-start(bf16[48,512]{1,0:T(8,128)(2,1)S(1)} %get-tuple-element.77), channel_id=1, source_target_pairs={{0,2},{1,3},{2,0},{3,1},{4,6},{5,7},{6,4},{7,5},{8,14},{9,15},{10,... | collective-permute-start | bytes 147464 | tf_op jit(solution)/shard_map/ppermute | solution.py:47
  239.7 13.2 %collective-permute-start.41 = (bf16[1024,256]{1,0:T(8,128)(2,1)S(1)}, bf16[1024,256]{1,0:T(8,128)(2,1)S(1)}, u32[]{:S(2)}, u32[]{:S(2)}) collective-permute-start(bf16[1024,256]{1,0:T(8,128)(2,1)S(1)} %fusion.15), channel_id=1, source_target_pairs={{0,1},{1,0},{2,3},{3,2},{4,5},{5,4},{6,7},{7,6},{8,9},{9,8},{10,11... | collective-permute-start | bytes 1572872 | tf_op jit(solution)/shard_map/ppermute | solution.py:44
  (57 other events, 445.1 us)

commit v2 on v1

--- a/solution.py
+++ b/solution.py
@@ -50,7 +50,8 @@
         return lax.optimization_barrier(values)
 
     def middle_exchanged(value, axis):
-        return jnp.take(value, jnp.array([0, 2, 1, 3]), axis=axis)
+        places = [lax.slice_in_dim(value, k, k + 1, axis=axis) for k in (0, 2, 1, 3)]
+        return jnp.concatenate(places, axis=axis)
 
     def place_of(distance):
         return jnp.where(distance == 0, 0, jnp.where(distance == 2, 3, jnp.where(distance == near, 1, 2)))
@@ -135,7 +136,11 @@
     spans = jnp.stack([span_ends - span_sizes, span_ends, span_sizes]).reshape(3, xs, 2, 2, block)
     spans = jnp.where(core == 0, spans, spans[:, :, :, ::-1])
     spans = jnp.where(zh == 0, spans, spans[:, :, ::-1])
-    spans = [lax.dynamic_slice_in_dim(spans, jnp.bitwise_xor(x, k), 1, 1) for k in masks]
+    spans = [
+        lax.dynamic_slice_in_dim(spans[:, :, :, kc], jnp.bitwise_xor(x, k), 1, 1)
+        for kc, order in enumerate((masks, (0, following, near, 2)))
+        for k in order
+    ]
     starts, ends, sizes = jnp.concatenate(spans, axis=1).reshape(3, count)
     positions = jnp.arange(stream.shape[0], dtype=jnp.int32)
     member = (positions[None, :] >= starts[:, None]) & (positions[None, :] < ends[:, None])
@@ -144,24 +149,24 @@
     pooled_near = over_both(pooled, y_near)
 
     features = projector.shape[1]
-    proj = jnp.dot(pooled, projector, preferred_element_type=F32).reshape(xs, 2, 2, block, features)
-    proj = proj[:, :, 0] + over_row(middle_exchanged(proj[:, :, 1].astype(BF16), 0), twin).astype(F32)
+    given = jnp.dot(pooled[count // 2 :], projector, preferred_element_type=F32).astype(BF16)
+    got = over_row(given, twin)
+    proj = jnp.dot(pooled[: count // 2], projector, preferred_element_type=F32) + got.astype(F32)
+    proj = proj.reshape(xs, 2, block, features)
     arrived = over_row(proj[2:].astype(BF16), x_next)
     proj = proj[:2] + arrived.astype(F32)
     arrived, pooled_near = tie(over_row(proj[1].astype(BF16), x_near), pooled_near)
-    pooled_lane = jnp.concatenate([pooled, pooled_near])
-    pooled_rest = over_both(pooled_lane, y_next)
     proj = proj[0] + arrived.astype(F32)
     full_proj = proj + over_row(proj[::-1].astype(BF16), z_far).astype(F32)
     places = [x * 4 + jnp.bitwise_xor(zh, kz) * 2 + core for kz in range(2)]
     student_rows = [lax.dynamic_slice_in_dim(student[0], place * block, block, 0) for place in places]
     mismatch = (full_proj - jnp.stack(student_rows).astype(F32)).astype(BF16)
 
-    by_owner = mismatch.reshape(2 * block, ys, 2, features // cols)
-    by_owner = jnp.where(zl == 0, by_owner, by_owner[:, :, ::-1]).reshape(2 * block, ys, features // ys)
+    mismatch = mismatch.reshape(2 * block, features)
 
     def quarter(distance):
-        return lax.dynamic_index_in_dim(by_owner, jnp.bitwise_xor(y, distance), 1, keepdims=False)
+        first_column = jnp.bitwise_xor(y, distance) * (features // ys)
+        return lax.dynamic_slice_in_dim(mismatch, first_column, features // ys, 1)
 
     part = [
         quarter(0),
@@ -169,13 +174,18 @@
         over_both(quarter(following), y_next),
         over_col(quarter(2), y_far),
     ]
+    part, pooled_near = tie(part, pooled_near)
+    pooled_lane = jnp.concatenate([pooled, pooled_near])
+    pooled_rest = over_both(pooled_lane, y_next)
     part = jnp.stack(part)[None]
-    part = jnp.concatenate([part, over_row(part, x_near)])
-    others, pooled_rest = tie(over_row(part, x_next), pooled_rest)
+    paired = over_row(part, x_near)
+    part = jnp.concatenate([part, paired])
+    others = over_row(part, x_next)
+    others, pooled_rest = tie(others, pooled_rest)
     part = jnp.concatenate([part, others])
-    twin_part = middle_exchanged(middle_exchanged(over_row(part, twin), 0), 1)
-    part = jnp.stack([part, twin_part]).reshape(2, xs, ys, 2, block, features // ys)
-    part = part.transpose(2, 1, 3, 0, 4, 5).reshape(ys * count, features // ys)
+    twin_part = middle_exchanged(over_row(part, twin), 1)
+    part = jnp.stack([part, twin_part]).transpose(2, 0, 1, 3, 4)
+    part = part.reshape(ys * count, features // ys)
     all_pooled = jnp.concatenate([pooled_lane, pooled_rest])
     loss_factor = 1.0 / math.sqrt(cols * count)
 
@@ -186,8 +196,8 @@
         return product * loss_factor
 
     own = features // cols
-    theirs = over_col(outer(part[:, own:]).astype(BF16), z_near)
-    ours, theirs = tie(outer(part[:, :own]), theirs)
+    theirs = over_col(outer(lax.dynamic_slice_in_dim(part, (1 - zl) * own, own, 1)).astype(BF16), z_near)
+    ours, theirs = tie(outer(lax.dynamic_slice_in_dim(part, zl * own, own, 1)), theirs)
     gradient = ours + theirs.astype(F32)
     return (full_proj[0].astype(BF16)[None], gradient)
 

time: 255 us -> 237 us (0.929)
  other arithmetic: 21 us -> 7.98 us
  local copies, waits for them, and re-layouts: 21.2 us -> 14.7 us
    ppermute x5, waiting for transfers between devices: 31 us -> 15.9 us  [over_col(): return lax.ppermute(value, 'col', pairs)]
    ppermute x12, waiting for transfers between devices: 31.4 us -> 44 us  [over_both(): return lax.ppermute(value, ('row', 'col'), pairs)]
    ppermute x25, waiting for transfers between devices: 59 us -> 63.4 us  [over_row(): return lax.ppermute(value, 'row', pairs)]
    convert_element_type x4, other arithmetic: 3.61 us -> 0.51 us  [second_of(): return (kept[0], over_both(kept[1].astype(BF16), y_near))]
    unnamed x90 -> x41, local copies, waits for them, and re-layouts: 8.7 us -> 7.29 us
  transfers between devices with their start and end apart: 42 -> 42, of which waited for: 28 -> 32; matrix products, arithmetic and copies ran while one was open for 20% -> 15% of each run, Pallas kernels for 0% -> 0%
where the time goes in v2:
time: 237 us
  waiting for transfers between devices  123 us (52%)
  starting transfers between devices  61.3 us (26%)
  matrix products  28.2 us (12%)
  local copies, waits for them, and re-layouts  14.7 us (6%)
  other arithmetic  7.98 us (3%)
    ppermute x25, waiting for transfers between devices, over_row(): return lax.ppermute(value, 'row', pairs)  63.4 us
    ppermute x12, waiting for transfers between devices, over_both(): return lax.ppermute(value, ('row', 'col'), pairs)  44 us
    ppermute x25, starting transfers between devices, over_row(): return lax.ppermute(value, 'row', pairs)  37.3 us
    dot_general x4, matrix products, body(): terms = jnp.dot(tokens, weight, preferred_element_type=F32).astype(BF16)  18.8 us
    ppermute x5, waiting for transfers between devices, over_col(): return lax.ppermute(value, 'col', pairs)  15.9 us
    ppermute x12, starting transfers between devices, over_both(): return lax.ppermute(value, ('row', 'col'), pairs)  15.7 us
    ppermute x5, starting transfers between devices, over_col(): return lax.ppermute(value, 'col', pairs)  8.32 us
    unnamed x41, local copies, waits for them, and re-layouts  7.29 us
  transfers between devices with their start and end apart: 42, of which 32 were waited for; matrix products, arithmetic and copies ran while one was open for 15% of the time, Pallas kernels for 0%

profile of v2, /device:TPU:1, one launch (start us, length us, event | category | flops | bytes accessed | tf_op | source)
XLA Modules:
  0.0 237.0 jit_solution(5299571144355739398)
XLA Ops:
  6.1 3.6 %collective-permute-start = (bf16[128,2048]{1,0:T(8,128)(2,1)S(1)}, bf16[128,2048]{1,0:T(8,128)(2,1)S(1)}, u32[]{:S(2)}, u32[]{:S(2)}) collective-permute-start(bf16[128,2048]{1,0:T(8,128)(2,1)S(1)} %get-tuple-element.77), channel_id=1, source_target_pairs={{0,16},{8,24},{16,0},{24,8},{32,48},{40,56},{48,32},{56,40},{64,80... | collective-permute-start | bytes 1572872 | tf_op jit(solution)/shard_map/ppermute | solution.py:41
  17.3 4.8 %collective-permute-done = bf16[128,2048]{1,0:T(8,128)(2,1)S(1)} collective-permute-done((bf16[128,2048]{1,0:T(8,128)(2,1)S(1)}, bf16[128,2048]{1,0:T(8,128)(2,1)S(1)}, u32[]{:S(2)}, u32[]{:S(2)}) %collective-permute-start) | collective-permute-done | bytes 524320 | tf_op jit(solution)/shard_map/ppermute | solution.py:41
  25.0 10.0 %collective-permute-done.5 = bf16[128,2048]{1,0:T(8,128)(2,1)S(1)} collective-permute-done((bf16[128,2048]{1,0:T(8,128)(2,1)S(1)}, bf16[128,2048]{1,0:T(8,128)(2,1)S(1)}, u32[]{:S(2)}, u32[]{:S(2)}) %collective-permute-start.5) | collective-permute-done | bytes 524320 | tf_op jit(solution)/shard_map/ppermute | solution.py:41
  37.7 4.7 %convolution_convert_fusion.3 = bf16[512,2048]{1,0:T(8,128)(2,1)S(1)} fusion(bf16[2048,2048]{1,0:T(8,128)(2,1)S(1)} %constant_dynamic-update-slice_fusion.11, bf16[256,2048]{1,0:T(8,128)(2,1)S(1)} %collective-permute-done.3, bf16[256,2048]{1,0:T(8,128)(2,1)S(1)} %pad_maximum_fusion.5), kind=kOutput, calls=%fused_computation.4 | convolution fusion | flops 4300210176 | bytes 12582912 | tf_op jit(solution)/shard_map/dot_general | solution.py:97
  44.0 6.5 %collective-permute-done.8 = bf16[128,2048]{1,0:T(8,128)(2,1)S(1)} collective-permute-done((bf16[128,2048]{1,0:T(8,128)(2,1)S(1)}, bf16[128,2048]{1,0:T(8,128)(2,1)S(1)}, u32[]{:S(2)}, u32[]{:S(2)}) %collective-permute-start.8) | collective-permute-done | bytes 524320 | tf_op jit(solution)/shard_map/ppermute | solution.py:41
  54.6 4.7 %convolution_convert_fusion.2 = bf16[512,2048]{1,0:T(8,128)(2,1)S(1)} fusion(bf16[2048,2048]{1,0:T(8,128)(2,1)S(1)} %constant_dynamic-update-slice_fusion.11, bf16[256,2048]{1,0:T(8,128)(2,1)S(1)} %collective-permute-done.6, bf16[256,2048]{1,0:T(8,128)(2,1)S(1)} %constant_dynamic-update-slice_fusion.13), kind=kOutput, calls=%fused_computation.3 | convolution fusion | flops 4300210176 | bytes 12582912 | tf_op jit(solution)/shard_map/dot_general | solution.py:97
  66.5 5.0 %collective-permute-done.9 = bf16[256,2048]{1,0:T(8,128)(2,1)S(1)} collective-permute-done((bf16[256,2048]{1,0:T(8,128)(2,1)S(1)}, bf16[256,2048]{1,0:T(8,128)(2,1)S(1)}, u32[]{:S(2)}, u32[]{:S(2)}) %collective-permute-start.9) | collective-permute-done | bytes 1048608 | tf_op jit(solution)/shard_map/ppermute | solution.py:41
  71.5 4.8 %convolution_convert_fusion.1 = bf16[512,2048]{1,0:T(8,128)(2,1)S(1)} fusion(bf16[2048,2048]{1,0:T(8,128)(2,1)S(1)} %constant_dynamic-update-slice_fusion.11, bf16[256,2048]{1,0:T(8,128)(2,1)S(1)} %collective-permute-done.9, bf16[256,2048]{1,0:T(8,128)(2,1)S(1)} %get-tuple-element.108), kind=kOutput, calls=%fused_computation.2 | convolution fusion | flops 4300210176 | bytes 12582912 | tf_op jit(solution)/shard_map/dot_general | solution.py:97
  76.3 2.9 %collective-permute-done.10 = bf16[2,128,2048]{2,1,0:T(8,128)(2,1)S(1)} collective-permute-done((bf16[2,128,2048]{2,1,0:T(8,128)(2,1)S(1)}, bf16[2,128,2048]{2,1,0:T(8,128)(2,1)S(1)}, u32[]{:S(2)}, u32[]{:S(2)}) %collective-permute-start.10) | collective-permute-done | bytes 1048608 | tf_op jit(solution)/shard_map/ppermute | solution.py:47
  82.7 4.7 %convolution_convert_fusion = bf16[512,2048]{1,0:T(8,128)(2,1)S(1)} fusion(bf16[2048,2048]{1,0:T(8,128)(2,1)S(1)} %constant_dynamic-update-slice_fusion.11, bf16[256,2048]{1,0:T(8,128)(2,1)S(1)} %collective-permute-done.18, bf16[128,2048]{1,0:T(8,128)(2,1)S(1)} %collective-permute-done.17, bf16[128,2048]{1,0:T(8,128)(2,1)S(1)} %get-tuple-element.47), kind=kOutput, calls=%fused_computation.1 | convolution fusion | flops 4302307328 | bytes 12582912 | tf_op jit(solution)/shard_map/dot_general | solution.py:97
  93.0 9.1 %collective-permute-done.14 = bf16[2,128,2048]{2,1,0:T(8,128)(2,1)S(1)} collective-permute-done((bf16[2,128,2048]{2,1,0:T(8,128)(2,1)S(1)}, bf16[2,128,2048]{2,1,0:T(8,128)(2,1)S(1)}, u32[]{:S(2)}, u32[]{:S(2)}) %collective-permute-start.14) | collective-permute-done | bytes 1048608 | tf_op jit(solution)/shard_map/ppermute | solution.py:47
  102.3 16.3 %collective-permute-done.19 = bf16[2,128,2048]{2,1,0:T(8,128)(2,1)S(1)} collective-permute-done((bf16[2,128,2048]{2,1,0:T(8,128)(2,1)S(1)}, bf16[2,128,2048]{2,1,0:T(8,128)(2,1)S(1)}, u32[]{:S(2)}, u32[]{:S(2)}) %collective-permute-start.19) | collective-permute-done | bytes 1048608 | tf_op jit(solution)/shard_map/ppermute | solution.py:47
  121.9 6.2 %collective-permute-done.20 = bf16[128,2048]{1,0:T(8,128)(2,1)S(1)} collective-permute-done((bf16[128,2048]{1,0:T(8,128)(2,1)S(1)}, bf16[128,2048]{1,0:T(8,128)(2,1)S(1)}, u32[]{:S(2)}, u32[]{:S(2)}) %collective-permute-start.20) | collective-permute-done | bytes 524320 | tf_op jit(solution)/shard_map/ppermute | solution.py:47
  130.3 5.2 %collective-permute-done.21 = bf16[64,2048]{1,0:T(8,128)(2,1)S(1)} collective-permute-done((bf16[64,2048]{1,0:T(8,128)(2,1)S(1)}, bf16[64,2048]{1,0:T(8,128)(2,1)S(1)}, u32[]{:S(2)}, u32[]{:S(2)}) %collective-permute-start.21) | collective-permute-done | bytes 262176 | tf_op jit(solution)/shard_map/ppermute | solution.py:44
  146.9 3.6 %collective-permute-start.28 = (f32[512]{0:T(512)S(1)}, f32[512]{0:T(512)S(1)}, u32[]{:S(2)}, u32[]{:S(2)}) collective-permute-start(f32[512]{0:T(512)S(1)} %add.212), channel_id=1, source_target_pairs={{0,16},{8,24},{16,0},{24,8},{32,48},{40,56},{48,32},{56,40},{64,80... | collective-permute-start | bytes 6152 | tf_op jit(solution)/shard_map/ppermute | solution.py:41
  151.5 3.0 %divide_convert_fusion = bf16[384,1024]{1,0:T(8,128)(2,1)S(1)} fusion(f32[1024]{0:T(1024)S(1)} %copy-done.10, f32[512]{0:T(512)S(1)} %add_rsqrt_fusion, f32[384]{0:T(512)S(1)} %convert_element_type.231, s32[384]{0:T(512)S(1)} %lt.90, s32[384]{0:T(512)S(1)} %ge.18, bf16[512,1024]{1,0:T(8,128)(2,1)} %param.9, ...), kind=kOutput, calls=%fused_computation.26 | convolution fusion | flops 407175168 | bytes 6040065 | tf_op jit(solution)/shard_map/dot_general | solution.py:147
  163.5 4.9 %collective-permute-done.30 = bf16[2,2,24,2048]{3,2,1,0:T(8,128)(2,1)S(1)} collective-permute-done((bf16[2,2,24,2048]{3,2,1,0:T(8,128)(2,1)S(1)}, bf16[2,2,24,2048]{3,2,1,0:T(8,128)(2,1)S(1)}, u32[]{:S(2)}, u32[]{:S(2)}) %collective-permute-start.30) | collective-permute-done | bytes 393248 | tf_op jit(solution)/shard_map/ppermute | solution.py:41
  170.5 3.1 %collective-permute-done.32 = bf16[384,1024]{1,0:T(8,128)(2,1)S(1)} collective-permute-done((bf16[384,1024]{1,0:T(8,128)(2,1)S(1)}, bf16[384,1024]{1,0:T(8,128)(2,1)S(1)}, u32[]{:S(2)}, u32[]{:S(2)}) %collective-permute-start.32) | collective-permute-done | bytes 786464 | tf_op jit(solution)/shard_map/ppermute | solution.py:47
  174.4 3.3 %collective-permute-start.33 = (bf16[2,24,2048]{2,1,0:T(8,128)(2,1)S(1)}, bf16[2,24,2048]{2,1,0:T(8,128)(2,1)S(1)}, u32[]{:S(2)}, u32[]{:S(2)}) collective-permute-start(bf16[2,24,2048]{2,1,0:T(8,128)(2,1)S(1)} %rev.14), channel_id=1, source_target_pairs={{0,16},{8,24},{16,0},{24,8},{32,48},{40,56},{48,32},{56,40},{64,80... | collective-permute-start | bytes 589832 | tf_op jit(solution)/shard_map/ppermute | solution.py:41
  191.0 4.4 %collective-permute-done.37 = bf16[1,4,48,512]{3,2,0,1:T(8,128)(2,1)S(1)} collective-permute-done((bf16[1,4,48,512]{3,2,0,1:T(8,128)(2,1)S(1)}, bf16[1,4,48,512]{3,2,0,1:T(8,128)(2,1)S(1)}, u32[]{:S(2)}, u32[]{:S(2)}) %collective-permute-start.37) | collective-permute-done | bytes 196640 | tf_op jit(solution)/shard_map/ppermute | solution.py:41
  195.5 8.4 %collective-permute-done.38 = bf16[2,4,48,512]{3,2,0,1:T(8,128)(2,1)S(1)} collective-permute-done((bf16[2,4,48,512]{3,2,0,1:T(8,128)(2,1)S(1)}, bf16[2,4,48,512]{3,2,0,1:T(8,128)(2,1)S(1)}, u32[]{:S(2)}, u32[]{:S(2)}) %collective-permute-start.38) | collective-permute-done | bytes 393248 | tf_op jit(solution)/shard_map/ppermute | solution.py:41
  203.9 3.8 %collective-permute-done.39 = bf16[768,1024]{1,0:T(8,128)(2,1)S(1)} collective-permute-done((bf16[768,1024]{1,0:T(8,128)(2,1)S(1)}, bf16[768,1024]{1,0:T(8,128)(2,1)S(1)}, u32[]{:S(2)}, u32[]{:S(2)}) %collective-permute-start.39) | collective-permute-done | bytes 1572896 | tf_op jit(solution)/shard_map/ppermute | solution.py:47
  208.9 7.0 %collective-permute-start.40 = (bf16[4,4,48,512]{3,2,0,1:T(8,128)(2,1)S(1)}, bf16[4,4,48,512]{3,2,0,1:T(8,128)(2,1)S(1)}, u32[]{:S(2)}, u32[]{:S(2)}) collective-permute-start(bf16[4,4,48,512]{3,2,0,1:T(8,128)(2,1)S(1)} %get-tuple-element.79), channel_id=1, source_target_pairs={{0,8},{8,0},{16,24},{24,16},{32,40},{40,32},{48,56},{56,48},{64,72... | collective-permute-start | bytes 2359304 | tf_op jit(solution)/shard_map/ppermute | solution.py:41
  225.6 9.2 %collective-permute-done.41 = bf16[1024,256]{1,0:T(8,128)(2,1)} collective-permute-done((bf16[1024,256]{1,0:T(8,128)(2,1)}, bf16[1024,256]{1,0:T(8,128)(2,1)}, u32[]{:S(2)}, u32[]{:S(2)}) %collective-permute-start.41) | collective-permute-done | bytes 524320 | tf_op jit(solution)/shard_map/ppermute | solution.py:44
  (189 shorter events, 96.3 us)
Async XLA Ops:
  0.6 12.4 %collective-permute-start.2 = (bf16[2048,1024]{1,0:T(8,128)(2,1)}, bf16[2048,1024]{1,0:T(8,128)(2,1)}, u32[]{:S(2)}, u32[]{:S(2)}) collective-permute-start(bf16[2048,1024]{1,0:T(8,128)(2,1)} %param.8), channel_id=1, source_target_pairs={{0,8},{8,0},{16,24},{24,16},{32,40},{40,32},{48,56},{56,48},{64,72... | collective-permute-start | bytes 12582920 | tf_op jit(solution)/shard_map/ppermute | solution.py:41
  3.4 9.6 %collective-permute-start.1 = (bf16[128,2048]{1,0:T(8,128)(2,1)S(1)}, bf16[128,2048]{1,0:T(8,128)(2,1)}, u32[]{:S(2)}, u32[]{:S(2)}) collective-permute-start(bf16[128,2048]{1,0:T(8,128)(2,1)S(1)} %get-tuple-element.77), channel_id=1, source_target_pairs={{0,32},{8,104},{16,48},{24,120},{32,0},{40,72},{48,16},{56,88},{64... | collective-permute-start | bytes 1572872 | tf_op jit(solution)/shard_map/ppermute | solution.py:41
  6.1 16.0 %collective-permute-start = (bf16[128,2048]{1,0:T(8,128)(2,1)S(1)}, bf16[128,2048]{1,0:T(8,128)(2,1)S(1)}, u32[]{:S(2)}, u32[]{:S(2)}) collective-permute-start(bf16[128,2048]{1,0:T(8,128)(2,1)S(1)} %get-tuple-element.77), channel_id=1, source_target_pairs={{0,16},{8,24},{16,0},{24,8},{32,48},{40,56},{48,32},{56,40},{64,80... | collective-permute-start | bytes 1572872 | tf_op jit(solution)/shard_map/ppermute | solution.py:41
  9.7 25.5 %collective-permute-start.4 = (bf16[128,2048]{1,0:T(8,128)(2,1)S(1)}, bf16[128,2048]{1,0:T(8,128)(2,1)S(1)}, u32[]{:S(2)}, u32[]{:S(2)}) collective-permute-start(bf16[128,2048]{1,0:T(8,128)(2,1)S(1)} %get-tuple-element.76), channel_id=1, source_target_pairs={{0,16},{8,24},{16,0},{24,8},{32,48},{40,56},{48,32},{56,40},{64,80... | collective-permute-start | bytes 1572872 | tf_op jit(solution)/shard_map/ppermute | solution.py:41
  14.2 21.0 %collective-permute-start.3 = (bf16[256,2048]{1,0:T(8,128)(2,1)S(1)}, bf16[256,2048]{1,0:T(8,128)(2,1)S(1)}, u32[]{:S(2)}, u32[]{:S(2)}) collective-permute-start(bf16[256,2048]{1,0:T(8,128)(2,1)S(1)} %pad_maximum_fusion.5), channel_id=1, source_target_pairs={{0,96},{8,40},{16,112},{24,56},{32,64},{40,8},{48,80},{56,24},{64,... | collective-permute-start | bytes 3145736 | tf_op jit(solution)/shard_map/ppermute | solution.py:41
  22.1 12.8 %collective-permute-start.5 = (bf16[128,2048]{1,0:T(8,128)(2,1)S(1)}, bf16[128,2048]{1,0:T(8,128)(2,1)S(1)}, u32[]{:S(2)}, u32[]{:S(2)}) collective-permute-start(bf16[128,2048]{1,0:T(8,128)(2,1)S(1)} %collective-permute-done), channel_id=1, source_target_pairs={{0,32},{8,104},{16,48},{24,120},{32,0},{40,72},{48,16},{56,88},{64... | collective-permute-start | bytes 1572872 | tf_op jit(solution)/shard_map/ppermute | solution.py:41
  35.0 19.6 %collective-permute-start.6 = (bf16[256,2048]{1,0:T(8,128)(2,1)S(1)}, bf16[256,2048]{1,0:T(8,128)(2,1)S(1)}, u32[]{:S(2)}, u32[]{:S(2)}) collective-permute-start(bf16[256,2048]{1,0:T(8,128)(2,1)S(1)} %constant_dynamic-update-slice_fusion.13), channel_id=1, source_target_pairs={{0,96},{8,40},{16,112},{24,56},{32,64},{40,8},{48,80},{56,24},{64,... | collective-permute-start | bytes 3145736 | tf_op jit(solution)/shard_map/ppermute | solution.py:41
  35.3 15.2 %collective-permute-start.8 = (bf16[128,2048]{1,0:T(8,128)(2,1)S(1)}, bf16[128,2048]{1,0:T(8,128)(2,1)S(1)}, u32[]{:S(2)}, u32[]{:S(2)}) collective-permute-start(bf16[128,2048]{1,0:T(8,128)(2,1)S(1)} %pad_maximum_fusion.12), channel_id=1, source_target_pairs={{0,32},{8,104},{16,48},{24,120},{32,0},{40,72},{48,16},{56,88},{64... | collective-permute-start | bytes 1572872 | tf_op jit(solution)/shard_map/ppermute | solution.py:41
  42.6 16.8 %collective-permute-start.7 = (bf16[2,128,2048]{2,1,0:T(8,128)(2,1)S(1)}, bf16[2,128,2048]{2,1,0:T(8,128)(2,1)S(1)}, u32[]{:S(2)}, u32[]{:S(2)}) collective-permute-start(bf16[2,128,2048]{2,1,0:T(8,128)(2,1)S(1)} %pad_maximum_fusion.6), channel_id=1, source_target_pairs={{0,6},{1,7},{2,4},{3,5},{4,2},{5,3},{6,0},{7,1},{8,10},{9,11},{10,... | collective-permute-start | bytes 3145736 | tf_op jit(solution)/shard_map/ppermute | solution.py:47
  50.5 21.0 %collective-permute-start.9 = (bf16[256,2048]{1,0:T(8,128)(2,1)S(1)}, bf16[256,2048]{1,0:T(8,128)(2,1)S(1)}, u32[]{:S(2)}, u32[]{:S(2)}) collective-permute-start(bf16[256,2048]{1,0:T(8,128)(2,1)S(1)} %get-tuple-element.108), channel_id=1, source_target_pairs={{0,96},{8,40},{16,112},{24,56},{32,64},{40,8},{48,80},{56,24},{64,... | collective-permute-start | bytes 3145736 | tf_op jit(solution)/shard_map/ppermute | solution.py:41
  51.2 14.4 %collective-permute-start.17 = (bf16[128,2048]{1,0:T(8,128)(2,1)S(1)}, bf16[128,2048]{1,0:T(8,128)(2,1)S(1)}, u32[]{:S(2)}, u32[]{:S(2)}) collective-permute-start(bf16[128,2048]{1,0:T(8,128)(2,1)S(1)} %get-tuple-element.47), channel_id=1, source_target_pairs={{0,32},{8,104},{16,48},{24,120},{32,0},{40,72},{48,16},{56,88},{64... | collective-permute-start | bytes 1572872 | tf_op jit(solution)/shard_map/ppermute | solution.py:41
  59.5 19.6 %collective-permute-start.10 = (bf16[2,128,2048]{2,1,0:T(8,128)(2,1)S(1)}, bf16[2,128,2048]{2,1,0:T(8,128)(2,1)S(1)}, u32[]{:S(2)}, u32[]{:S(2)}) collective-permute-start(bf16[2,128,2048]{2,1,0:T(8,128)(2,1)S(1)} %pad_maximum_fusion.7), channel_id=1, source_target_pairs={{0,6},{1,7},{2,4},{3,5},{4,2},{5,3},{6,0},{7,1},{8,10},{9,11},{10,... | collective-permute-start | bytes 3145736 | tf_op jit(solution)/shard_map/ppermute | solution.py:47
  61.1 18.1 %collective-permute-start.11 = (bf16[128,2048]{1,0:T(8,128)(2,1)S(1)}, bf16[128,2048]{1,0:T(8,128)(2,1)S(1)}, u32[]{:S(2)}, u32[]{:S(2)}) collective-permute-start(bf16[128,2048]{1,0:T(8,128)(2,1)S(1)} %fusion.21), channel_id=1, source_target_pairs={{0,2},{1,3},{2,0},{3,1},{4,6},{5,7},{6,4},{7,5},{8,14},{9,15},{10,... | collective-permute-start | bytes 1572872 | tf_op jit(solution)/shard_map/ppermute | solution.py:47
  65.7 17.1 %collective-permute-start.18 = (bf16[256,2048]{1,0:T(8,128)(2,1)S(1)}, bf16[256,2048]{1,0:T(8,128)(2,1)S(1)}, u32[]{:S(2)}, u32[]{:S(2)}) collective-permute-start(bf16[256,2048]{1,0:T(8,128)(2,1)S(1)} %pad_maximum_fusion.9), channel_id=1, source_target_pairs={{0,96},{8,40},{16,112},{24,56},{32,64},{40,8},{48,80},{56,24},{64,... | collective-permute-start | bytes 3145736 | tf_op jit(solution)/shard_map/ppermute | solution.py:41
  79.3 11.5 %collective-permute-start.12 = (bf16[128,2048]{1,0:T(8,128)(2,1)S(1)}, bf16[128,2048]{1,0:T(8,128)(2,1)S(1)}, u32[]{:S(2)}, u32[]{:S(2)}) collective-permute-start(bf16[128,2048]{1,0:T(8,128)(2,1)S(1)} %fusion.22), channel_id=1, source_target_pairs={{0,2},{1,3},{2,0},{3,1},{4,6},{5,7},{6,4},{7,5},{8,14},{9,15},{10,... | collective-permute-start | bytes 1572872 | tf_op jit(solution)/shard_map/ppermute | solution.py:47
  82.4 19.7 %collective-permute-start.14 = (bf16[2,128,2048]{2,1,0:T(8,128)(2,1)S(1)}, bf16[2,128,2048]{2,1,0:T(8,128)(2,1)S(1)}, u32[]{:S(2)}, u32[]{:S(2)}) collective-permute-start(bf16[2,128,2048]{2,1,0:T(8,128)(2,1)S(1)} %pad_maximum_fusion.8), channel_id=1, source_target_pairs={{0,6},{1,7},{2,4},{3,5},{4,2},{5,3},{6,0},{7,1},{8,10},{9,11},{10,... | collective-permute-start | bytes 3145736 | tf_op jit(solution)/shard_map/ppermute | solution.py:47
  87.7 31.0 %collective-permute-start.19 = (bf16[2,128,2048]{2,1,0:T(8,128)(2,1)S(1)}, bf16[2,128,2048]{2,1,0:T(8,128)(2,1)S(1)}, u32[]{:S(2)}, u32[]{:S(2)}) collective-permute-start(bf16[2,128,2048]{2,1,0:T(8,128)(2,1)S(1)} %pad_maximum_fusion.10), channel_id=1, source_target_pairs={{0,6},{1,7},{2,4},{3,5},{4,2},{5,3},{6,0},{7,1},{8,10},{9,11},{10,... | collective-permute-start | bytes 3145736 | tf_op jit(solution)/shard_map/ppermute | solution.py:47
  91.3 27.9 %collective-permute-start.13 = (bf16[128,2048]{1,0:T(8,128)(2,1)S(1)}, bf16[128,2048]{1,0:T(8,128)(2,1)S(1)}, u32[]{:S(2)}, u32[]{:S(2)}) collective-permute-start(bf16[128,2048]{1,0:T(8,128)(2,1)S(1)} %select_convert_fusion), channel_id=1, source_target_pairs={{0,1},{1,0},{2,3},{3,2},{4,5},{5,4},{6,7},{7,6},{8,9},{9,8},{10,11... | collective-permute-start | bytes 1572872 | tf_op jit(solution)/shard_map/ppermute | solution.py:44
  102.2 17.6 %collective-permute-start.15 = (bf16[128,2048]{1,0:T(8,128)(2,1)S(1)}, bf16[128,2048]{1,0:T(8,128)(2,1)S(1)}, u32[]{:S(2)}, u32[]{:S(2)}) collective-permute-start(bf16[128,2048]{1,0:T(8,128)(2,1)S(1)} %fusion.23), channel_id=1, source_target_pairs={{0,2},{1,3},{2,0},{3,1},{4,6},{5,7},{6,4},{7,5},{8,14},{9,15},{10,... | collective-permute-start | bytes 1572872 | tf_op jit(solution)/shard_map/ppermute | solution.py:47
  119.8 15.9 %collective-permute-start.22 = (f32[128,1024]{1,0:T(8,128)S(1)}, f32[128,1024]{1,0:T(8,128)S(1)}, u32[]{:S(2)}, u32[]{:S(2)}) collective-permute-start(f32[128,1024]{1,0:T(8,128)S(1)} %slice.189), channel_id=1, source_target_pairs={{0,8},{8,0},{16,24},{24,16},{32,40},{40,32},{48,56},{56,48},{64,72... | collective-permute-start | bytes 1572872 | tf_op jit(solution)/shard_map/ppermute | solution.py:41
  120.2 9.9 %collective-permute-start.16 = (bf16[64,2048]{1,0:T(8,128)(2,1)S(1)}, bf16[64,2048]{1,0:T(8,128)(2,1)S(1)}, u32[]{:S(2)}, u32[]{:S(2)}) collective-permute-start(bf16[64,2048]{1,0:T(8,128)(2,1)S(1)} %select_convert_fusion.2), channel_id=1, source_target_pairs={{0,1},{1,0},{2,3},{3,2},{4,5},{5,4},{6,7},{7,6},{8,9},{9,8},{10,11... | collective-permute-start | bytes 786440 | tf_op jit(solution)/shard_map/ppermute | solution.py:44
  161.5 12.1 %collective-permute-start.32 = (bf16[384,1024]{1,0:T(8,128)(2,1)S(1)}, bf16[384,1024]{1,0:T(8,128)(2,1)S(1)}, u32[]{:S(2)}, u32[]{:S(2)}) collective-permute-start(bf16[384,1024]{1,0:T(8,128)(2,1)S(1)} %divide_convert_fusion), channel_id=1, source_target_pairs={{0,2},{1,3},{2,0},{3,1},{4,6},{5,7},{6,4},{7,5},{8,14},{9,15},{10,... | collective-permute-start | bytes 2359304 | tf_op jit(solution)/shard_map/ppermute | solution.py:47
  187.4 20.3 %collective-permute-start.39 = (bf16[768,1024]{1,0:T(8,128)(2,1)S(1)}, bf16[768,1024]{1,0:T(8,128)(2,1)S(1)}, u32[]{:S(2)}, u32[]{:S(2)}) collective-permute-start(bf16[768,1024]{1,0:T(8,128)(2,1)S(1)} %pad_maximum_fusion.1), channel_id=1, source_target_pairs={{0,6},{1,7},{2,4},{3,5},{4,2},{5,3},{6,0},{7,1},{8,10},{9,11},{10,... | collective-permute-start | bytes 4718600 | tf_op jit(solution)/shard_map/ppermute | solution.py:47
  221.4 13.5 %collective-permute-start.41 = (bf16[1024,256]{1,0:T(8,128)(2,1)}, bf16[1024,256]{1,0:T(8,128)(2,1)}, u32[]{:S(2)}, u32[]{:S(2)}) collective-permute-start(bf16[1024,256]{1,0:T(8,128)(2,1)} %fusion.14), channel_id=1, source_target_pairs={{0,1},{1,0},{2,3},{3,2},{4,5},{5,4},{6,7},{7,6},{8,9},{9,8},{10,11... | collective-permute-start | bytes 1572872 | tf_op jit(solution)/shard_map/ppermute | solution.py:44
  (29 other events, 154.5 us)

commit v3 on v2

--- a/solution.py
+++ b/solution.py
@@ -8,6 +8,7 @@
 F32 = jnp.float32
 BF16 = jnp.bfloat16
 RUNS = (64, 64)
+Z_FIRST = 2
 
 
 def body(context, out_weight, residual, norm_gain, span_lengths, projector, student):
@@ -81,6 +82,7 @@
         ]
         return kept[0], over_both(kept[1].astype(BF16), y_near)
 
+    same = zl == zh
     units, unit, coming = 2 + len(RUNS), first, first_far
     halves, firsts, seconds, all_terms = ([None] * units for _ in range(4))
     for j in range(units):
@@ -100,6 +102,11 @@
         if 2 <= j < units - 1:
             terms, seconds[j - 2] = tie(terms, seconds[j - 2])
         all_terms[j] = terms.reshape(xs, -1, 2 * width)
+        if j == Z_FIRST:
+            own, other = all_terms[j][:, : RUNS[j - 2]], all_terms[j][:, RUNS[j - 2] :]
+            held, away = jnp.where(same, own, other), jnp.where(same, other, own)
+            held = held.astype(F32) + over_col(away, z_near).astype(F32)
+            all_terms[j] = held.astype(BF16)
         firsts[j] = over_both(
             jnp.stack([toward(all_terms[j], following), toward(all_terms[j], 2)]), y_next
         )
@@ -112,10 +119,12 @@
     halves[-1], seconds[-1] = second_of(all_terms[-1], firsts[-1])
     sums = [half + second.astype(F32) for half, second in zip(halves, seconds)]
 
-    same = zl == zh
     attended = []
     pairs = [(sums[0], sums[1])] + [(value[:run], value[run:]) for value, run in zip(sums[2:], RUNS)]
-    for own, other in pairs:
+    for j, (own, other) in enumerate(pairs):
+        if j + 1 == Z_FIRST:
+            attended.append(sums[j + 1])
+            continue
         held, away = jnp.where(same, own, other), jnp.where(same, other, own)
         attended.append(held + over_col(away.astype(BF16), z_near).astype(F32))
     held = jnp.concatenate([value[:, :width] for value in attended])

time: 237 us -> 231 us (0.975)
  waiting for transfers between devices: 123 us -> 117 us
    ppermute x12, waiting for transfers between devices: 44 us -> 15.5 us  [over_both(): return lax.ppermute(value, ('row', 'col'), pairs)]
    ppermute x5, waiting for transfers between devices: 15.9 us -> 36.8 us  [over_col(): return lax.ppermute(value, 'col', pairs)]
    ppermute x12, starting transfers between devices: 15.7 us -> 10.9 us  [over_both(): return lax.ppermute(value, ('row', 'col'), pairs)]
    ppermute x25, starting transfers between devices: 37.3 us -> 41.5 us  [over_row(): return lax.ppermute(value, 'row', pairs)]
  transfers between devices with their start and end apart: 42 -> 42, of which waited for: 32 -> 29; matrix products, arithmetic and copies ran while one was open for 15% -> 16% of each run, Pallas kernels for 0% -> 0%
where the time goes in v3:
time: 231 us
  waiting for transfers between devices  117 us (51%)
  starting transfers between devices  61.1 us (26%)
  matrix products  28.1 us (12%)
  local copies, waits for them, and re-layouts  14.7 us (6%)
  other arithmetic  8.21 us (4%)
    ppermute x25, waiting for transfers between devices, over_row(): return lax.ppermute(value, 'row', pairs)  65.1 us
    ppermute x25, starting transfers between devices, over_row(): return lax.ppermute(value, 'row', pairs)  41.5 us
    ppermute x5, waiting for transfers between devices, over_col(): return lax.ppermute(value, 'col', pairs)  36.8 us
    dot_general x4, matrix products, body(): terms = jnp.dot(tokens, weight, preferred_element_type=F32).astype(BF16)  18.8 us
    ppermute x12, waiting for transfers between devices, over_both(): return lax.ppermute(value, ('row', 'col'), pairs)  15.5 us
    ppermute x12, starting transfers between devices, over_both(): return lax.ppermute(value, ('row', 'col'), pairs)  10.9 us
    ppermute x5, starting transfers between devices, over_col(): return lax.ppermute(value, 'col', pairs)  8.7 us
    unnamed x41, local copies, waits for them, and re-layouts  7.27 us
  transfers between devices with their start and end apart: 42, of which 29 were waited for; matrix products, arithmetic and copies ran while one was open for 16% of the time, Pallas kernels for 0%

profile of v3, /device:TPU:1, one launch (start us, length us, event | category | flops | bytes accessed | tf_op | source)
XLA Modules:
  0.0 230.9 jit_solution(15565527150148460121)
XLA Ops:
  6.1 3.6 %collective-permute-start = (bf16[128,2048]{1,0:T(8,128)(2,1)S(1)}, bf16[128,2048]{1,0:T(8,128)(2,1)S(1)}, u32[]{:S(2)}, u32[]{:S(2)}) collective-permute-start(bf16[128,2048]{1,0:T(8,128)(2,1)S(1)} %get-tuple-element.77), channel_id=1, source_target_pairs={{0,16},{8,24},{16,0},{24,8},{32,48},{40,56},{48,32},{56,40},{64,80... | collective-permute-start | bytes 1572872 | tf_op jit(solution)/shard_map/ppermute | solution.py:42
  17.3 4.8 %collective-permute-done = bf16[128,2048]{1,0:T(8,128)(2,1)S(1)} collective-permute-done((bf16[128,2048]{1,0:T(8,128)(2,1)S(1)}, bf16[128,2048]{1,0:T(8,128)(2,1)S(1)}, u32[]{:S(2)}, u32[]{:S(2)}) %collective-permute-start) | collective-permute-done | bytes 524320 | tf_op jit(solution)/shard_map/ppermute | solution.py:42
  25.0 10.0 %collective-permute-done.5 = bf16[128,2048]{1,0:T(8,128)(2,1)S(1)} collective-permute-done((bf16[128,2048]{1,0:T(8,128)(2,1)S(1)}, bf16[128,2048]{1,0:T(8,128)(2,1)S(1)}, u32[]{:S(2)}, u32[]{:S(2)}) %collective-permute-start.5) | collective-permute-done | bytes 524320 | tf_op jit(solution)/shard_map/ppermute | solution.py:42
  37.7 4.7 %convolution_convert_fusion.3 = bf16[512,2048]{1,0:T(8,128)(2,1)S(1)} fusion(bf16[2048,2048]{1,0:T(8,128)(2,1)S(1)} %constant_dynamic-update-slice_fusion.11, bf16[256,2048]{1,0:T(8,128)(2,1)S(1)} %collective-permute-done.3, bf16[256,2048]{1,0:T(8,128)(2,1)S(1)} %pad_maximum_fusion.5), kind=kOutput, calls=%fused_computation.4 | convolution fusion | flops 4300210176 | bytes 12582912 | tf_op jit(solution)/shard_map/dot_general | solution.py:99
  44.0 6.5 %collective-permute-done.8 = bf16[128,2048]{1,0:T(8,128)(2,1)S(1)} collective-permute-done((bf16[128,2048]{1,0:T(8,128)(2,1)S(1)}, bf16[128,2048]{1,0:T(8,128)(2,1)S(1)}, u32[]{:S(2)}, u32[]{:S(2)}) %collective-permute-start.8) | collective-permute-done | bytes 524320 | tf_op jit(solution)/shard_map/ppermute | solution.py:42
  54.6 4.7 %convolution_convert_fusion.2 = bf16[512,2048]{1,0:T(8,128)(2,1)S(1)} fusion(bf16[2048,2048]{1,0:T(8,128)(2,1)S(1)} %constant_dynamic-update-slice_fusion.11, bf16[256,2048]{1,0:T(8,128)(2,1)S(1)} %collective-permute-done.6, bf16[256,2048]{1,0:T(8,128)(2,1)S(1)} %constant_dynamic-update-slice_fusion.13), kind=kOutput, calls=%fused_computation.3 | convolution fusion | flops 4300210176 | bytes 12582912 | tf_op jit(solution)/shard_map/dot_general | solution.py:99
  66.5 5.0 %collective-permute-done.9 = bf16[256,2048]{1,0:T(8,128)(2,1)S(1)} collective-permute-done((bf16[256,2048]{1,0:T(8,128)(2,1)S(1)}, bf16[256,2048]{1,0:T(8,128)(2,1)S(1)}, u32[]{:S(2)}, u32[]{:S(2)}) %collective-permute-start.9) | collective-permute-done | bytes 1048608 | tf_op jit(solution)/shard_map/ppermute | solution.py:42
  71.5 4.8 %convolution_convert_fusion.1 = bf16[512,2048]{1,0:T(8,128)(2,1)S(1)} fusion(bf16[2048,2048]{1,0:T(8,128)(2,1)S(1)} %constant_dynamic-update-slice_fusion.11, bf16[256,2048]{1,0:T(8,128)(2,1)S(1)} %collective-permute-done.9, bf16[256,2048]{1,0:T(8,128)(2,1)S(1)} %get-tuple-element.108), kind=kOutput, calls=%fused_computation.2 | convolution fusion | flops 4300210176 | bytes 12582912 | tf_op jit(solution)/shard_map/dot_general | solution.py:99
  84.1 4.7 %convolution_convert_fusion = bf16[512,2048]{1,0:T(8,128)(2,1)S(1)} fusion(bf16[2048,2048]{1,0:T(8,128)(2,1)S(1)} %constant_dynamic-update-slice_fusion.11, bf16[256,2048]{1,0:T(8,128)(2,1)S(1)} %collective-permute-done.18, bf16[128,2048]{1,0:T(8,128)(2,1)S(1)} %collective-permute-done.17, bf16[128,2048]{1,0:T(8,128)(2,1)S(1)} %get-tuple-element.47), kind=kOutput, calls=%fused_computation.1 | convolution fusion | flops 4302307328 | bytes 12582912 | tf_op jit(solution)/shard_map/dot_general | solution.py:99
  91.3 15.8 %collective-permute-done.14 = bf16[4,64,2048]{2,1,0:T(8,128)(2,1)S(1)} collective-permute-done((bf16[4,64,2048]{2,1,0:T(8,128)(2,1)S(1)}, bf16[4,64,2048]{2,1,0:T(8,128)(2,1)S(1)}, u32[]{:S(2)}, u32[]{:S(2)}) %collective-permute-start.14) | collective-permute-done | bytes 1048608 | tf_op jit(solution)/shard_map/ppermute | solution.py:45
  108.2 10.2 %collective-permute-done.13 = bf16[128,2048]{1,0:T(8,128)(2,1)S(1)} collective-permute-done((bf16[128,2048]{1,0:T(8,128)(2,1)S(1)}, bf16[128,2048]{1,0:T(8,128)(2,1)S(1)}, u32[]{:S(2)}, u32[]{:S(2)}) %collective-permute-start.13) | collective-permute-done | bytes 524320 | tf_op jit(solution)/shard_map/ppermute | solution.py:45
  122.6 4.1 %collective-permute-done.16 = bf16[64,2048]{1,0:T(8,128)(2,1)S(1)} collective-permute-done((bf16[64,2048]{1,0:T(8,128)(2,1)S(1)}, bf16[64,2048]{1,0:T(8,128)(2,1)S(1)}, u32[]{:S(2)}, u32[]{:S(2)}) %collective-permute-start.16) | collective-permute-done | bytes 262176 | tf_op jit(solution)/shard_map/ppermute | solution.py:48
  126.8 3.6 %collective-permute-start.23 = (f32[64,1024]{1,0:T(8,128)S(1)}, f32[64,1024]{1,0:T(8,128)S(1)}, u32[]{:S(2)}, u32[]{:S(2)}) collective-permute-start(f32[64,1024]{1,0:T(8,128)S(1)} %slice.190), channel_id=1, source_target_pairs={{0,8},{8,0},{16,24},{24,16},{32,40},{40,32},{48,56},{56,48},{64,72... | collective-permute-start | bytes 786440 | tf_op jit(solution)/shard_map/ppermute | solution.py:42
  142.7 3.1 %collective-permute-start.28 = (f32[512]{0:T(512)S(1)}, f32[512]{0:T(512)S(1)}, u32[]{:S(2)}, u32[]{:S(2)}) collective-permute-start(f32[512]{0:T(512)S(1)} %add.213), channel_id=1, source_target_pairs={{0,16},{8,24},{16,0},{24,8},{32,48},{40,56},{48,32},{56,40},{64,80... | collective-permute-start | bytes 6152 | tf_op jit(solution)/shard_map/ppermute | solution.py:42
  146.7 3.0 %divide_convert_fusion = bf16[384,1024]{1,0:T(8,128)(2,1)S(1)} fusion(f32[1024]{0:T(1024)S(1)} %copy-done.10, f32[512]{0:T(512)S(1)} %add_rsqrt_fusion, f32[384]{0:T(512)S(1)} %convert_element_type.235, s32[384]{0:T(512)S(1)} %lt.91, s32[384]{0:T(512)S(1)} %ge.18, bf16[512,1024]{1,0:T(8,128)(2,1)} %param.9, ...), kind=kOutput, calls=%fused_computation.27 | convolution fusion | flops 407175168 | bytes 6040065 | tf_op jit(solution)/shard_map/dot_general | solution.py:156
  150.9 3.1 %collective-permute-start.29 = (bf16[192,2048]{1,0:T(8,128)(2,1)S(1)}, bf16[192,2048]{1,0:T(8,128)(2,1)S(1)}, u32[]{:S(2)}, u32[]{:S(2)}) collective-permute-start(bf16[192,2048]{1,0:T(8,128)(2,1)S(1)} %convolution_convert_fusion.4), channel_id=1, source_target_pairs={{0,8},{8,0},{16,24},{24,16},{32,40},{40,32},{48,56},{56,48},{64,72... | collective-permute-start | bytes 2359304 | tf_op jit(solution)/shard_map/ppermute | solution.py:42
  157.7 6.3 %collective-permute-done.30 = bf16[2,2,24,2048]{3,2,1,0:T(8,128)(2,1)S(1)} collective-permute-done((bf16[2,2,24,2048]{3,2,1,0:T(8,128)(2,1)S(1)}, bf16[2,2,24,2048]{3,2,1,0:T(8,128)(2,1)S(1)}, u32[]{:S(2)}, u32[]{:S(2)}) %collective-permute-start.30) | collective-permute-done | bytes 393248 | tf_op jit(solution)/shard_map/ppermute | solution.py:42
  166.0 3.3 %collective-permute-done.32 = bf16[384,1024]{1,0:T(8,128)(2,1)S(1)} collective-permute-done((bf16[384,1024]{1,0:T(8,128)(2,1)S(1)}, bf16[384,1024]{1,0:T(8,128)(2,1)S(1)}, u32[]{:S(2)}, u32[]{:S(2)}) %collective-permute-start.32) | collective-permute-done | bytes 786464 | tf_op jit(solution)/shard_map/ppermute | solution.py:48
  170.0 3.1 %collective-permute-start.33 = (bf16[2,24,2048]{2,1,0:T(8,128)(2,1)S(1)}, bf16[2,24,2048]{2,1,0:T(8,128)(2,1)S(1)}, u32[]{:S(2)}, u32[]{:S(2)}) collective-permute-start(bf16[2,24,2048]{2,1,0:T(8,128)(2,1)S(1)} %rev.14), channel_id=1, source_target_pairs={{0,16},{8,24},{16,0},{24,8},{32,48},{40,56},{48,32},{56,40},{64,80... | collective-permute-start | bytes 589832 | tf_op jit(solution)/shard_map/ppermute | solution.py:42
  185.2 4.3 %collective-permute-done.37 = bf16[1,4,48,512]{3,2,0,1:T(8,128)(2,1)S(1)} collective-permute-done((bf16[1,4,48,512]{3,2,0,1:T(8,128)(2,1)S(1)}, bf16[1,4,48,512]{3,2,0,1:T(8,128)(2,1)S(1)}, u32[]{:S(2)}, u32[]{:S(2)}) %collective-permute-start.37) | collective-permute-done | bytes 196640 | tf_op jit(solution)/shard_map/ppermute | solution.py:42
  189.7 9.0 %collective-permute-done.38 = bf16[2,4,48,512]{3,2,0,1:T(8,128)(2,1)S(1)} collective-permute-done((bf16[2,4,48,512]{3,2,0,1:T(8,128)(2,1)S(1)}, bf16[2,4,48,512]{3,2,0,1:T(8,128)(2,1)S(1)}, u32[]{:S(2)}, u32[]{:S(2)}) %collective-permute-start.38) | collective-permute-done | bytes 393248 | tf_op jit(solution)/shard_map/ppermute | solution.py:42
  198.7 3.9 %collective-permute-done.39 = bf16[768,1024]{1,0:T(8,128)(2,1)S(1)} collective-permute-done((bf16[768,1024]{1,0:T(8,128)(2,1)S(1)}, bf16[768,1024]{1,0:T(8,128)(2,1)S(1)}, u32[]{:S(2)}, u32[]{:S(2)}) %collective-permute-start.39) | collective-permute-done | bytes 1572896 | tf_op jit(solution)/shard_map/ppermute | solution.py:48
  203.7 6.1 %collective-permute-start.40 = (bf16[4,4,48,512]{3,2,0,1:T(8,128)(2,1)S(1)}, bf16[4,4,48,512]{3,2,0,1:T(8,128)(2,1)S(1)}, u32[]{:S(2)}, u32[]{:S(2)}) collective-permute-start(bf16[4,4,48,512]{3,2,0,1:T(8,128)(2,1)S(1)} %get-tuple-element.79), channel_id=1, source_target_pairs={{0,8},{8,0},{16,24},{24,16},{32,40},{40,32},{48,56},{56,48},{64,72... | collective-permute-start | bytes 2359304 | tf_op jit(solution)/shard_map/ppermute | solution.py:42
  219.7 9.1 %collective-permute-done.41 = bf16[1024,256]{1,0:T(8,128)(2,1)} collective-permute-done((bf16[1024,256]{1,0:T(8,128)(2,1)}, bf16[1024,256]{1,0:T(8,128)(2,1)}, u32[]{:S(2)}, u32[]{:S(2)}) %collective-permute-start.41) | collective-permute-done | bytes 524320 | tf_op jit(solution)/shard_map/ppermute | solution.py:45
  (189 shorter events, 92.8 us)
Async XLA Ops:
  0.6 12.4 %collective-permute-start.2 = (bf16[2048,1024]{1,0:T(8,128)(2,1)}, bf16[2048,1024]{1,0:T(8,128)(2,1)}, u32[]{:S(2)}, u32[]{:S(2)}) collective-permute-start(bf16[2048,1024]{1,0:T(8,128)(2,1)} %param.8), channel_id=1, source_target_pairs={{0,8},{8,0},{16,24},{24,16},{32,40},{40,32},{48,56},{56,48},{64,72... | collective-permute-start | bytes 12582920 | tf_op jit(solution)/shard_map/ppermute | solution.py:42
  3.4 9.6 %collective-permute-start.1 = (bf16[128,2048]{1,0:T(8,128)(2,1)S(1)}, bf16[128,2048]{1,0:T(8,128)(2,1)}, u32[]{:S(2)}, u32[]{:S(2)}) collective-permute-start(bf16[128,2048]{1,0:T(8,128)(2,1)S(1)} %get-tuple-element.77), channel_id=1, source_target_pairs={{0,32},{8,104},{16,48},{24,120},{32,0},{40,72},{48,16},{56,88},{64... | collective-permute-start | bytes 1572872 | tf_op jit(solution)/shard_map/ppermute | solution.py:42
  6.1 16.0 %collective-permute-start = (bf16[128,2048]{1,0:T(8,128)(2,1)S(1)}, bf16[128,2048]{1,0:T(8,128)(2,1)S(1)}, u32[]{:S(2)}, u32[]{:S(2)}) collective-permute-start(bf16[128,2048]{1,0:T(8,128)(2,1)S(1)} %get-tuple-element.77), channel_id=1, source_target_pairs={{0,16},{8,24},{16,0},{24,8},{32,48},{40,56},{48,32},{56,40},{64,80... | collective-permute-start | bytes 1572872 | tf_op jit(solution)/shard_map/ppermute | solution.py:42
  9.7 25.5 %collective-permute-start.4 = (bf16[128,2048]{1,0:T(8,128)(2,1)S(1)}, bf16[128,2048]{1,0:T(8,128)(2,1)S(1)}, u32[]{:S(2)}, u32[]{:S(2)}) collective-permute-start(bf16[128,2048]{1,0:T(8,128)(2,1)S(1)} %get-tuple-element.76), channel_id=1, source_target_pairs={{0,16},{8,24},{16,0},{24,8},{32,48},{40,56},{48,32},{56,40},{64,80... | collective-permute-start | bytes 1572872 | tf_op jit(solution)/shard_map/ppermute | solution.py:42
  14.2 21.0 %collective-permute-start.3 = (bf16[256,2048]{1,0:T(8,128)(2,1)S(1)}, bf16[256,2048]{1,0:T(8,128)(2,1)S(1)}, u32[]{:S(2)}, u32[]{:S(2)}) collective-permute-start(bf16[256,2048]{1,0:T(8,128)(2,1)S(1)} %pad_maximum_fusion.5), channel_id=1, source_target_pairs={{0,96},{8,40},{16,112},{24,56},{32,64},{40,8},{48,80},{56,24},{64,... | collective-permute-start | bytes 3145736 | tf_op jit(solution)/shard_map/ppermute | solution.py:42
  22.1 12.8 %collective-permute-start.5 = (bf16[128,2048]{1,0:T(8,128)(2,1)S(1)}, bf16[128,2048]{1,0:T(8,128)(2,1)S(1)}, u32[]{:S(2)}, u32[]{:S(2)}) collective-permute-start(bf16[128,2048]{1,0:T(8,128)(2,1)S(1)} %collective-permute-done), channel_id=1, source_target_pairs={{0,32},{8,104},{16,48},{24,120},{32,0},{40,72},{48,16},{56,88},{64... | collective-permute-start | bytes 1572872 | tf_op jit(solution)/shard_map/ppermute | solution.py:42
  35.0 19.6 %collective-permute-start.6 = (bf16[256,2048]{1,0:T(8,128)(2,1)S(1)}, bf16[256,2048]{1,0:T(8,128)(2,1)S(1)}, u32[]{:S(2)}, u32[]{:S(2)}) collective-permute-start(bf16[256,2048]{1,0:T(8,128)(2,1)S(1)} %constant_dynamic-update-slice_fusion.13), channel_id=1, source_target_pairs={{0,96},{8,40},{16,112},{24,56},{32,64},{40,8},{48,80},{56,24},{64,... | collective-permute-start | bytes 3145736 | tf_op jit(solution)/shard_map/ppermute | solution.py:42
  35.3 15.2 %collective-permute-start.8 = (bf16[128,2048]{1,0:T(8,128)(2,1)S(1)}, bf16[128,2048]{1,0:T(8,128)(2,1)S(1)}, u32[]{:S(2)}, u32[]{:S(2)}) collective-permute-start(bf16[128,2048]{1,0:T(8,128)(2,1)S(1)} %pad_maximum_fusion.11), channel_id=1, source_target_pairs={{0,32},{8,104},{16,48},{24,120},{32,0},{40,72},{48,16},{56,88},{64... | collective-permute-start | bytes 1572872 | tf_op jit(solution)/shard_map/ppermute | solution.py:42
  42.6 16.8 %collective-permute-start.7 = (bf16[2,128,2048]{2,1,0:T(8,128)(2,1)S(1)}, bf16[2,128,2048]{2,1,0:T(8,128)(2,1)S(1)}, u32[]{:S(2)}, u32[]{:S(2)}) collective-permute-start(bf16[2,128,2048]{2,1,0:T(8,128)(2,1)S(1)} %pad_maximum_fusion.6), channel_id=1, source_target_pairs={{0,6},{1,7},{2,4},{3,5},{4,2},{5,3},{6,0},{7,1},{8,10},{9,11},{10,... | collective-permute-start | bytes 3145736 | tf_op jit(solution)/shard_map/ppermute | solution.py:48
  50.5 21.0 %collective-permute-start.9 = (bf16[256,2048]{1,0:T(8,128)(2,1)S(1)}, bf16[256,2048]{1,0:T(8,128)(2,1)S(1)}, u32[]{:S(2)}, u32[]{:S(2)}) collective-permute-start(bf16[256,2048]{1,0:T(8,128)(2,1)S(1)} %get-tuple-element.108), channel_id=1, source_target_pairs={{0,96},{8,40},{16,112},{24,56},{32,64},{40,8},{48,80},{56,24},{64,... | collective-permute-start | bytes 3145736 | tf_op jit(solution)/shard_map/ppermute | solution.py:42
  51.2 14.3 %collective-permute-start.17 = (bf16[128,2048]{1,0:T(8,128)(2,1)S(1)}, bf16[128,2048]{1,0:T(8,128)(2,1)S(1)}, u32[]{:S(2)}, u32[]{:S(2)}) collective-permute-start(bf16[128,2048]{1,0:T(8,128)(2,1)S(1)} %get-tuple-element.47), channel_id=1, source_target_pairs={{0,32},{8,104},{16,48},{24,120},{32,0},{40,72},{48,16},{56,88},{64... | collective-permute-start | bytes 1572872 | tf_op jit(solution)/shard_map/ppermute | solution.py:42
  59.6 19.6 %collective-permute-start.10 = (bf16[2,128,2048]{2,1,0:T(8,128)(2,1)S(1)}, bf16[2,128,2048]{2,1,0:T(8,128)(2,1)S(1)}, u32[]{:S(2)}, u32[]{:S(2)}) collective-permute-start(bf16[2,128,2048]{2,1,0:T(8,128)(2,1)S(1)} %pad_maximum_fusion.7), channel_id=1, source_target_pairs={{0,6},{1,7},{2,4},{3,5},{4,2},{5,3},{6,0},{7,1},{8,10},{9,11},{10,... | collective-permute-start | bytes 3145736 | tf_op jit(solution)/shard_map/ppermute | solution.py:48
  61.1 18.1 %collective-permute-start.11 = (bf16[128,2048]{1,0:T(8,128)(2,1)S(1)}, bf16[128,2048]{1,0:T(8,128)(2,1)S(1)}, u32[]{:S(2)}, u32[]{:S(2)}) collective-permute-start(bf16[128,2048]{1,0:T(8,128)(2,1)S(1)} %fusion.21), channel_id=1, source_target_pairs={{0,2},{1,3},{2,0},{3,1},{4,6},{5,7},{6,4},{7,5},{8,14},{9,15},{10,... | collective-permute-start | bytes 1572872 | tf_op jit(solution)/shard_map/ppermute | solution.py:48
  65.7 18.4 %collective-permute-start.18 = (bf16[256,2048]{1,0:T(8,128)(2,1)S(1)}, bf16[256,2048]{1,0:T(8,128)(2,1)S(1)}, u32[]{:S(2)}, u32[]{:S(2)}) collective-permute-start(bf16[256,2048]{1,0:T(8,128)(2,1)S(1)} %pad_maximum_fusion.8), channel_id=1, source_target_pairs={{0,96},{8,40},{16,112},{24,56},{32,64},{40,8},{48,80},{56,24},{64,... | collective-permute-start | bytes 3145736 | tf_op jit(solution)/shard_map/ppermute | solution.py:42
  79.3 9.8 %collective-permute-start.12 = (bf16[128,2048]{1,0:T(8,128)(2,1)S(1)}, bf16[128,2048]{1,0:T(8,128)(2,1)S(1)}, u32[]{:S(2)}, u32[]{:S(2)}) collective-permute-start(bf16[128,2048]{1,0:T(8,128)(2,1)S(1)} %fusion.22), channel_id=1, source_target_pairs={{0,2},{1,3},{2,0},{3,1},{4,6},{5,7},{6,4},{7,5},{8,14},{9,15},{10,... | collective-permute-start | bytes 1572872 | tf_op jit(solution)/shard_map/ppermute | solution.py:48
  82.3 24.8 %collective-permute-start.14 = (bf16[4,64,2048]{2,1,0:T(8,128)(2,1)S(1)}, bf16[4,64,2048]{2,1,0:T(8,128)(2,1)S(1)}, u32[]{:S(2)}, u32[]{:S(2)}) collective-permute-start(bf16[4,64,2048]{2,1,0:T(8,128)(2,1)S(1)} %broadcast_select_fusion), channel_id=1, source_target_pairs={{0,1},{1,0},{2,3},{3,2},{4,5},{5,4},{6,7},{7,6},{8,9},{9,8},{10,11... | collective-permute-start | bytes 3145736 | tf_op jit(solution)/shard_map/ppermute | solution.py:45
  89.0 18.9 %collective-permute-start.19 = (bf16[2,128,2048]{2,1,0:T(8,128)(2,1)S(1)}, bf16[2,128,2048]{2,1,0:T(8,128)(2,1)S(1)}, u32[]{:S(2)}, u32[]{:S(2)}) collective-permute-start(bf16[2,128,2048]{2,1,0:T(8,128)(2,1)S(1)} %pad_maximum_fusion.9), channel_id=1, source_target_pairs={{0,6},{1,7},{2,4},{3,5},{4,2},{5,3},{6,0},{7,1},{8,10},{9,11},{10,... | collective-permute-start | bytes 3145736 | tf_op jit(solution)/shard_map/ppermute | solution.py:48
  89.6 28.7 %collective-permute-start.13 = (bf16[128,2048]{1,0:T(8,128)(2,1)S(1)}, bf16[128,2048]{1,0:T(8,128)(2,1)S(1)}, u32[]{:S(2)}, u32[]{:S(2)}) collective-permute-start(bf16[128,2048]{1,0:T(8,128)(2,1)S(1)} %select_convert_fusion), channel_id=1, source_target_pairs={{0,1},{1,0},{2,3},{3,2},{4,5},{5,4},{6,7},{7,6},{8,9},{9,8},{10,11... | collective-permute-start | bytes 1572872 | tf_op jit(solution)/shard_map/ppermute | solution.py:45
  107.8 12.3 %collective-permute-start.15 = (bf16[2,64,2048]{2,1,0:T(8,128)(2,1)S(1)}, bf16[2,64,2048]{2,1,0:T(8,128)(2,1)S(1)}, u32[]{:S(2)}, u32[]{:S(2)}) collective-permute-start(bf16[2,64,2048]{2,1,0:T(8,128)(2,1)S(1)} %pad_maximum_fusion.13), channel_id=1, source_target_pairs={{0,6},{1,7},{2,4},{3,5},{4,2},{5,3},{6,0},{7,1},{8,10},{9,11},{10,... | collective-permute-start | bytes 1572872 | tf_op jit(solution)/shard_map/ppermute | solution.py:48
  108.1 13.2 %collective-permute-start.20 = (bf16[128,2048]{1,0:T(8,128)(2,1)S(1)}, bf16[128,2048]{1,0:T(8,128)(2,1)S(1)}, u32[]{:S(2)}, u32[]{:S(2)}) collective-permute-start(bf16[128,2048]{1,0:T(8,128)(2,1)S(1)} %fusion.23), channel_id=1, source_target_pairs={{0,2},{1,3},{2,0},{3,1},{4,6},{5,7},{6,4},{7,5},{8,14},{9,15},{10,... | collective-permute-start | bytes 1572872 | tf_op jit(solution)/shard_map/ppermute | solution.py:48
  119.0 12.9 %collective-permute-start.22 = (f32[128,1024]{1,0:T(8,128)S(1)}, f32[128,1024]{1,0:T(8,128)S(1)}, u32[]{:S(2)}, u32[]{:S(2)}) collective-permute-start(f32[128,1024]{1,0:T(8,128)S(1)} %slice.189), channel_id=1, source_target_pairs={{0,8},{8,0},{16,24},{24,16},{32,40},{40,32},{48,56},{56,48},{64,72... | collective-permute-start | bytes 1572872 | tf_op jit(solution)/shard_map/ppermute | solution.py:42
  157.1 12.1 %collective-permute-start.32 = (bf16[384,1024]{1,0:T(8,128)(2,1)S(1)}, bf16[384,1024]{1,0:T(8,128)(2,1)S(1)}, u32[]{:S(2)}, u32[]{:S(2)}) collective-permute-start(bf16[384,1024]{1,0:T(8,128)(2,1)S(1)} %divide_convert_fusion), channel_id=1, source_target_pairs={{0,2},{1,3},{2,0},{3,1},{4,6},{5,7},{6,4},{7,5},{8,14},{9,15},{10,... | collective-permute-start | bytes 2359304 | tf_op jit(solution)/shard_map/ppermute | solution.py:48
  182.4 20.2 %collective-permute-start.39 = (bf16[768,1024]{1,0:T(8,128)(2,1)S(1)}, bf16[768,1024]{1,0:T(8,128)(2,1)S(1)}, u32[]{:S(2)}, u32[]{:S(2)}) collective-permute-start(bf16[768,1024]{1,0:T(8,128)(2,1)S(1)} %pad_maximum_fusion.1), channel_id=1, source_target_pairs={{0,6},{1,7},{2,4},{3,5},{4,2},{5,3},{6,0},{7,1},{8,10},{9,11},{10,... | collective-permute-start | bytes 4718600 | tf_op jit(solution)/shard_map/ppermute | solution.py:48
  215.3 13.5 %collective-permute-start.41 = (bf16[1024,256]{1,0:T(8,128)(2,1)}, bf16[1024,256]{1,0:T(8,128)(2,1)}, u32[]{:S(2)}, u32[]{:S(2)}) collective-permute-start(bf16[1024,256]{1,0:T(8,128)(2,1)} %fusion.14), channel_id=1, source_target_pairs={{0,1},{1,0},{2,3},{3,2},{4,5},{5,4},{6,7},{7,6},{8,9},{9,8},{10,11... | collective-permute-start | bytes 1572872 | tf_op jit(solution)/shard_map/ppermute | solution.py:45
  (29 other events, 153.1 us)

commit v4 on v2

--- a/solution.py
+++ b/solution.py
@@ -81,10 +81,11 @@
         ]
         return kept[0], over_both(kept[1].astype(BF16), y_near)
 
+    same = zl == zh
     units, unit, coming = 2 + len(RUNS), first, first_far
     halves, firsts, seconds, all_terms = ([None] * units for _ in range(4))
     for j in range(units):
-        if j >= 2:
+        if j >= 2 and j - 2 != units - 2:
             paired, all_terms[j - 2] = tie(paired, all_terms[j - 2])
         lane = jnp.concatenate([unit, paired])
         others = over_row(lane, x_next)
@@ -95,27 +96,51 @@
             coming_paired = over_row(coming, x_near)
         tokens = jnp.concatenate([lane, others])
         terms = jnp.dot(tokens, weight, preferred_element_type=F32).astype(BF16)
-        if 1 <= j < units - 1:
+        arrived_pair = coming_paired if j + 1 < units else None
+        arrived_unit = coming
+        if j + 2 < units:
+            coming = later_unit(j)
+        z_first = j == units - 2
+        if z_first:
+            by_place = terms.reshape(xs, 2, RUNS[j - 2], 2 * width)
+            held, away = (
+                lax.dynamic_index_in_dim(by_place, place, 1, keepdims=False)
+                for place in (jnp.bitwise_xor(zl, zh), 1 - jnp.bitwise_xor(zl, zh))
+            )
+            swapped = over_col(away, z_near)
+            held, firsts[j - 1], seconds[j - 2] = tie(held, firsts[j - 1], seconds[j - 2])
+            terms = held, swapped
+        elif j == 1:
             terms, firsts[j - 1] = tie(terms, firsts[j - 1])
-        if 2 <= j < units - 1:
-            terms, seconds[j - 2] = tie(terms, seconds[j - 2])
-        all_terms[j] = terms.reshape(xs, -1, 2 * width)
+        all_terms[j] = terms if z_first else terms.reshape(xs, -1, 2 * width)
+        if z_first:
+            if j + 1 < units:
+                unit, paired = arrived_unit, arrived_pair
+            halves[j - 1], seconds[j - 1] = second_of(all_terms[j - 1], firsts[j - 1])
+            continue
         firsts[j] = over_both(
             jnp.stack([toward(all_terms[j], following), toward(all_terms[j], 2)]), y_next
         )
-        if j >= 1:
+        if j >= 1 and j - 1 != units - 2:
             halves[j - 1], seconds[j - 1] = second_of(all_terms[j - 1], firsts[j - 1])
         if j + 1 < units:
-            unit, paired = coming, coming_paired
-        if j + 2 < units:
-            coming = later_unit(j)
+            unit, paired = arrived_unit, arrived_pair
+    held, swapped = all_terms[-2]
+    swapped, firsts[-1] = tie(swapped, firsts[-1])
     halves[-1], seconds[-1] = second_of(all_terms[-1], firsts[-1])
+    all_terms[-2] = (held.astype(F32) + swapped.astype(F32)).astype(BF16)
+    firsts[-2] = over_both(
+        jnp.stack([toward(all_terms[-2], following), toward(all_terms[-2], 2)]), y_next
+    )
+    halves[-2], seconds[-2] = second_of(all_terms[-2], firsts[-2])
     sums = [half + second.astype(F32) for half, second in zip(halves, seconds)]
 
-    same = zl == zh
     attended = []
     pairs = [(sums[0], sums[1])] + [(value[:run], value[run:]) for value, run in zip(sums[2:], RUNS)]
-    for own, other in pairs:
+    for j, (own, other) in enumerate(pairs):
+        if j + 1 == units - 2:
+            attended.append(sums[j + 1])
+            continue
         held, away = jnp.where(same, own, other), jnp.where(same, other, own)
         attended.append(held + over_col(away.astype(BF16), z_near).astype(F32))
     held = jnp.concatenate([value[:, :width] for value in attended])
@@ -146,7 +171,7 @@
     member = (positions[None, :] >= starts[:, None]) & (positions[None, :] < ends[:, None])
     summed = jnp.dot(member.astype(BF16), hidden, preferred_element_type=F32)
     pooled = (summed / sizes.astype(F32)[:, None]).astype(BF16)
-    pooled_near = over_both(pooled, y_near)
+    pooled_near, pooled_next = over_both(pooled, y_near), over_both(pooled, y_next)
 
     features = projector.shape[1]
     given = jnp.dot(pooled[count // 2 :], projector, preferred_element_type=F32).astype(BF16)
@@ -155,8 +180,7 @@
     proj = proj.reshape(xs, 2, block, features)
     arrived = over_row(proj[2:].astype(BF16), x_next)
     proj = proj[:2] + arrived.astype(F32)
-    arrived, pooled_near = tie(over_row(proj[1].astype(BF16), x_near), pooled_near)
-    proj = proj[0] + arrived.astype(F32)
+    proj = proj[0] + over_row(proj[1].astype(BF16), x_near).astype(F32)
     full_proj = proj + over_row(proj[::-1].astype(BF16), z_far).astype(F32)
     places = [x * 4 + jnp.bitwise_xor(zh, kz) * 2 + core for kz in range(2)]
     student_rows = [lax.dynamic_slice_in_dim(student[0], place * block, block, 0) for place in places]
@@ -174,9 +198,9 @@
         over_both(quarter(following), y_next),
         over_col(quarter(2), y_far),
     ]
-    part, pooled_near = tie(part, pooled_near)
-    pooled_lane = jnp.concatenate([pooled, pooled_near])
-    pooled_rest = over_both(pooled_lane, y_next)
+    part, pooled_near, pooled_next = tie(part, pooled_near, pooled_next)
+    pooled_lane = jnp.concatenate([pooled, pooled_near, pooled_next])
+    pooled_rest = over_both(pooled_near, y_next)
     part = jnp.stack(part)[None]
     paired = over_row(part, x_near)
     part = jnp.concatenate([part, paired])

time: 237 us -> 226 us (0.954)
  waiting for transfers between devices: 123 us -> 108 us
  matrix products: 28.2 us -> 32.9 us
  local copies, waits for them, and re-layouts: 14.7 us -> 18.1 us
  starting transfers between devices: 61.3 us -> 58 us
    ppermute x12 -> x13, waiting for transfers between devices: 44 us -> 14.3 us  [over_both(): return lax.ppermute(value, ('row', 'col'), pairs)]
    ppermute x5, waiting for transfers between devices: 15.9 us -> 27.1 us  [over_col(): return lax.ppermute(value, 'col', pairs)]
    ppermute x25, starting transfers between devices: 37.3 us -> 33.6 us  [over_row(): return lax.ppermute(value, 'row', pairs)]
    dot_general x4, matrix products: 18.8 us -> 22.5 us  [body(): terms = jnp.dot(tokens, weight, preferred_element_type=F32).astype(BF16)]
    ppermute x25, waiting for transfers between devices: 63.4 us -> 66.7 us  [over_row(): return lax.ppermute(value, 'row', pairs)]
    ppermute x12 -> x13, starting transfers between devices: 15.7 us -> 18.6 us  [over_both(): return lax.ppermute(value, ('row', 'col'), pairs)]
    ppermute x5, starting transfers between devices: 8.32 us -> 5.72 us  [over_col(): return lax.ppermute(value, 'col', pairs)]
    unnamed x41 -> x43, local copies, waits for them, and re-layouts: 7.29 us -> 7.67 us
  transfers between devices with their start and end apart: 42 -> 43, of which waited for: 32 -> 30; matrix products, arithmetic and copies ran while one was open for 15% -> 20% of each run, Pallas kernels for 0% -> 0%
where the time goes in v4:
time: 226 us; the launch traced here: 225 us
  waiting for transfers between devices  108 us (48%)
  starting transfers between devices  58 us (26%)
  matrix products  32.9 us (15%)
  local copies, waits for them, and re-layouts  18.1 us (8%)
  other arithmetic  6.77 us (3%)
    ppermute x25, waiting for transfers between devices, over_row(): return lax.ppermute(value, 'row', pairs)  66.7 us
    ppermute x25, starting transfers between devices, over_row(): return lax.ppermute(value, 'row', pairs)  33.6 us
    ppermute x5, waiting for transfers between devices, over_col(): return lax.ppermute(value, 'col', pairs)  27.1 us
    dot_general x4, matrix products, body(): terms = jnp.dot(tokens, weight, preferred_element_type=F32).astype(BF16)  22.5 us
    ppermute x13, starting transfers between devices, over_both(): return lax.ppermute(value, ('row', 'col'), pairs)  18.6 us
    ppermute x13, waiting for transfers between devices, over_both(): return lax.ppermute(value, ('row', 'col'), pairs)  14.3 us
    unnamed x43, local copies, waits for them, and re-layouts  7.67 us
    dot_general x2, matrix products, outer(): lax.dot_general(all_pooled, columns, (((0,), (0,)), ((), ())), preferred_...  5.74 us
  transfers between devices with their start and end apart: 43, of which 30 were waited for; matrix products, arithmetic and copies ran while one was open for 20% of the time, Pallas kernels for 0%

profile of v4, /device:TPU:1, one launch (start us, length us, event | category | flops | bytes accessed | tf_op | source)
XLA Modules:
  0.0 225.4 jit_solution(13795884385744843564)
XLA Ops:
  6.8 3.6 %collective-permute-start = (bf16[128,2048]{1,0:T(8,128)(2,1)S(1)}, bf16[128,2048]{1,0:T(8,128)(2,1)S(1)}, u32[]{:S(2)}, u32[]{:S(2)}) collective-permute-start(bf16[128,2048]{1,0:T(8,128)(2,1)S(1)} %get-tuple-element.79), channel_id=1, source_target_pairs={{0,16},{8,24},{16,0},{24,8},{32,48},{40,56},{48,32},{56,40},{64,80... | collective-permute-start | bytes 1572872 | tf_op jit(solution)/shard_map/ppermute | solution.py:41
  11.6 4.8 %constant_dynamic-update-slice_fusion.12 = bf16[2048,2048]{1,0:T(8,128)(2,1)} fusion(bf16[2048,1024]{1,0:T(8,128)(2,1)} %param.8), kind=kLoop, calls=%fused_computation.101 | loop fusion | bytes 8388608
  17.9 4.9 %collective-permute-done = bf16[128,2048]{1,0:T(8,128)(2,1)S(1)} collective-permute-done((bf16[128,2048]{1,0:T(8,128)(2,1)S(1)}, bf16[128,2048]{1,0:T(8,128)(2,1)S(1)}, u32[]{:S(2)}, u32[]{:S(2)}) %collective-permute-start) | collective-permute-done | bytes 524320 | tf_op jit(solution)/shard_map/ppermute | solution.py:41
  22.9 4.8 %constant_dynamic-update-slice_fusion.11 = bf16[2048,2048]{1,0:T(8,128)(2,1)} fusion(bf16[2048,2048]{1,0:T(8,128)(2,1)} %constant_dynamic-update-slice_fusion.12, bf16[2048,1024]{1,0:T(8,128)(2,1)} %collective-permute-done.2), kind=kLoop, calls=%fused_computation.100 | loop fusion | bytes 8388608 | tf_op jit(solution)/shard_map/concatenate | solution.py:68
  27.6 10.5 %collective-permute-done.5 = bf16[128,2048]{1,0:T(8,128)(2,1)S(1)} collective-permute-done((bf16[128,2048]{1,0:T(8,128)(2,1)S(1)}, bf16[128,2048]{1,0:T(8,128)(2,1)S(1)}, u32[]{:S(2)}, u32[]{:S(2)}) %collective-permute-start.5) | collective-permute-done | bytes 524320 | tf_op jit(solution)/shard_map/ppermute | solution.py:41
  38.5 8.3 %convolution_convert_fusion.3 = bf16[512,2048]{1,0:T(8,128)(2,1)S(1)} fusion(bf16[2048,2048]{1,0:T(8,128)(2,1)} %constant_dynamic-update-slice_fusion.11, bf16[256,2048]{1,0:T(8,128)(2,1)} %collective-permute-done.3, bf16[256,2048]{1,0:T(8,128)(2,1)S(1)} %pad_maximum_fusion.2), kind=kOutput, calls=%fused_computation.4 | convolution fusion | flops 4300210176 | bytes 12582912 | tf_op jit(solution)/shard_map/dot_general | solution.py:98
  48.5 5.2 %collective-permute-done.8 = bf16[128,2048]{1,0:T(8,128)(2,1)S(1)} collective-permute-done((bf16[128,2048]{1,0:T(8,128)(2,1)S(1)}, bf16[128,2048]{1,0:T(8,128)(2,1)S(1)}, u32[]{:S(2)}, u32[]{:S(2)}) %collective-permute-start.8) | collective-permute-done | bytes 524320 | tf_op jit(solution)/shard_map/ppermute | solution.py:41
  54.7 3.1 %collective-permute-done.6 = bf16[256,2048]{1,0:T(8,128)(2,1)S(1)} collective-permute-done((bf16[256,2048]{1,0:T(8,128)(2,1)S(1)}, bf16[256,2048]{1,0:T(8,128)(2,1)S(1)}, u32[]{:S(2)}, u32[]{:S(2)}) %collective-permute-start.6) | collective-permute-done | bytes 1048608 | tf_op jit(solution)/shard_map/ppermute | solution.py:41
  57.8 4.7 %convolution_convert_fusion.2 = bf16[512,2048]{1,0:T(8,128)(2,1)S(1)} fusion(bf16[2048,2048]{1,0:T(8,128)(2,1)S(1)} %bitcast.95, bf16[256,2048]{1,0:T(8,128)(2,1)S(1)} %collective-permute-done.6, bf16[256,2048]{1,0:T(8,128)(2,1)S(1)} %constant_dynamic-update-slice_fusion.13), kind=kOutput, calls=%fused_computation.3 | convolution fusion | flops 4300210176 | bytes 12582912 | tf_op jit(solution)/shard_map/dot_general | solution.py:98
  69.7 5.0 %collective-permute-done.9 = bf16[256,2048]{1,0:T(8,128)(2,1)S(1)} collective-permute-done((bf16[256,2048]{1,0:T(8,128)(2,1)S(1)}, bf16[256,2048]{1,0:T(8,128)(2,1)S(1)}, u32[]{:S(2)}, u32[]{:S(2)}) %collective-permute-start.9) | collective-permute-done | bytes 1048608 | tf_op jit(solution)/shard_map/ppermute | solution.py:41
  74.7 4.8 %convolution_convert_fusion.1 = bf16[512,2048]{1,0:T(8,128)(2,1)S(1)} fusion(bf16[2048,2048]{1,0:T(8,128)(2,1)S(1)} %bitcast.95, bf16[256,2048]{1,0:T(8,128)(2,1)S(1)} %collective-permute-done.9, bf16[256,2048]{1,0:T(8,128)(2,1)S(1)} %get-tuple-element.110), kind=kOutput, calls=%fused_computation.2 | convolution fusion | flops 4300210176 | bytes 12582912 | tf_op jit(solution)/shard_map/dot_general | solution.py:98
  85.9 4.7 %convolution_convert_fusion = bf16[512,2048]{1,0:T(8,128)(2,1)S(1)} fusion(bf16[2048,2048]{1,0:T(8,128)(2,1)S(1)} %bitcast.95, bf16[256,2048]{1,0:T(8,128)(2,1)S(1)} %collective-permute-done.16, bf16[128,2048]{1,0:T(8,128)(2,1)S(1)} %collective-permute-done.15, bf16[128,2048]{1,0:T(8,128)(2,1)S(1)} %get-tuple-element.46), kind=kOutput, calls=%fused_computation.1 | convolution fusion | flops 4302307328 | bytes 12582912 | tf_op jit(solution)/shard_map/dot_general | solution.py:98
  94.0 9.9 %collective-permute-done.14 = bf16[4,64,2048]{2,1,0:T(8,128)(2,1)S(1)} collective-permute-done((bf16[4,64,2048]{2,1,0:T(8,128)(2,1)S(1)}, bf16[4,64,2048]{2,1,0:T(8,128)(2,1)S(1)}, u32[]{:S(2)}, u32[]{:S(2)}) %collective-permute-start.14) | collective-permute-done | bytes 1048608 | tf_op jit(solution)/shard_map/ppermute | solution.py:44
  108.9 6.3 %collective-permute-done.13 = bf16[128,2048]{1,0:T(8,128)(2,1)S(1)} collective-permute-done((bf16[128,2048]{1,0:T(8,128)(2,1)S(1)}, bf16[128,2048]{1,0:T(8,128)(2,1)S(1)}, u32[]{:S(2)}, u32[]{:S(2)}) %collective-permute-start.13) | collective-permute-done | bytes 524320 | tf_op jit(solution)/shard_map/ppermute | solution.py:44
  124.8 5.1 %collective-permute-start.23 = (f32[64,1024]{1,0:T(8,128)S(1)}, f32[64,1024]{1,0:T(8,128)S(1)}, u32[]{:S(2)}, u32[]{:S(2)}) collective-permute-start(f32[64,1024]{1,0:T(8,128)S(1)} %slice.178), channel_id=1, source_target_pairs={{0,8},{8,0},{16,24},{24,16},{32,40},{40,32},{48,56},{56,48},{64,72... | collective-permute-start | bytes 786440 | tf_op jit(solution)/shard_map/ppermute | solution.py:41
  155.2 6.8 %collective-permute-done.30 = bf16[2,2,24,2048]{3,2,1,0:T(8,128)(2,1)S(1)} collective-permute-done((bf16[2,2,24,2048]{3,2,1,0:T(8,128)(2,1)S(1)}, bf16[2,2,24,2048]{3,2,1,0:T(8,128)(2,1)S(1)}, u32[]{:S(2)}, u32[]{:S(2)}) %collective-permute-start.30) | collective-permute-done | bytes 393248 | tf_op jit(solution)/shard_map/ppermute | solution.py:41
  168.1 3.1 %collective-permute-start.32 = (bf16[2,24,2048]{2,1,0:T(8,128)(2,1)S(1)}, bf16[2,24,2048]{2,1,0:T(8,128)(2,1)S(1)}, u32[]{:S(2)}, u32[]{:S(2)}) collective-permute-start(bf16[2,24,2048]{2,1,0:T(8,128)(2,1)S(1)} %rev.14), channel_id=1, source_target_pairs={{0,16},{8,24},{16,0},{24,8},{32,48},{40,56},{48,32},{56,40},{64,80... | collective-permute-start | bytes 589832 | tf_op jit(solution)/shard_map/ppermute | solution.py:41
  178.3 3.2 %collective-permute-done.36 = bf16[384,1024]{1,0:T(8,128)(2,1)S(1)} collective-permute-done((bf16[384,1024]{1,0:T(8,128)(2,1)S(1)}, bf16[384,1024]{1,0:T(8,128)(2,1)S(1)}, u32[]{:S(2)}, u32[]{:S(2)}) %collective-permute-start.36) | collective-permute-done | bytes 786464 | tf_op jit(solution)/shard_map/ppermute | solution.py:47
  181.5 3.9 %collective-permute-done.37 = bf16[384,1024]{1,0:T(8,128)(2,1)} collective-permute-done((bf16[384,1024]{1,0:T(8,128)(2,1)S(1)}, bf16[384,1024]{1,0:T(8,128)(2,1)}, u32[]{:S(2)}, u32[]{:S(2)}) %collective-permute-start.37) | collective-permute-done | bytes 786464 | tf_op jit(solution)/shard_map/ppermute | solution.py:47
  188.5 5.4 %collective-permute-done.38 = bf16[1,4,48,512]{3,2,0,1:T(8,128)(2,1)S(1)} collective-permute-done((bf16[1,4,48,512]{3,2,0,1:T(8,128)(2,1)S(1)}, bf16[1,4,48,512]{3,2,0,1:T(8,128)(2,1)S(1)}, u32[]{:S(2)}, u32[]{:S(2)}) %collective-permute-start.38) | collective-permute-done | bytes 196640 | tf_op jit(solution)/shard_map/ppermute | solution.py:41
  194.0 7.0 %collective-permute-done.39 = bf16[2,4,48,512]{3,2,0,1:T(8,128)(2,1)S(1)} collective-permute-done((bf16[2,4,48,512]{3,2,0,1:T(8,128)(2,1)S(1)}, bf16[2,4,48,512]{3,2,0,1:T(8,128)(2,1)S(1)}, u32[]{:S(2)}, u32[]{:S(2)}) %collective-permute-start.39) | collective-permute-done | bytes 393248 | tf_op jit(solution)/shard_map/ppermute | solution.py:41
  201.2 3.5 %collective-permute-start.41 = (bf16[4,4,48,512]{3,2,0,1:T(8,128)(2,1)S(1)}, bf16[4,4,48,512]{3,2,0,1:T(8,128)(2,1)S(1)}, u32[]{:S(2)}, u32[]{:S(2)}) collective-permute-start(bf16[4,4,48,512]{3,2,0,1:T(8,128)(2,1)S(1)} %get-tuple-element.81), channel_id=1, source_target_pairs={{0,8},{8,0},{16,24},{24,16},{32,40},{40,32},{48,56},{56,48},{64,72... | collective-permute-start | bytes 2359304 | tf_op jit(solution)/shard_map/ppermute | solution.py:41
  207.7 3.2 %fusion.14 = bf16[1024,256]{1,0:T(8,128)(2,1)} fusion(bf16[1536,512]{1,0:T(8,128)(2,1)S(1)} %bitcast.99, s32[]{:T(128)S(6)} %select_n.253, bf16[384,1024]{1,0:T(8,128)(2,1)} %collective-permute-done.40, bf16[384,1024]{1,0:T(8,128)(2,1)} %collective-permute-done.37, bf16[384,1024]{1,0:T(8,128)(2,1)S(1)} %copy-done.8, bf16[384,1024]{1,0:T(8,128)(2,1)S(1)} %copy-done.5), kind=kOutput, calls=%fused_computation.29 | convolution fusion | flops 818413568 | bytes 4456452 | tf_op jit(solution)/shard_map/dot_general | solution.py:217
  214.9 9.4 %collective-permute-done.42 = bf16[1024,256]{1,0:T(8,128)(2,1)S(1)} collective-permute-done((bf16[1024,256]{1,0:T(8,128)(2,1)}, bf16[1024,256]{1,0:T(8,128)(2,1)S(1)}, u32[]{:S(2)}, u32[]{:S(2)}) %collective-permute-start.42) | collective-permute-done | bytes 524320 | tf_op jit(solution)/shard_map/ppermute | solution.py:44
  (193 shorter events, 92.7 us)
Async XLA Ops:
  0.6 15.8 %collective-permute-start.2 = (bf16[2048,1024]{1,0:T(8,128)(2,1)}, bf16[2048,1024]{1,0:T(8,128)(2,1)}, u32[]{:S(2)}, u32[]{:S(2)}) collective-permute-start(bf16[2048,1024]{1,0:T(8,128)(2,1)} %param.8), channel_id=1, source_target_pairs={{0,8},{8,0},{16,24},{24,16},{32,40},{40,32},{48,56},{56,48},{64,72... | collective-permute-start | bytes 12582920 | tf_op jit(solution)/shard_map/ppermute | solution.py:41
  4.2 12.2 %collective-permute-start.1 = (bf16[128,2048]{1,0:T(8,128)(2,1)S(1)}, bf16[128,2048]{1,0:T(8,128)(2,1)}, u32[]{:S(2)}, u32[]{:S(2)}) collective-permute-start(bf16[128,2048]{1,0:T(8,128)(2,1)S(1)} %get-tuple-element.79), channel_id=1, source_target_pairs={{0,32},{8,104},{16,48},{24,120},{32,0},{40,72},{48,16},{56,88},{64... | collective-permute-start | bytes 1572872 | tf_op jit(solution)/shard_map/ppermute | solution.py:41
  6.8 16.0 %collective-permute-start = (bf16[128,2048]{1,0:T(8,128)(2,1)S(1)}, bf16[128,2048]{1,0:T(8,128)(2,1)S(1)}, u32[]{:S(2)}, u32[]{:S(2)}) collective-permute-start(bf16[128,2048]{1,0:T(8,128)(2,1)S(1)} %get-tuple-element.79), channel_id=1, source_target_pairs={{0,16},{8,24},{16,0},{24,8},{32,48},{40,56},{48,32},{56,40},{64,80... | collective-permute-start | bytes 1572872 | tf_op jit(solution)/shard_map/ppermute | solution.py:41
  10.4 27.9 %collective-permute-start.4 = (bf16[128,2048]{1,0:T(8,128)(2,1)}, bf16[128,2048]{1,0:T(8,128)(2,1)S(1)}, u32[]{:S(2)}, u32[]{:S(2)}) collective-permute-start(bf16[128,2048]{1,0:T(8,128)(2,1)} %get-tuple-element.78), channel_id=1, source_target_pairs={{0,16},{8,24},{16,0},{24,8},{32,48},{40,56},{48,32},{56,40},{64,80... | collective-permute-start | bytes 1572872 | tf_op jit(solution)/shard_map/ppermute | solution.py:41
  17.6 20.7 %collective-permute-start.3 = (bf16[256,2048]{1,0:T(8,128)(2,1)S(1)}, bf16[256,2048]{1,0:T(8,128)(2,1)}, u32[]{:S(2)}, u32[]{:S(2)}) collective-permute-start(bf16[256,2048]{1,0:T(8,128)(2,1)S(1)} %pad_maximum_fusion.2), channel_id=1, source_target_pairs={{0,96},{8,40},{16,112},{24,56},{32,64},{40,8},{48,80},{56,24},{64,... | collective-permute-start | bytes 3145736 | tf_op jit(solution)/shard_map/ppermute | solution.py:41
  22.8 15.3 %collective-permute-start.5 = (bf16[128,2048]{1,0:T(8,128)(2,1)S(1)}, bf16[128,2048]{1,0:T(8,128)(2,1)S(1)}, u32[]{:S(2)}, u32[]{:S(2)}) collective-permute-start(bf16[128,2048]{1,0:T(8,128)(2,1)S(1)} %collective-permute-done), channel_id=1, source_target_pairs={{0,32},{8,104},{16,48},{24,120},{32,0},{40,72},{48,16},{56,88},{64... | collective-permute-start | bytes 1572872 | tf_op jit(solution)/shard_map/ppermute | solution.py:41
  38.2 19.6 %collective-permute-start.6 = (bf16[256,2048]{1,0:T(8,128)(2,1)S(1)}, bf16[256,2048]{1,0:T(8,128)(2,1)S(1)}, u32[]{:S(2)}, u32[]{:S(2)}) collective-permute-start(bf16[256,2048]{1,0:T(8,128)(2,1)S(1)} %constant_dynamic-update-slice_fusion.13), channel_id=1, source_target_pairs={{0,96},{8,40},{16,112},{24,56},{32,64},{40,8},{48,80},{56,24},{64,... | collective-permute-start | bytes 3145736 | tf_op jit(solution)/shard_map/ppermute | solution.py:41
  38.4 15.3 %collective-permute-start.8 = (bf16[128,2048]{1,0:T(8,128)(2,1)S(1)}, bf16[128,2048]{1,0:T(8,128)(2,1)S(1)}, u32[]{:S(2)}, u32[]{:S(2)}) collective-permute-start(bf16[128,2048]{1,0:T(8,128)(2,1)S(1)} %pad_maximum_fusion.10), channel_id=1, source_target_pairs={{0,32},{8,104},{16,48},{24,120},{32,0},{40,72},{48,16},{56,88},{64... | collective-permute-start | bytes 1572872 | tf_op jit(solution)/shard_map/ppermute | solution.py:41
  47.1 15.5 %collective-permute-start.7 = (bf16[2,128,2048]{2,1,0:T(8,128)(2,1)S(1)}, bf16[2,128,2048]{2,1,0:T(8,128)(2,1)S(1)}, u32[]{:S(2)}, u32[]{:S(2)}) collective-permute-start(bf16[2,128,2048]{2,1,0:T(8,128)(2,1)S(1)} %pad_maximum_fusion.3), channel_id=1, source_target_pairs={{0,6},{1,7},{2,4},{3,5},{4,2},{5,3},{6,0},{7,1},{8,10},{9,11},{10,... | collective-permute-start | bytes 3145736 | tf_op jit(solution)/shard_map/ppermute | solution.py:47
  53.8 20.9 %collective-permute-start.9 = (bf16[256,2048]{1,0:T(8,128)(2,1)S(1)}, bf16[256,2048]{1,0:T(8,128)(2,1)S(1)}, u32[]{:S(2)}, u32[]{:S(2)}) collective-permute-start(bf16[256,2048]{1,0:T(8,128)(2,1)S(1)} %get-tuple-element.110), channel_id=1, source_target_pairs={{0,96},{8,40},{16,112},{24,56},{32,64},{40,8},{48,80},{56,24},{64,... | collective-permute-start | bytes 3145736 | tf_op jit(solution)/shard_map/ppermute | solution.py:41
  54.1 14.9 %collective-permute-start.15 = (bf16[128,2048]{1,0:T(8,128)(2,1)S(1)}, bf16[128,2048]{1,0:T(8,128)(2,1)S(1)}, u32[]{:S(2)}, u32[]{:S(2)}) collective-permute-start(bf16[128,2048]{1,0:T(8,128)(2,1)S(1)} %get-tuple-element.46), channel_id=1, source_target_pairs={{0,32},{8,104},{16,48},{24,120},{32,0},{40,72},{48,16},{56,88},{64... | collective-permute-start | bytes 1572872 | tf_op jit(solution)/shard_map/ppermute | solution.py:41
  62.8 19.6 %collective-permute-start.10 = (bf16[2,128,2048]{2,1,0:T(8,128)(2,1)S(1)}, bf16[2,128,2048]{2,1,0:T(8,128)(2,1)S(1)}, u32[]{:S(2)}, u32[]{:S(2)}) collective-permute-start(bf16[2,128,2048]{2,1,0:T(8,128)(2,1)S(1)} %pad_maximum_fusion.4), channel_id=1, source_target_pairs={{0,6},{1,7},{2,4},{3,5},{4,2},{5,3},{6,0},{7,1},{8,10},{9,11},{10,... | collective-permute-start | bytes 3145736 | tf_op jit(solution)/shard_map/ppermute | solution.py:47
  64.3 16.6 %collective-permute-start.11 = (bf16[128,2048]{1,0:T(8,128)(2,1)S(1)}, bf16[128,2048]{1,0:T(8,128)(2,1)S(1)}, u32[]{:S(2)}, u32[]{:S(2)}) collective-permute-start(bf16[128,2048]{1,0:T(8,128)(2,1)S(1)} %fusion.21), channel_id=1, source_target_pairs={{0,2},{1,3},{2,0},{3,1},{4,6},{5,7},{6,4},{7,5},{8,14},{9,15},{10,... | collective-permute-start | bytes 1572872 | tf_op jit(solution)/shard_map/ppermute | solution.py:47
  69.1 16.8 %collective-permute-start.16 = (bf16[256,2048]{1,0:T(8,128)(2,1)S(1)}, bf16[256,2048]{1,0:T(8,128)(2,1)S(1)}, u32[]{:S(2)}, u32[]{:S(2)}) collective-permute-start(bf16[256,2048]{1,0:T(8,128)(2,1)S(1)} %pad_maximum_fusion.5), channel_id=1, source_target_pairs={{0,96},{8,40},{16,112},{24,56},{32,64},{40,8},{48,80},{56,24},{64,... | collective-permute-start | bytes 3145736 | tf_op jit(solution)/shard_map/ppermute | solution.py:41
  79.7 24.2 %collective-permute-start.14 = (bf16[4,64,2048]{2,1,0:T(8,128)(2,1)S(1)}, bf16[4,64,2048]{2,1,0:T(8,128)(2,1)S(1)}, u32[]{:S(2)}, u32[]{:S(2)}) collective-permute-start(bf16[4,64,2048]{2,1,0:T(8,128)(2,1)S(1)} %get-tuple-element.64), channel_id=1, source_target_pairs={{0,1},{1,0},{2,3},{3,2},{4,5},{5,4},{6,7},{7,6},{8,9},{9,8},{10,11... | collective-permute-start | bytes 3145736 | tf_op jit(solution)/shard_map/ppermute | solution.py:44
  90.8 14.9 %collective-permute-start.17 = (bf16[2,128,2048]{2,1,0:T(8,128)(2,1)S(1)}, bf16[2,128,2048]{2,1,0:T(8,128)(2,1)S(1)}, u32[]{:S(2)}, u32[]{:S(2)}) collective-permute-start(bf16[2,128,2048]{2,1,0:T(8,128)(2,1)S(1)} %pad_maximum_fusion.6), channel_id=1, source_target_pairs={{0,6},{1,7},{2,4},{3,5},{4,2},{5,3},{6,0},{7,1},{8,10},{9,11},{10,... | collective-permute-start | bytes 3145736 | tf_op jit(solution)/shard_map/ppermute | solution.py:47
  92.8 22.3 %collective-permute-start.13 = (bf16[128,2048]{1,0:T(8,128)(2,1)S(1)}, bf16[128,2048]{1,0:T(8,128)(2,1)S(1)}, u32[]{:S(2)}, u32[]{:S(2)}) collective-permute-start(bf16[128,2048]{1,0:T(8,128)(2,1)S(1)} %select_convert_fusion), channel_id=1, source_target_pairs={{0,1},{1,0},{2,3},{3,2},{4,5},{5,4},{6,7},{7,6},{8,9},{9,8},{10,11... | collective-permute-start | bytes 1572872 | tf_op jit(solution)/shard_map/ppermute | solution.py:44
  106.9 13.3 %collective-permute-start.20 = (bf16[128,2048]{1,0:T(8,128)(2,1)S(1)}, bf16[128,2048]{1,0:T(8,128)(2,1)S(1)}, u32[]{:S(2)}, u32[]{:S(2)}) collective-permute-start(bf16[128,2048]{1,0:T(8,128)(2,1)S(1)} %fusion.23), channel_id=1, source_target_pairs={{0,2},{1,3},{2,0},{3,1},{4,6},{5,7},{6,4},{7,5},{8,14},{9,15},{10,... | collective-permute-start | bytes 1572872 | tf_op jit(solution)/shard_map/ppermute | solution.py:47
  115.8 14.5 %collective-permute-start.22 = (f32[128,1024]{1,0:T(8,128)S(1)}, f32[128,1024]{1,0:T(8,128)S(1)}, u32[]{:S(2)}, u32[]{:S(2)}) collective-permute-start(f32[128,1024]{1,0:T(8,128)S(1)} %slice.177), channel_id=1, source_target_pairs={{0,8},{8,0},{16,24},{24,16},{32,40},{40,32},{48,56},{56,48},{64,72... | collective-permute-start | bytes 1572872 | tf_op jit(solution)/shard_map/ppermute | solution.py:41
  164.0 17.5 %collective-permute-start.36 = (bf16[384,1024]{1,0:T(8,128)(2,1)S(1)}, bf16[384,1024]{1,0:T(8,128)(2,1)S(1)}, u32[]{:S(2)}, u32[]{:S(2)}) collective-permute-start(bf16[384,1024]{1,0:T(8,128)(2,1)S(1)} %copy-done.5), channel_id=1, source_target_pairs={{0,2},{1,3},{2,0},{3,1},{4,6},{5,7},{6,4},{7,5},{8,14},{9,15},{10,... | collective-permute-start | bytes 2359304 | tf_op jit(solution)/shard_map/ppermute | solution.py:47
  165.9 19.5 %collective-permute-start.37 = (bf16[384,1024]{1,0:T(8,128)(2,1)S(1)}, bf16[384,1024]{1,0:T(8,128)(2,1)}, u32[]{:S(2)}, u32[]{:S(2)}) collective-permute-start(bf16[384,1024]{1,0:T(8,128)(2,1)S(1)} %copy-done.5), channel_id=1, source_target_pairs={{0,6},{1,7},{2,4},{3,5},{4,2},{5,3},{6,0},{7,1},{8,10},{9,11},{10,... | collective-permute-start | bytes 2359304 | tf_op jit(solution)/shard_map/ppermute | solution.py:47
  174.4 11.1 %collective-permute-start.33 = (bf16[48,512]{1,0:T(8,128)(2,1)S(1)}, bf16[48,512]{1,0:T(8,128)(2,1)S(1)}, u32[]{:S(2)}, u32[]{:S(2)}) collective-permute-start(bf16[48,512]{1,0:T(8,128)(2,1)S(1)} %get-tuple-element.94), channel_id=1, source_target_pairs={{0,2},{1,3},{2,0},{3,1},{4,6},{5,7},{6,4},{7,5},{8,14},{9,15},{10,... | collective-permute-start | bytes 147464 | tf_op jit(solution)/shard_map/ppermute | solution.py:47
  187.7 13.4 %collective-permute-start.40 = (bf16[384,1024]{1,0:T(8,128)(2,1)S(1)}, bf16[384,1024]{1,0:T(8,128)(2,1)}, u32[]{:S(2)}, u32[]{:S(2)}) collective-permute-start(bf16[384,1024]{1,0:T(8,128)(2,1)S(1)} %collective-permute-done.36), channel_id=1, source_target_pairs={{0,6},{1,7},{2,4},{3,5},{4,2},{5,3},{6,0},{7,1},{8,10},{9,11},{10,... | collective-permute-start | bytes 2359304 | tf_op jit(solution)/shard_map/ppermute | solution.py:47
  211.0 13.3 %collective-permute-start.42 = (bf16[1024,256]{1,0:T(8,128)(2,1)}, bf16[1024,256]{1,0:T(8,128)(2,1)S(1)}, u32[]{:S(2)}, u32[]{:S(2)}) collective-permute-start(bf16[1024,256]{1,0:T(8,128)(2,1)} %fusion.14), channel_id=1, source_target_pairs={{0,1},{1,0},{2,3},{3,2},{4,5},{5,4},{6,7},{7,6},{8,9},{9,8},{10,11... | collective-permute-start | bytes 1572872 | tf_op jit(solution)/shard_map/ppermute | solution.py:44
  (31 other events, 227.5 us)

commit v5 on v4

--- a/solution.py
+++ b/solution.py
@@ -85,7 +85,7 @@
     units, unit, coming = 2 + len(RUNS), first, first_far
     halves, firsts, seconds, all_terms = ([None] * units for _ in range(4))
     for j in range(units):
-        if j >= 2 and j - 2 != units - 2:
+        if j >= 3 and j - 2 != units - 2:
             paired, all_terms[j - 2] = tie(paired, all_terms[j - 2])
         lane = jnp.concatenate([unit, paired])
         others = over_row(lane, x_next)
@@ -208,8 +208,7 @@
     others, pooled_rest = tie(others, pooled_rest)
     part = jnp.concatenate([part, others])
     twin_part = middle_exchanged(over_row(part, twin), 1)
-    part = jnp.stack([part, twin_part]).transpose(2, 0, 1, 3, 4)
-    part = part.reshape(ys * count, features // ys)
+    part = jnp.stack([part, twin_part])
     all_pooled = jnp.concatenate([pooled_lane, pooled_rest])
     loss_factor = 1.0 / math.sqrt(cols * count)
 
@@ -220,8 +219,14 @@
         return product * loss_factor
 
     own = features // cols
-    theirs = over_col(outer(lax.dynamic_slice_in_dim(part, (1 - zl) * own, own, 1)).astype(BF16), z_near)
-    ours, theirs = tie(outer(lax.dynamic_slice_in_dim(part, zl * own, own, 1)), theirs)
+    def columns_of(place):
+        columns = lax.dynamic_slice_in_dim(part, place * own, own, part.ndim - 1)
+        return columns.transpose(2, 0, 1, 3, 4).reshape(ys * count, own)
+
+    theirs, ours = columns_of(1 - zl), columns_of(zl)
+    (theirs,) = tie(theirs)
+    theirs = over_col(outer(theirs).astype(BF16), z_near)
+    ours, theirs = tie(outer(ours), theirs)
     gradient = ours + theirs.astype(F32)
     return (full_proj[0].astype(BF16)[None], gradient)
 

time: 226 us -> 225 us (level)
  no operation moved by 1% of the time
where the time goes in v5:
time: 225 us
  waiting for transfers between devices  108 us (48%)
  starting transfers between devices  58.2 us (26%)
  matrix products  32 us (14%)
  local copies, waits for them, and re-layouts  18.1 us (8%)
  other arithmetic  6.68 us (3%)
    ppermute x25, waiting for transfers between devices, over_row(): return lax.ppermute(value, 'row', pairs)  66.1 us
    ppermute x25, starting transfers between devices, over_row(): return lax.ppermute(value, 'row', pairs)  33.7 us
    ppermute x5, waiting for transfers between devices, over_col(): return lax.ppermute(value, 'col', pairs)  27.7 us
    dot_general x4, matrix products, body(): terms = jnp.dot(tokens, weight, preferred_element_type=F32).astype(BF16)  22.5 us
    ppermute x13, starting transfers between devices, over_both(): return lax.ppermute(value, ('row', 'col'), pairs)  18.6 us
    ppermute x13, waiting for transfers between devices, over_both(): return lax.ppermute(value, ('row', 'col'), pairs)  14.1 us
    unnamed x43, local copies, waits for them, and re-layouts  7.7 us
    ppermute x5, starting transfers between devices, over_col(): return lax.ppermute(value, 'col', pairs)  5.81 us
  transfers between devices with their start and end apart: 43, of which 30 were waited for; matrix products, arithmetic and copies ran while one was open for 20% of the time, Pallas kernels for 0%

profile of v5, /device:TPU:1, one launch (start us, length us, event | category | flops | bytes accessed | tf_op | source)
XLA Modules:
  0.0 224.5 jit_solution(10708431069879318747)
XLA Ops:
  6.8 3.6 %collective-permute-start = (bf16[128,2048]{1,0:T(8,128)(2,1)S(1)}, bf16[128,2048]{1,0:T(8,128)(2,1)S(1)}, u32[]{:S(2)}, u32[]{:S(2)}) collective-permute-start(bf16[128,2048]{1,0:T(8,128)(2,1)S(1)} %get-tuple-element.79), channel_id=1, source_target_pairs={{0,16},{8,24},{16,0},{24,8},{32,48},{40,56},{48,32},{56,40},{64,80... | collective-permute-start | bytes 1572872 | tf_op jit(solution)/shard_map/ppermute | solution.py:41
  11.6 4.8 %constant_dynamic-update-slice_fusion.12 = bf16[2048,2048]{1,0:T(8,128)(2,1)} fusion(bf16[2048,1024]{1,0:T(8,128)(2,1)} %param.8), kind=kLoop, calls=%fused_computation.104 | loop fusion | bytes 8388608
  17.9 4.9 %collective-permute-done = bf16[128,2048]{1,0:T(8,128)(2,1)S(1)} collective-permute-done((bf16[128,2048]{1,0:T(8,128)(2,1)S(1)}, bf16[128,2048]{1,0:T(8,128)(2,1)S(1)}, u32[]{:S(2)}, u32[]{:S(2)}) %collective-permute-start) | collective-permute-done | bytes 524320 | tf_op jit(solution)/shard_map/ppermute | solution.py:41
  22.9 4.8 %constant_dynamic-update-slice_fusion.11 = bf16[2048,2048]{1,0:T(8,128)(2,1)} fusion(bf16[2048,2048]{1,0:T(8,128)(2,1)} %constant_dynamic-update-slice_fusion.12, bf16[2048,1024]{1,0:T(8,128)(2,1)} %collective-permute-done.2), kind=kLoop, calls=%fused_computation.103 | loop fusion | bytes 8388608 | tf_op jit(solution)/shard_map/concatenate | solution.py:68
  27.6 10.5 %collective-permute-done.5 = bf16[128,2048]{1,0:T(8,128)(2,1)S(1)} collective-permute-done((bf16[128,2048]{1,0:T(8,128)(2,1)S(1)}, bf16[128,2048]{1,0:T(8,128)(2,1)S(1)}, u32[]{:S(2)}, u32[]{:S(2)}) %collective-permute-start.5) | collective-permute-done | bytes 524320 | tf_op jit(solution)/shard_map/ppermute | solution.py:41
  38.5 8.3 %convolution_convert_fusion.3 = bf16[512,2048]{1,0:T(8,128)(2,1)S(1)} fusion(bf16[2048,2048]{1,0:T(8,128)(2,1)} %constant_dynamic-update-slice_fusion.11, bf16[256,2048]{1,0:T(8,128)(2,1)} %collective-permute-done.3, bf16[256,2048]{1,0:T(8,128)(2,1)S(1)} %pad_maximum_fusion.1), kind=kOutput, calls=%fused_computation.4 | convolution fusion | flops 4300210176 | bytes 12582912 | tf_op jit(solution)/shard_map/dot_general | solution.py:98
  48.6 5.1 %collective-permute-done.8 = bf16[128,2048]{1,0:T(8,128)(2,1)S(1)} collective-permute-done((bf16[128,2048]{1,0:T(8,128)(2,1)S(1)}, bf16[128,2048]{1,0:T(8,128)(2,1)S(1)}, u32[]{:S(2)}, u32[]{:S(2)}) %collective-permute-start.8) | collective-permute-done | bytes 524320 | tf_op jit(solution)/shard_map/ppermute | solution.py:41
  54.7 3.2 %collective-permute-done.6 = bf16[256,2048]{1,0:T(8,128)(2,1)S(1)} collective-permute-done((bf16[256,2048]{1,0:T(8,128)(2,1)S(1)}, bf16[256,2048]{1,0:T(8,128)(2,1)S(1)}, u32[]{:S(2)}, u32[]{:S(2)}) %collective-permute-start.6) | collective-permute-done | bytes 1048608 | tf_op jit(solution)/shard_map/ppermute | solution.py:41
  57.8 4.7 %convolution_convert_fusion.2 = bf16[512,2048]{1,0:T(8,128)(2,1)S(1)} fusion(bf16[2048,2048]{1,0:T(8,128)(2,1)S(1)} %bitcast.100, bf16[256,2048]{1,0:T(8,128)(2,1)S(1)} %collective-permute-done.6, bf16[256,2048]{1,0:T(8,128)(2,1)S(1)} %constant_dynamic-update-slice_fusion.13), kind=kOutput, calls=%fused_computation.3 | convolution fusion | flops 4300210176 | bytes 12582912 | tf_op jit(solution)/shard_map/dot_general | solution.py:98
  69.7 5.0 %collective-permute-done.9 = bf16[256,2048]{1,0:T(8,128)(2,1)S(1)} collective-permute-done((bf16[256,2048]{1,0:T(8,128)(2,1)S(1)}, bf16[256,2048]{1,0:T(8,128)(2,1)S(1)}, u32[]{:S(2)}, u32[]{:S(2)}) %collective-permute-start.9) | collective-permute-done | bytes 1048608 | tf_op jit(solution)/shard_map/ppermute | solution.py:41
  74.7 4.8 %convolution_convert_fusion.1 = bf16[512,2048]{1,0:T(8,128)(2,1)S(1)} fusion(bf16[2048,2048]{1,0:T(8,128)(2,1)S(1)} %bitcast.100, bf16[256,2048]{1,0:T(8,128)(2,1)S(1)} %collective-permute-done.9, bf16[256,2048]{1,0:T(8,128)(2,1)S(1)} %constant_dynamic-update-slice_fusion.15), kind=kOutput, calls=%fused_computation.2 | convolution fusion | flops 4300210176 | bytes 12582912 | tf_op jit(solution)/shard_map/dot_general | solution.py:98
  85.9 4.7 %convolution_convert_fusion = bf16[512,2048]{1,0:T(8,128)(2,1)S(1)} fusion(bf16[2048,2048]{1,0:T(8,128)(2,1)S(1)} %bitcast.100, bf16[256,2048]{1,0:T(8,128)(2,1)S(1)} %collective-permute-done.16, bf16[128,2048]{1,0:T(8,128)(2,1)S(1)} %collective-permute-done.15, bf16[128,2048]{1,0:T(8,128)(2,1)S(1)} %pad_maximum_fusion.10), kind=kOutput, calls=%fused_computation.1 | convolution fusion | flops 4302307328 | bytes 12582912 | tf_op jit(solution)/shard_map/dot_general | solution.py:98
  94.0 10.0 %collective-permute-done.14 = bf16[4,64,2048]{2,1,0:T(8,128)(2,1)S(1)} collective-permute-done((bf16[4,64,2048]{2,1,0:T(8,128)(2,1)S(1)}, bf16[4,64,2048]{2,1,0:T(8,128)(2,1)S(1)}, u32[]{:S(2)}, u32[]{:S(2)}) %collective-permute-start.14) | collective-permute-done | bytes 1048608 | tf_op jit(solution)/shard_map/ppermute | solution.py:44
  108.9 6.3 %collective-permute-done.13 = bf16[128,2048]{1,0:T(8,128)(2,1)S(1)} collective-permute-done((bf16[128,2048]{1,0:T(8,128)(2,1)S(1)}, bf16[128,2048]{1,0:T(8,128)(2,1)S(1)}, u32[]{:S(2)}, u32[]{:S(2)}) %collective-permute-start.13) | collective-permute-done | bytes 524320 | tf_op jit(solution)/shard_map/ppermute | solution.py:44
  124.8 5.1 %collective-permute-start.23 = (f32[64,1024]{1,0:T(8,128)S(1)}, f32[64,1024]{1,0:T(8,128)S(1)}, u32[]{:S(2)}, u32[]{:S(2)}) collective-permute-start(f32[64,1024]{1,0:T(8,128)S(1)} %slice.178), channel_id=1, source_target_pairs={{0,8},{8,0},{16,24},{24,16},{32,40},{40,32},{48,56},{56,48},{64,72... | collective-permute-start | bytes 786440 | tf_op jit(solution)/shard_map/ppermute | solution.py:41
  141.2 3.0 %collective-permute-start.28 = (f32[512]{0:T(512)S(1)}, f32[512]{0:T(512)S(1)}, u32[]{:S(2)}, u32[]{:S(2)}) collective-permute-start(f32[512]{0:T(512)S(1)} %add.223), channel_id=1, source_target_pairs={{0,16},{8,24},{16,0},{24,8},{32,48},{40,56},{48,32},{56,40},{64,80... | collective-permute-start | bytes 6152 | tf_op jit(solution)/shard_map/ppermute | solution.py:41
  155.2 6.8 %collective-permute-done.30 = bf16[2,2,24,2048]{3,2,1,0:T(8,128)(2,1)S(1)} collective-permute-done((bf16[2,2,24,2048]{3,2,1,0:T(8,128)(2,1)S(1)}, bf16[2,2,24,2048]{3,2,1,0:T(8,128)(2,1)S(1)}, u32[]{:S(2)}, u32[]{:S(2)}) %collective-permute-start.30) | collective-permute-done | bytes 393248 | tf_op jit(solution)/shard_map/ppermute | solution.py:41
  168.1 3.1 %collective-permute-start.32 = (bf16[2,24,2048]{2,1,0:T(8,128)(2,1)S(1)}, bf16[2,24,2048]{2,1,0:T(8,128)(2,1)S(1)}, u32[]{:S(2)}, u32[]{:S(2)}) collective-permute-start(bf16[2,24,2048]{2,1,0:T(8,128)(2,1)S(1)} %rev.14), channel_id=1, source_target_pairs={{0,16},{8,24},{16,0},{24,8},{32,48},{40,56},{48,32},{56,40},{64,80... | collective-permute-start | bytes 589832 | tf_op jit(solution)/shard_map/ppermute | solution.py:41
  178.3 3.1 %collective-permute-done.36 = bf16[384,1024]{1,0:T(8,128)(2,1)S(1)} collective-permute-done((bf16[384,1024]{1,0:T(8,128)(2,1)S(1)}, bf16[384,1024]{1,0:T(8,128)(2,1)S(1)}, u32[]{:S(2)}, u32[]{:S(2)}) %collective-permute-start.36) | collective-permute-done | bytes 786464 | tf_op jit(solution)/shard_map/ppermute | solution.py:47
  181.4 4.0 %collective-permute-done.37 = bf16[384,1024]{1,0:T(8,128)(2,1)} collective-permute-done((bf16[384,1024]{1,0:T(8,128)(2,1)S(1)}, bf16[384,1024]{1,0:T(8,128)(2,1)}, u32[]{:S(2)}, u32[]{:S(2)}) %collective-permute-start.37) | collective-permute-done | bytes 786464 | tf_op jit(solution)/shard_map/ppermute | solution.py:47
  188.5 5.3 %collective-permute-done.38 = bf16[1,4,48,512]{3,2,0,1:T(8,128)(2,1)S(1)} collective-permute-done((bf16[1,4,48,512]{3,2,0,1:T(8,128)(2,1)S(1)}, bf16[1,4,48,512]{3,2,0,1:T(8,128)(2,1)S(1)}, u32[]{:S(2)}, u32[]{:S(2)}) %collective-permute-start.38) | collective-permute-done | bytes 196640 | tf_op jit(solution)/shard_map/ppermute | solution.py:41
  193.9 7.0 %collective-permute-done.39 = bf16[2,4,48,512]{3,2,0,1:T(8,128)(2,1)S(1)} collective-permute-done((bf16[2,4,48,512]{3,2,0,1:T(8,128)(2,1)S(1)}, bf16[2,4,48,512]{3,2,0,1:T(8,128)(2,1)S(1)}, u32[]{:S(2)}, u32[]{:S(2)}) %collective-permute-start.39) | collective-permute-done | bytes 393248 | tf_op jit(solution)/shard_map/ppermute | solution.py:41
  201.1 3.6 %collective-permute-start.41 = (bf16[4,4,48,512]{3,2,0,1:T(8,128)(2,1)S(1)}, bf16[4,4,48,512]{3,2,0,1:T(8,128)(2,1)S(1)}, u32[]{:S(2)}, u32[]{:S(2)}) collective-permute-start(bf16[4,4,48,512]{3,2,0,1:T(8,128)(2,1)S(1)} %get-tuple-element.84), channel_id=1, source_target_pairs={{0,8},{8,0},{16,24},{24,16},{32,40},{40,32},{48,56},{56,48},{64,72... | collective-permute-start | bytes 2359304 | tf_op jit(solution)/shard_map/ppermute | solution.py:41
  213.5 9.9 %collective-permute-done.42 = bf16[1024,256]{1,0:T(8,128)(2,1)S(1)} collective-permute-done((bf16[1024,256]{1,0:T(8,128)(2,1)S(1)}, bf16[1024,256]{1,0:T(8,128)(2,1)S(1)}, u32[]{:S(2)}, u32[]{:S(2)}) %collective-permute-start.42) | collective-permute-done | bytes 524320 | tf_op jit(solution)/shard_map/ppermute | solution.py:44
  (194 shorter events, 91.2 us)
Async XLA Ops:
  0.6 15.8 %collective-permute-start.2 = (bf16[2048,1024]{1,0:T(8,128)(2,1)}, bf16[2048,1024]{1,0:T(8,128)(2,1)}, u32[]{:S(2)}, u32[]{:S(2)}) collective-permute-start(bf16[2048,1024]{1,0:T(8,128)(2,1)} %param.8), channel_id=1, source_target_pairs={{0,8},{8,0},{16,24},{24,16},{32,40},{40,32},{48,56},{56,48},{64,72... | collective-permute-start | bytes 12582920 | tf_op jit(solution)/shard_map/ppermute | solution.py:41
  4.2 12.2 %collective-permute-start.1 = (bf16[128,2048]{1,0:T(8,128)(2,1)S(1)}, bf16[128,2048]{1,0:T(8,128)(2,1)}, u32[]{:S(2)}, u32[]{:S(2)}) collective-permute-start(bf16[128,2048]{1,0:T(8,128)(2,1)S(1)} %get-tuple-element.79), channel_id=1, source_target_pairs={{0,32},{8,104},{16,48},{24,120},{32,0},{40,72},{48,16},{56,88},{64... | collective-permute-start | bytes 1572872 | tf_op jit(solution)/shard_map/ppermute | solution.py:41
  6.8 16.0 %collective-permute-start = (bf16[128,2048]{1,0:T(8,128)(2,1)S(1)}, bf16[128,2048]{1,0:T(8,128)(2,1)S(1)}, u32[]{:S(2)}, u32[]{:S(2)}) collective-permute-start(bf16[128,2048]{1,0:T(8,128)(2,1)S(1)} %get-tuple-element.79), channel_id=1, source_target_pairs={{0,16},{8,24},{16,0},{24,8},{32,48},{40,56},{48,32},{56,40},{64,80... | collective-permute-start | bytes 1572872 | tf_op jit(solution)/shard_map/ppermute | solution.py:41
  10.4 27.9 %collective-permute-start.4 = (bf16[128,2048]{1,0:T(8,128)(2,1)}, bf16[128,2048]{1,0:T(8,128)(2,1)S(1)}, u32[]{:S(2)}, u32[]{:S(2)}) collective-permute-start(bf16[128,2048]{1,0:T(8,128)(2,1)} %get-tuple-element.78), channel_id=1, source_target_pairs={{0,16},{8,24},{16,0},{24,8},{32,48},{40,56},{48,32},{56,40},{64,80... | collective-permute-start | bytes 1572872 | tf_op jit(solution)/shard_map/ppermute | solution.py:41
  17.6 20.7 %collective-permute-start.3 = (bf16[256,2048]{1,0:T(8,128)(2,1)S(1)}, bf16[256,2048]{1,0:T(8,128)(2,1)}, u32[]{:S(2)}, u32[]{:S(2)}) collective-permute-start(bf16[256,2048]{1,0:T(8,128)(2,1)S(1)} %pad_maximum_fusion.1), channel_id=1, source_target_pairs={{0,96},{8,40},{16,112},{24,56},{32,64},{40,8},{48,80},{56,24},{64,... | collective-permute-start | bytes 3145736 | tf_op jit(solution)/shard_map/ppermute | solution.py:41
  22.8 15.3 %collective-permute-start.5 = (bf16[128,2048]{1,0:T(8,128)(2,1)S(1)}, bf16[128,2048]{1,0:T(8,128)(2,1)S(1)}, u32[]{:S(2)}, u32[]{:S(2)}) collective-permute-start(bf16[128,2048]{1,0:T(8,128)(2,1)S(1)} %collective-permute-done), channel_id=1, source_target_pairs={{0,32},{8,104},{16,48},{24,120},{32,0},{40,72},{48,16},{56,88},{64... | collective-permute-start | bytes 1572872 | tf_op jit(solution)/shard_map/ppermute | solution.py:41
  38.2 19.6 %collective-permute-start.6 = (bf16[256,2048]{1,0:T(8,128)(2,1)S(1)}, bf16[256,2048]{1,0:T(8,128)(2,1)S(1)}, u32[]{:S(2)}, u32[]{:S(2)}) collective-permute-start(bf16[256,2048]{1,0:T(8,128)(2,1)S(1)} %constant_dynamic-update-slice_fusion.13), channel_id=1, source_target_pairs={{0,96},{8,40},{16,112},{24,56},{32,64},{40,8},{48,80},{56,24},{64,... | collective-permute-start | bytes 3145736 | tf_op jit(solution)/shard_map/ppermute | solution.py:41
  38.4 15.3 %collective-permute-start.8 = (bf16[128,2048]{1,0:T(8,128)(2,1)S(1)}, bf16[128,2048]{1,0:T(8,128)(2,1)S(1)}, u32[]{:S(2)}, u32[]{:S(2)}) collective-permute-start(bf16[128,2048]{1,0:T(8,128)(2,1)S(1)} %pad_maximum_fusion.9), channel_id=1, source_target_pairs={{0,32},{8,104},{16,48},{24,120},{32,0},{40,72},{48,16},{56,88},{64... | collective-permute-start | bytes 1572872 | tf_op jit(solution)/shard_map/ppermute | solution.py:41
  47.1 15.5 %collective-permute-start.7 = (bf16[2,128,2048]{2,1,0:T(8,128)(2,1)S(1)}, bf16[2,128,2048]{2,1,0:T(8,128)(2,1)S(1)}, u32[]{:S(2)}, u32[]{:S(2)}) collective-permute-start(bf16[2,128,2048]{2,1,0:T(8,128)(2,1)S(1)} %pad_maximum_fusion.2), channel_id=1, source_target_pairs={{0,6},{1,7},{2,4},{3,5},{4,2},{5,3},{6,0},{7,1},{8,10},{9,11},{10,... | collective-permute-start | bytes 3145736 | tf_op jit(solution)/shard_map/ppermute | solution.py:47
  53.7 20.9 %collective-permute-start.9 = (bf16[256,2048]{1,0:T(8,128)(2,1)S(1)}, bf16[256,2048]{1,0:T(8,128)(2,1)S(1)}, u32[]{:S(2)}, u32[]{:S(2)}) collective-permute-start(bf16[256,2048]{1,0:T(8,128)(2,1)S(1)} %constant_dynamic-update-slice_fusion.15), channel_id=1, source_target_pairs={{0,96},{8,40},{16,112},{24,56},{32,64},{40,8},{48,80},{56,24},{64,... | collective-permute-start | bytes 3145736 | tf_op jit(solution)/shard_map/ppermute | solution.py:41
  54.1 14.9 %collective-permute-start.15 = (bf16[128,2048]{1,0:T(8,128)(2,1)S(1)}, bf16[128,2048]{1,0:T(8,128)(2,1)S(1)}, u32[]{:S(2)}, u32[]{:S(2)}) collective-permute-start(bf16[128,2048]{1,0:T(8,128)(2,1)S(1)} %pad_maximum_fusion.10), channel_id=1, source_target_pairs={{0,32},{8,104},{16,48},{24,120},{32,0},{40,72},{48,16},{56,88},{64... | collective-permute-start | bytes 1572872 | tf_op jit(solution)/shard_map/ppermute | solution.py:41
  62.8 19.6 %collective-permute-start.10 = (bf16[2,128,2048]{2,1,0:T(8,128)(2,1)S(1)}, bf16[2,128,2048]{2,1,0:T(8,128)(2,1)S(1)}, u32[]{:S(2)}, u32[]{:S(2)}) collective-permute-start(bf16[2,128,2048]{2,1,0:T(8,128)(2,1)S(1)} %pad_maximum_fusion.3), channel_id=1, source_target_pairs={{0,6},{1,7},{2,4},{3,5},{4,2},{5,3},{6,0},{7,1},{8,10},{9,11},{10,... | collective-permute-start | bytes 3145736 | tf_op jit(solution)/shard_map/ppermute | solution.py:47
  64.3 16.6 %collective-permute-start.11 = (bf16[128,2048]{1,0:T(8,128)(2,1)S(1)}, bf16[128,2048]{1,0:T(8,128)(2,1)S(1)}, u32[]{:S(2)}, u32[]{:S(2)}) collective-permute-start(bf16[128,2048]{1,0:T(8,128)(2,1)S(1)} %fusion.21), channel_id=1, source_target_pairs={{0,2},{1,3},{2,0},{3,1},{4,6},{5,7},{6,4},{7,5},{8,14},{9,15},{10,... | collective-permute-start | bytes 1572872 | tf_op jit(solution)/shard_map/ppermute | solution.py:47
  69.1 16.9 %collective-permute-start.16 = (bf16[256,2048]{1,0:T(8,128)(2,1)S(1)}, bf16[256,2048]{1,0:T(8,128)(2,1)S(1)}, u32[]{:S(2)}, u32[]{:S(2)}) collective-permute-start(bf16[256,2048]{1,0:T(8,128)(2,1)S(1)} %pad_maximum_fusion.4), channel_id=1, source_target_pairs={{0,96},{8,40},{16,112},{24,56},{32,64},{40,8},{48,80},{56,24},{64,... | collective-permute-start | bytes 3145736 | tf_op jit(solution)/shard_map/ppermute | solution.py:41
  79.7 24.3 %collective-permute-start.14 = (bf16[4,64,2048]{2,1,0:T(8,128)(2,1)S(1)}, bf16[4,64,2048]{2,1,0:T(8,128)(2,1)S(1)}, u32[]{:S(2)}, u32[]{:S(2)}) collective-permute-start(bf16[4,64,2048]{2,1,0:T(8,128)(2,1)S(1)} %get-tuple-element.62), channel_id=1, source_target_pairs={{0,1},{1,0},{2,3},{3,2},{4,5},{5,4},{6,7},{7,6},{8,9},{9,8},{10,11... | collective-permute-start | bytes 3145736 | tf_op jit(solution)/shard_map/ppermute | solution.py:44
  90.8 14.9 %collective-permute-start.17 = (bf16[2,128,2048]{2,1,0:T(8,128)(2,1)S(1)}, bf16[2,128,2048]{2,1,0:T(8,128)(2,1)S(1)}, u32[]{:S(2)}, u32[]{:S(2)}) collective-permute-start(bf16[2,128,2048]{2,1,0:T(8,128)(2,1)S(1)} %pad_maximum_fusion.5), channel_id=1, source_target_pairs={{0,6},{1,7},{2,4},{3,5},{4,2},{5,3},{6,0},{7,1},{8,10},{9,11},{10,... | collective-permute-start | bytes 3145736 | tf_op jit(solution)/shard_map/ppermute | solution.py:47
  92.8 22.4 %collective-permute-start.13 = (bf16[128,2048]{1,0:T(8,128)(2,1)S(1)}, bf16[128,2048]{1,0:T(8,128)(2,1)S(1)}, u32[]{:S(2)}, u32[]{:S(2)}) collective-permute-start(bf16[128,2048]{1,0:T(8,128)(2,1)S(1)} %select_convert_fusion), channel_id=1, source_target_pairs={{0,1},{1,0},{2,3},{3,2},{4,5},{5,4},{6,7},{7,6},{8,9},{9,8},{10,11... | collective-permute-start | bytes 1572872 | tf_op jit(solution)/shard_map/ppermute | solution.py:44
  106.3 11.0 %collective-permute-start.18 = (bf16[2,64,2048]{2,1,0:T(8,128)(2,1)S(1)}, bf16[2,64,2048]{2,1,0:T(8,128)(2,1)S(1)}, u32[]{:S(2)}, u32[]{:S(2)}) collective-permute-start(bf16[2,64,2048]{2,1,0:T(8,128)(2,1)S(1)} %pad_maximum_fusion.11), channel_id=1, source_target_pairs={{0,6},{1,7},{2,4},{3,5},{4,2},{5,3},{6,0},{7,1},{8,10},{9,11},{10,... | collective-permute-start | bytes 1572872 | tf_op jit(solution)/shard_map/ppermute | solution.py:47
  106.9 13.3 %collective-permute-start.20 = (bf16[128,2048]{1,0:T(8,128)(2,1)S(1)}, bf16[128,2048]{1,0:T(8,128)(2,1)S(1)}, u32[]{:S(2)}, u32[]{:S(2)}) collective-permute-start(bf16[128,2048]{1,0:T(8,128)(2,1)S(1)} %fusion.23), channel_id=1, source_target_pairs={{0,2},{1,3},{2,0},{3,1},{4,6},{5,7},{6,4},{7,5},{8,14},{9,15},{10,... | collective-permute-start | bytes 1572872 | tf_op jit(solution)/shard_map/ppermute | solution.py:47
  115.8 14.4 %collective-permute-start.22 = (f32[128,1024]{1,0:T(8,128)S(1)}, f32[128,1024]{1,0:T(8,128)S(1)}, u32[]{:S(2)}, u32[]{:S(2)}) collective-permute-start(f32[128,1024]{1,0:T(8,128)S(1)} %slice.177), channel_id=1, source_target_pairs={{0,8},{8,0},{16,24},{24,16},{32,40},{40,32},{48,56},{56,48},{64,72... | collective-permute-start | bytes 1572872 | tf_op jit(solution)/shard_map/ppermute | solution.py:41
  163.9 17.4 %collective-permute-start.36 = (bf16[384,1024]{1,0:T(8,128)(2,1)S(1)}, bf16[384,1024]{1,0:T(8,128)(2,1)S(1)}, u32[]{:S(2)}, u32[]{:S(2)}) collective-permute-start(bf16[384,1024]{1,0:T(8,128)(2,1)S(1)} %copy-done.5), channel_id=1, source_target_pairs={{0,2},{1,3},{2,0},{3,1},{4,6},{5,7},{6,4},{7,5},{8,14},{9,15},{10,... | collective-permute-start | bytes 2359304 | tf_op jit(solution)/shard_map/ppermute | solution.py:47
  165.8 19.5 %collective-permute-start.37 = (bf16[384,1024]{1,0:T(8,128)(2,1)S(1)}, bf16[384,1024]{1,0:T(8,128)(2,1)}, u32[]{:S(2)}, u32[]{:S(2)}) collective-permute-start(bf16[384,1024]{1,0:T(8,128)(2,1)S(1)} %copy-done.5), channel_id=1, source_target_pairs={{0,6},{1,7},{2,4},{3,5},{4,2},{5,3},{6,0},{7,1},{8,10},{9,11},{10,... | collective-permute-start | bytes 2359304 | tf_op jit(solution)/shard_map/ppermute | solution.py:47
  187.5 13.4 %collective-permute-start.40 = (bf16[384,1024]{1,0:T(8,128)(2,1)S(1)}, bf16[384,1024]{1,0:T(8,128)(2,1)}, u32[]{:S(2)}, u32[]{:S(2)}) collective-permute-start(bf16[384,1024]{1,0:T(8,128)(2,1)S(1)} %collective-permute-done.36), channel_id=1, source_target_pairs={{0,6},{1,7},{2,4},{3,5},{4,2},{5,3},{6,0},{7,1},{8,10},{9,11},{10,... | collective-permute-start | bytes 2359304 | tf_op jit(solution)/shard_map/ppermute | solution.py:47
  210.2 13.2 %collective-permute-start.42 = (bf16[1024,256]{1,0:T(8,128)(2,1)S(1)}, bf16[1024,256]{1,0:T(8,128)(2,1)S(1)}, u32[]{:S(2)}, u32[]{:S(2)}) collective-permute-start(bf16[1024,256]{1,0:T(8,128)(2,1)S(1)} %fusion.14), channel_id=1, source_target_pairs={{0,1},{1,0},{2,3},{3,2},{4,5},{5,4},{6,7},{7,6},{8,9},{9,8},{10,11... | collective-permute-start | bytes 1572872 | tf_op jit(solution)/shard_map/ppermute | solution.py:44
  (31 other events, 227.4 us)

commit v6 on v5

--- a/solution.py
+++ b/solution.py
@@ -149,7 +149,7 @@
     stream = attended + residual.astype(F32)
 
     squares = jnp.sum(stream * stream, axis=1)
-    for pairs in (twin, x_near, x_next, z_far):
+    for pairs in (z_far, x_near, x_next, twin):
         squares = squares + over_row(squares, pairs)
     inverse_rms = lax.rsqrt(squares / (width * rows) + 1e-05)
     hidden = (stream * inverse_rms[:, None] * norm_gain[None, :]).astype(BF16)

time: 225 us -> 225 us (level)
  no operation moved by 1% of the time
where the time goes in v6:
time: 225 us
  waiting for transfers between devices  108 us (48%)
  starting transfers between devices  58.5 us (26%)
  matrix products  32 us (14%)
  local copies, waits for them, and re-layouts  18.2 us (8%)
  other arithmetic  6.68 us (3%)
    ppermute x25, waiting for transfers between devices, over_row(): return lax.ppermute(value, 'row', pairs)  66 us
    ppermute x25, starting transfers between devices, over_row(): return lax.ppermute(value, 'row', pairs)  33.8 us
    ppermute x5, waiting for transfers between devices, over_col(): return lax.ppermute(value, 'col', pairs)  27.8 us
    dot_general x4, matrix products, body(): terms = jnp.dot(tokens, weight, preferred_element_type=F32).astype(BF16)  22.5 us
    ppermute x13, starting transfers between devices, over_both(): return lax.ppermute(value, ('row', 'col'), pairs)  18.6 us
    ppermute x13, waiting for transfers between devices, over_both(): return lax.ppermute(value, ('row', 'col'), pairs)  14 us
    unnamed x43, local copies, waits for them, and re-layouts  7.7 us
    ppermute x5, starting transfers between devices, over_col(): return lax.ppermute(value, 'col', pairs)  6.06 us
  transfers between devices with their start and end apart: 43, of which 30 were waited for; matrix products, arithmetic and copies ran while one was open for 20% of the time, Pallas kernels for 0%

profile of v6, /device:TPU:1, one launch (start us, length us, event | category | flops | bytes accessed | tf_op | source)
XLA Modules:
  0.0 224.7 jit_solution(10014444652979536847)
XLA Ops:
  6.8 3.6 %collective-permute-start = (bf16[128,2048]{1,0:T(8,128)(2,1)S(1)}, bf16[128,2048]{1,0:T(8,128)(2,1)S(1)}, u32[]{:S(2)}, u32[]{:S(2)}) collective-permute-start(bf16[128,2048]{1,0:T(8,128)(2,1)S(1)} %get-tuple-element.79), channel_id=1, source_target_pairs={{0,16},{8,24},{16,0},{24,8},{32,48},{40,56},{48,32},{56,40},{64,80... | collective-permute-start | bytes 1572872 | tf_op jit(solution)/shard_map/ppermute | solution.py:41
  11.6 4.8 %constant_dynamic-update-slice_fusion.12 = bf16[2048,2048]{1,0:T(8,128)(2,1)} fusion(bf16[2048,1024]{1,0:T(8,128)(2,1)} %param.8), kind=kLoop, calls=%fused_computation.104 | loop fusion | bytes 8388608
  17.9 4.9 %collective-permute-done = bf16[128,2048]{1,0:T(8,128)(2,1)S(1)} collective-permute-done((bf16[128,2048]{1,0:T(8,128)(2,1)S(1)}, bf16[128,2048]{1,0:T(8,128)(2,1)S(1)}, u32[]{:S(2)}, u32[]{:S(2)}) %collective-permute-start) | collective-permute-done | bytes 524320 | tf_op jit(solution)/shard_map/ppermute | solution.py:41
  22.9 4.8 %constant_dynamic-update-slice_fusion.11 = bf16[2048,2048]{1,0:T(8,128)(2,1)} fusion(bf16[2048,2048]{1,0:T(8,128)(2,1)} %constant_dynamic-update-slice_fusion.12, bf16[2048,1024]{1,0:T(8,128)(2,1)} %collective-permute-done.2), kind=kLoop, calls=%fused_computation.103 | loop fusion | bytes 8388608 | tf_op jit(solution)/shard_map/concatenate | solution.py:68
  27.6 10.5 %collective-permute-done.5 = bf16[128,2048]{1,0:T(8,128)(2,1)S(1)} collective-permute-done((bf16[128,2048]{1,0:T(8,128)(2,1)S(1)}, bf16[128,2048]{1,0:T(8,128)(2,1)S(1)}, u32[]{:S(2)}, u32[]{:S(2)}) %collective-permute-start.5) | collective-permute-done | bytes 524320 | tf_op jit(solution)/shard_map/ppermute | solution.py:41
  38.5 8.3 %convolution_convert_fusion.3 = bf16[512,2048]{1,0:T(8,128)(2,1)S(1)} fusion(bf16[2048,2048]{1,0:T(8,128)(2,1)} %constant_dynamic-update-slice_fusion.11, bf16[256,2048]{1,0:T(8,128)(2,1)} %collective-permute-done.3, bf16[256,2048]{1,0:T(8,128)(2,1)S(1)} %pad_maximum_fusion.1), kind=kOutput, calls=%fused_computation.4 | convolution fusion | flops 4300210176 | bytes 12582912 | tf_op jit(solution)/shard_map/dot_general | solution.py:98
  48.6 5.1 %collective-permute-done.8 = bf16[128,2048]{1,0:T(8,128)(2,1)S(1)} collective-permute-done((bf16[128,2048]{1,0:T(8,128)(2,1)S(1)}, bf16[128,2048]{1,0:T(8,128)(2,1)S(1)}, u32[]{:S(2)}, u32[]{:S(2)}) %collective-permute-start.8) | collective-permute-done | bytes 524320 | tf_op jit(solution)/shard_map/ppermute | solution.py:41
  54.7 3.2 %collective-permute-done.6 = bf16[256,2048]{1,0:T(8,128)(2,1)S(1)} collective-permute-done((bf16[256,2048]{1,0:T(8,128)(2,1)S(1)}, bf16[256,2048]{1,0:T(8,128)(2,1)S(1)}, u32[]{:S(2)}, u32[]{:S(2)}) %collective-permute-start.6) | collective-permute-done | bytes 1048608 | tf_op jit(solution)/shard_map/ppermute | solution.py:41
  57.8 4.7 %convolution_convert_fusion.2 = bf16[512,2048]{1,0:T(8,128)(2,1)S(1)} fusion(bf16[2048,2048]{1,0:T(8,128)(2,1)S(1)} %bitcast.100, bf16[256,2048]{1,0:T(8,128)(2,1)S(1)} %collective-permute-done.6, bf16[256,2048]{1,0:T(8,128)(2,1)S(1)} %constant_dynamic-update-slice_fusion.13), kind=kOutput, calls=%fused_computation.3 | convolution fusion | flops 4300210176 | bytes 12582912 | tf_op jit(solution)/shard_map/dot_general | solution.py:98
  69.7 5.0 %collective-permute-done.9 = bf16[256,2048]{1,0:T(8,128)(2,1)S(1)} collective-permute-done((bf16[256,2048]{1,0:T(8,128)(2,1)S(1)}, bf16[256,2048]{1,0:T(8,128)(2,1)S(1)}, u32[]{:S(2)}, u32[]{:S(2)}) %collective-permute-start.9) | collective-permute-done | bytes 1048608 | tf_op jit(solution)/shard_map/ppermute | solution.py:41
  74.7 4.8 %convolution_convert_fusion.1 = bf16[512,2048]{1,0:T(8,128)(2,1)S(1)} fusion(bf16[2048,2048]{1,0:T(8,128)(2,1)S(1)} %bitcast.100, bf16[256,2048]{1,0:T(8,128)(2,1)S(1)} %collective-permute-done.9, bf16[256,2048]{1,0:T(8,128)(2,1)S(1)} %constant_dynamic-update-slice_fusion.15), kind=kOutput, calls=%fused_computation.2 | convolution fusion | flops 4300210176 | bytes 12582912 | tf_op jit(solution)/shard_map/dot_general | solution.py:98
  85.9 4.7 %convolution_convert_fusion = bf16[512,2048]{1,0:T(8,128)(2,1)S(1)} fusion(bf16[2048,2048]{1,0:T(8,128)(2,1)S(1)} %bitcast.100, bf16[256,2048]{1,0:T(8,128)(2,1)S(1)} %collective-permute-done.16, bf16[128,2048]{1,0:T(8,128)(2,1)S(1)} %collective-permute-done.15, bf16[128,2048]{1,0:T(8,128)(2,1)S(1)} %pad_maximum_fusion.10), kind=kOutput, calls=%fused_computation.1 | convolution fusion | flops 4302307328 | bytes 12582912 | tf_op jit(solution)/shard_map/dot_general | solution.py:98
  94.0 10.0 %collective-permute-done.14 = bf16[4,64,2048]{2,1,0:T(8,128)(2,1)S(1)} collective-permute-done((bf16[4,64,2048]{2,1,0:T(8,128)(2,1)S(1)}, bf16[4,64,2048]{2,1,0:T(8,128)(2,1)S(1)}, u32[]{:S(2)}, u32[]{:S(2)}) %collective-permute-start.14) | collective-permute-done | bytes 1048608 | tf_op jit(solution)/shard_map/ppermute | solution.py:44
  108.9 6.3 %collective-permute-done.13 = bf16[128,2048]{1,0:T(8,128)(2,1)S(1)} collective-permute-done((bf16[128,2048]{1,0:T(8,128)(2,1)S(1)}, bf16[128,2048]{1,0:T(8,128)(2,1)S(1)}, u32[]{:S(2)}, u32[]{:S(2)}) %collective-permute-start.13) | collective-permute-done | bytes 524320 | tf_op jit(solution)/shard_map/ppermute | solution.py:44
  124.8 5.1 %collective-permute-start.23 = (f32[64,1024]{1,0:T(8,128)S(1)}, f32[64,1024]{1,0:T(8,128)S(1)}, u32[]{:S(2)}, u32[]{:S(2)}) collective-permute-start(f32[64,1024]{1,0:T(8,128)S(1)} %slice.178), channel_id=1, source_target_pairs={{0,8},{8,0},{16,24},{24,16},{32,40},{40,32},{48,56},{56,48},{64,72... | collective-permute-start | bytes 786440 | tf_op jit(solution)/shard_map/ppermute | solution.py:41
  133.9 3.1 %collective-permute-start.25 = (f32[512]{0:T(512)S(1)}, f32[512]{0:T(512)S(1)}, u32[]{:S(2)}, u32[]{:S(2)}) collective-permute-start(f32[512]{0:T(512)S(1)} %multiply_reduce_fusion), channel_id=1, source_target_pairs={{0,16},{8,24},{16,0},{24,8},{32,48},{40,56},{48,32},{56,40},{64,80... | collective-permute-start | bytes 6152 | tf_op jit(solution)/shard_map/ppermute | solution.py:41
  144.1 3.6 %collective-permute-start.28 = (f32[512]{0:T(512)S(1)}, f32[512]{0:T(512)S(1)}, u32[]{:S(2)}, u32[]{:S(2)}) collective-permute-start(f32[512]{0:T(512)S(1)} %add.223), channel_id=1, source_target_pairs={{0,8},{8,0},{16,24},{24,16},{32,40},{40,32},{48,56},{56,48},{64,72... | collective-permute-start | bytes 6152 | tf_op jit(solution)/shard_map/ppermute | solution.py:41
  155.9 6.8 %collective-permute-done.30 = bf16[2,2,24,2048]{3,2,1,0:T(8,128)(2,1)S(1)} collective-permute-done((bf16[2,2,24,2048]{3,2,1,0:T(8,128)(2,1)S(1)}, bf16[2,2,24,2048]{3,2,1,0:T(8,128)(2,1)S(1)}, u32[]{:S(2)}, u32[]{:S(2)}) %collective-permute-start.30) | collective-permute-done | bytes 393248 | tf_op jit(solution)/shard_map/ppermute | solution.py:41
  168.7 3.1 %collective-permute-start.32 = (bf16[2,24,2048]{2,1,0:T(8,128)(2,1)S(1)}, bf16[2,24,2048]{2,1,0:T(8,128)(2,1)S(1)}, u32[]{:S(2)}, u32[]{:S(2)}) collective-permute-start(bf16[2,24,2048]{2,1,0:T(8,128)(2,1)S(1)} %rev.14), channel_id=1, source_target_pairs={{0,16},{8,24},{16,0},{24,8},{32,48},{40,56},{48,32},{56,40},{64,80... | collective-permute-start | bytes 589832 | tf_op jit(solution)/shard_map/ppermute | solution.py:41
  179.0 3.3 %collective-permute-done.36 = bf16[384,1024]{1,0:T(8,128)(2,1)S(1)} collective-permute-done((bf16[384,1024]{1,0:T(8,128)(2,1)S(1)}, bf16[384,1024]{1,0:T(8,128)(2,1)S(1)}, u32[]{:S(2)}, u32[]{:S(2)}) %collective-permute-start.36) | collective-permute-done | bytes 786464 | tf_op jit(solution)/shard_map/ppermute | solution.py:47
  182.3 3.7 %collective-permute-done.37 = bf16[384,1024]{1,0:T(8,128)(2,1)} collective-permute-done((bf16[384,1024]{1,0:T(8,128)(2,1)S(1)}, bf16[384,1024]{1,0:T(8,128)(2,1)}, u32[]{:S(2)}, u32[]{:S(2)}) %collective-permute-start.37) | collective-permute-done | bytes 786464 | tf_op jit(solution)/shard_map/ppermute | solution.py:47
  189.4 5.2 %collective-permute-done.38 = bf16[1,4,48,512]{3,2,0,1:T(8,128)(2,1)S(1)} collective-permute-done((bf16[1,4,48,512]{3,2,0,1:T(8,128)(2,1)S(1)}, bf16[1,4,48,512]{3,2,0,1:T(8,128)(2,1)S(1)}, u32[]{:S(2)}, u32[]{:S(2)}) %collective-permute-start.38) | collective-permute-done | bytes 196640 | tf_op jit(solution)/shard_map/ppermute | solution.py:41
  194.7 7.0 %collective-permute-done.39 = bf16[2,4,48,512]{3,2,0,1:T(8,128)(2,1)S(1)} collective-permute-done((bf16[2,4,48,512]{3,2,0,1:T(8,128)(2,1)S(1)}, bf16[2,4,48,512]{3,2,0,1:T(8,128)(2,1)S(1)}, u32[]{:S(2)}, u32[]{:S(2)}) %collective-permute-start.39) | collective-permute-done | bytes 393248 | tf_op jit(solution)/shard_map/ppermute | solution.py:41
  214.0 9.6 %collective-permute-done.42 = bf16[1024,256]{1,0:T(8,128)(2,1)S(1)} collective-permute-done((bf16[1024,256]{1,0:T(8,128)(2,1)S(1)}, bf16[1024,256]{1,0:T(8,128)(2,1)S(1)}, u32[]{:S(2)}, u32[]{:S(2)}) %collective-permute-start.42) | collective-permute-done | bytes 524320 | tf_op jit(solution)/shard_map/ppermute | solution.py:44
  (194 shorter events, 91.7 us)
Async XLA Ops:
  0.6 15.8 %collective-permute-start.2 = (bf16[2048,1024]{1,0:T(8,128)(2,1)}, bf16[2048,1024]{1,0:T(8,128)(2,1)}, u32[]{:S(2)}, u32[]{:S(2)}) collective-permute-start(bf16[2048,1024]{1,0:T(8,128)(2,1)} %param.8), channel_id=1, source_target_pairs={{0,8},{8,0},{16,24},{24,16},{32,40},{40,32},{48,56},{56,48},{64,72... | collective-permute-start | bytes 12582920 | tf_op jit(solution)/shard_map/ppermute | solution.py:41
  4.2 12.2 %collective-permute-start.1 = (bf16[128,2048]{1,0:T(8,128)(2,1)S(1)}, bf16[128,2048]{1,0:T(8,128)(2,1)}, u32[]{:S(2)}, u32[]{:S(2)}) collective-permute-start(bf16[128,2048]{1,0:T(8,128)(2,1)S(1)} %get-tuple-element.79), channel_id=1, source_target_pairs={{0,32},{8,104},{16,48},{24,120},{32,0},{40,72},{48,16},{56,88},{64... | collective-permute-start | bytes 1572872 | tf_op jit(solution)/shard_map/ppermute | solution.py:41
  6.8 16.0 %collective-permute-start = (bf16[128,2048]{1,0:T(8,128)(2,1)S(1)}, bf16[128,2048]{1,0:T(8,128)(2,1)S(1)}, u32[]{:S(2)}, u32[]{:S(2)}) collective-permute-start(bf16[128,2048]{1,0:T(8,128)(2,1)S(1)} %get-tuple-element.79), channel_id=1, source_target_pairs={{0,16},{8,24},{16,0},{24,8},{32,48},{40,56},{48,32},{56,40},{64,80... | collective-permute-start | bytes 1572872 | tf_op jit(solution)/shard_map/ppermute | solution.py:41
  10.4 27.9 %collective-permute-start.4 = (bf16[128,2048]{1,0:T(8,128)(2,1)}, bf16[128,2048]{1,0:T(8,128)(2,1)S(1)}, u32[]{:S(2)}, u32[]{:S(2)}) collective-permute-start(bf16[128,2048]{1,0:T(8,128)(2,1)} %get-tuple-element.78), channel_id=1, source_target_pairs={{0,16},{8,24},{16,0},{24,8},{32,48},{40,56},{48,32},{56,40},{64,80... | collective-permute-start | bytes 1572872 | tf_op jit(solution)/shard_map/ppermute | solution.py:41
  17.6 20.7 %collective-permute-start.3 = (bf16[256,2048]{1,0:T(8,128)(2,1)S(1)}, bf16[256,2048]{1,0:T(8,128)(2,1)}, u32[]{:S(2)}, u32[]{:S(2)}) collective-permute-start(bf16[256,2048]{1,0:T(8,128)(2,1)S(1)} %pad_maximum_fusion.1), channel_id=1, source_target_pairs={{0,96},{8,40},{16,112},{24,56},{32,64},{40,8},{48,80},{56,24},{64,... | collective-permute-start | bytes 3145736 | tf_op jit(solution)/shard_map/ppermute | solution.py:41
  22.8 15.3 %collective-permute-start.5 = (bf16[128,2048]{1,0:T(8,128)(2,1)S(1)}, bf16[128,2048]{1,0:T(8,128)(2,1)S(1)}, u32[]{:S(2)}, u32[]{:S(2)}) collective-permute-start(bf16[128,2048]{1,0:T(8,128)(2,1)S(1)} %collective-permute-done), channel_id=1, source_target_pairs={{0,32},{8,104},{16,48},{24,120},{32,0},{40,72},{48,16},{56,88},{64... | collective-permute-start | bytes 1572872 | tf_op jit(solution)/shard_map/ppermute | solution.py:41
  38.2 19.6 %collective-permute-start.6 = (bf16[256,2048]{1,0:T(8,128)(2,1)S(1)}, bf16[256,2048]{1,0:T(8,128)(2,1)S(1)}, u32[]{:S(2)}, u32[]{:S(2)}) collective-permute-start(bf16[256,2048]{1,0:T(8,128)(2,1)S(1)} %constant_dynamic-update-slice_fusion.13), channel_id=1, source_target_pairs={{0,96},{8,40},{16,112},{24,56},{32,64},{40,8},{48,80},{56,24},{64,... | collective-permute-start | bytes 3145736 | tf_op jit(solution)/shard_map/ppermute | solution.py:41
  38.4 15.3 %collective-permute-start.8 = (bf16[128,2048]{1,0:T(8,128)(2,1)S(1)}, bf16[128,2048]{1,0:T(8,128)(2,1)S(1)}, u32[]{:S(2)}, u32[]{:S(2)}) collective-permute-start(bf16[128,2048]{1,0:T(8,128)(2,1)S(1)} %pad_maximum_fusion.9), channel_id=1, source_target_pairs={{0,32},{8,104},{16,48},{24,120},{32,0},{40,72},{48,16},{56,88},{64... | collective-permute-start | bytes 1572872 | tf_op jit(solution)/shard_map/ppermute | solution.py:41
  47.1 15.5 %collective-permute-start.7 = (bf16[2,128,2048]{2,1,0:T(8,128)(2,1)S(1)}, bf16[2,128,2048]{2,1,0:T(8,128)(2,1)S(1)}, u32[]{:S(2)}, u32[]{:S(2)}) collective-permute-start(bf16[2,128,2048]{2,1,0:T(8,128)(2,1)S(1)} %pad_maximum_fusion.2), channel_id=1, source_target_pairs={{0,6},{1,7},{2,4},{3,5},{4,2},{5,3},{6,0},{7,1},{8,10},{9,11},{10,... | collective-permute-start | bytes 3145736 | tf_op jit(solution)/shard_map/ppermute | solution.py:47
  53.7 20.9 %collective-permute-start.9 = (bf16[256,2048]{1,0:T(8,128)(2,1)S(1)}, bf16[256,2048]{1,0:T(8,128)(2,1)S(1)}, u32[]{:S(2)}, u32[]{:S(2)}) collective-permute-start(bf16[256,2048]{1,0:T(8,128)(2,1)S(1)} %constant_dynamic-update-slice_fusion.15), channel_id=1, source_target_pairs={{0,96},{8,40},{16,112},{24,56},{32,64},{40,8},{48,80},{56,24},{64,... | collective-permute-start | bytes 3145736 | tf_op jit(solution)/shard_map/ppermute | solution.py:41
  54.1 14.9 %collective-permute-start.15 = (bf16[128,2048]{1,0:T(8,128)(2,1)S(1)}, bf16[128,2048]{1,0:T(8,128)(2,1)S(1)}, u32[]{:S(2)}, u32[]{:S(2)}) collective-permute-start(bf16[128,2048]{1,0:T(8,128)(2,1)S(1)} %pad_maximum_fusion.10), channel_id=1, source_target_pairs={{0,32},{8,104},{16,48},{24,120},{32,0},{40,72},{48,16},{56,88},{64... | collective-permute-start | bytes 1572872 | tf_op jit(solution)/shard_map/ppermute | solution.py:41
  62.8 19.6 %collective-permute-start.10 = (bf16[2,128,2048]{2,1,0:T(8,128)(2,1)S(1)}, bf16[2,128,2048]{2,1,0:T(8,128)(2,1)S(1)}, u32[]{:S(2)}, u32[]{:S(2)}) collective-permute-start(bf16[2,128,2048]{2,1,0:T(8,128)(2,1)S(1)} %pad_maximum_fusion.3), channel_id=1, source_target_pairs={{0,6},{1,7},{2,4},{3,5},{4,2},{5,3},{6,0},{7,1},{8,10},{9,11},{10,... | collective-permute-start | bytes 3145736 | tf_op jit(solution)/shard_map/ppermute | solution.py:47
  64.3 16.6 %collective-permute-start.11 = (bf16[128,2048]{1,0:T(8,128)(2,1)S(1)}, bf16[128,2048]{1,0:T(8,128)(2,1)S(1)}, u32[]{:S(2)}, u32[]{:S(2)}) collective-permute-start(bf16[128,2048]{1,0:T(8,128)(2,1)S(1)} %fusion.21), channel_id=1, source_target_pairs={{0,2},{1,3},{2,0},{3,1},{4,6},{5,7},{6,4},{7,5},{8,14},{9,15},{10,... | collective-permute-start | bytes 1572872 | tf_op jit(solution)/shard_map/ppermute | solution.py:47
  69.1 16.9 %collective-permute-start.16 = (bf16[256,2048]{1,0:T(8,128)(2,1)S(1)}, bf16[256,2048]{1,0:T(8,128)(2,1)S(1)}, u32[]{:S(2)}, u32[]{:S(2)}) collective-permute-start(bf16[256,2048]{1,0:T(8,128)(2,1)S(1)} %pad_maximum_fusion.4), channel_id=1, source_target_pairs={{0,96},{8,40},{16,112},{24,56},{32,64},{40,8},{48,80},{56,24},{64,... | collective-permute-start | bytes 3145736 | tf_op jit(solution)/shard_map/ppermute | solution.py:41
  79.7 24.3 %collective-permute-start.14 = (bf16[4,64,2048]{2,1,0:T(8,128)(2,1)S(1)}, bf16[4,64,2048]{2,1,0:T(8,128)(2,1)S(1)}, u32[]{:S(2)}, u32[]{:S(2)}) collective-permute-start(bf16[4,64,2048]{2,1,0:T(8,128)(2,1)S(1)} %get-tuple-element.62), channel_id=1, source_target_pairs={{0,1},{1,0},{2,3},{3,2},{4,5},{5,4},{6,7},{7,6},{8,9},{9,8},{10,11... | collective-permute-start | bytes 3145736 | tf_op jit(solution)/shard_map/ppermute | solution.py:44
  90.8 14.9 %collective-permute-start.17 = (bf16[2,128,2048]{2,1,0:T(8,128)(2,1)S(1)}, bf16[2,128,2048]{2,1,0:T(8,128)(2,1)S(1)}, u32[]{:S(2)}, u32[]{:S(2)}) collective-permute-start(bf16[2,128,2048]{2,1,0:T(8,128)(2,1)S(1)} %pad_maximum_fusion.5), channel_id=1, source_target_pairs={{0,6},{1,7},{2,4},{3,5},{4,2},{5,3},{6,0},{7,1},{8,10},{9,11},{10,... | collective-permute-start | bytes 3145736 | tf_op jit(solution)/shard_map/ppermute | solution.py:47
  92.8 22.4 %collective-permute-start.13 = (bf16[128,2048]{1,0:T(8,128)(2,1)S(1)}, bf16[128,2048]{1,0:T(8,128)(2,1)S(1)}, u32[]{:S(2)}, u32[]{:S(2)}) collective-permute-start(bf16[128,2048]{1,0:T(8,128)(2,1)S(1)} %select_convert_fusion), channel_id=1, source_target_pairs={{0,1},{1,0},{2,3},{3,2},{4,5},{5,4},{6,7},{7,6},{8,9},{9,8},{10,11... | collective-permute-start | bytes 1572872 | tf_op jit(solution)/shard_map/ppermute | solution.py:44
  106.3 11.0 %collective-permute-start.18 = (bf16[2,64,2048]{2,1,0:T(8,128)(2,1)S(1)}, bf16[2,64,2048]{2,1,0:T(8,128)(2,1)S(1)}, u32[]{:S(2)}, u32[]{:S(2)}) collective-permute-start(bf16[2,64,2048]{2,1,0:T(8,128)(2,1)S(1)} %pad_maximum_fusion.11), channel_id=1, source_target_pairs={{0,6},{1,7},{2,4},{3,5},{4,2},{5,3},{6,0},{7,1},{8,10},{9,11},{10,... | collective-permute-start | bytes 1572872 | tf_op jit(solution)/shard_map/ppermute | solution.py:47
  106.9 13.3 %collective-permute-start.20 = (bf16[128,2048]{1,0:T(8,128)(2,1)S(1)}, bf16[128,2048]{1,0:T(8,128)(2,1)S(1)}, u32[]{:S(2)}, u32[]{:S(2)}) collective-permute-start(bf16[128,2048]{1,0:T(8,128)(2,1)S(1)} %fusion.23), channel_id=1, source_target_pairs={{0,2},{1,3},{2,0},{3,1},{4,6},{5,7},{6,4},{7,5},{8,14},{9,15},{10,... | collective-permute-start | bytes 1572872 | tf_op jit(solution)/shard_map/ppermute | solution.py:47
  115.8 14.4 %collective-permute-start.22 = (f32[128,1024]{1,0:T(8,128)S(1)}, f32[128,1024]{1,0:T(8,128)S(1)}, u32[]{:S(2)}, u32[]{:S(2)}) collective-permute-start(f32[128,1024]{1,0:T(8,128)S(1)} %slice.177), channel_id=1, source_target_pairs={{0,8},{8,0},{16,24},{24,16},{32,40},{40,32},{48,56},{56,48},{64,72... | collective-permute-start | bytes 1572872 | tf_op jit(solution)/shard_map/ppermute | solution.py:41
  164.6 17.7 %collective-permute-start.36 = (bf16[384,1024]{1,0:T(8,128)(2,1)S(1)}, bf16[384,1024]{1,0:T(8,128)(2,1)S(1)}, u32[]{:S(2)}, u32[]{:S(2)}) collective-permute-start(bf16[384,1024]{1,0:T(8,128)(2,1)S(1)} %copy-done.5), channel_id=1, source_target_pairs={{0,2},{1,3},{2,0},{3,1},{4,6},{5,7},{6,4},{7,5},{8,14},{9,15},{10,... | collective-permute-start | bytes 2359304 | tf_op jit(solution)/shard_map/ppermute | solution.py:47
  166.5 19.5 %collective-permute-start.37 = (bf16[384,1024]{1,0:T(8,128)(2,1)S(1)}, bf16[384,1024]{1,0:T(8,128)(2,1)}, u32[]{:S(2)}, u32[]{:S(2)}) collective-permute-start(bf16[384,1024]{1,0:T(8,128)(2,1)S(1)} %copy-done.5), channel_id=1, source_target_pairs={{0,6},{1,7},{2,4},{3,5},{4,2},{5,3},{6,0},{7,1},{8,10},{9,11},{10,... | collective-permute-start | bytes 2359304 | tf_op jit(solution)/shard_map/ppermute | solution.py:47
  188.4 13.4 %collective-permute-start.40 = (bf16[384,1024]{1,0:T(8,128)(2,1)S(1)}, bf16[384,1024]{1,0:T(8,128)(2,1)}, u32[]{:S(2)}, u32[]{:S(2)}) collective-permute-start(bf16[384,1024]{1,0:T(8,128)(2,1)S(1)} %collective-permute-done.36), channel_id=1, source_target_pairs={{0,6},{1,7},{2,4},{3,5},{4,2},{5,3},{6,0},{7,1},{8,10},{9,11},{10,... | collective-permute-start | bytes 2359304 | tf_op jit(solution)/shard_map/ppermute | solution.py:47
  210.4 13.2 %collective-permute-start.42 = (bf16[1024,256]{1,0:T(8,128)(2,1)S(1)}, bf16[1024,256]{1,0:T(8,128)(2,1)S(1)}, u32[]{:S(2)}, u32[]{:S(2)}) collective-permute-start(bf16[1024,256]{1,0:T(8,128)(2,1)S(1)} %fusion.14), channel_id=1, source_target_pairs={{0,1},{1,0},{2,3},{3,2},{4,5},{5,4},{6,7},{7,6},{8,9},{9,8},{10,11... | collective-permute-start | bytes 1572872 | tf_op jit(solution)/shard_map/ppermute | solution.py:44
  (31 other events, 228.0 us)
